TPU v7x, 32 devices: a whole 2x2x4 slice. The times are simulated.
32 devices in a mesh: gen: 2 (over x), learn: 16 (over z, y, core).
Axes of the slice: x: 2, y: 2, z: 4, core: 2. Of those that a mesh axis runs over, the one named last changes fastest.
Arguments:
- hidden: bfloat16 [8192, 5120], P(('gen', 'learn')), may hold values from -0.59765625 to 0.59765625
- cotangent: bfloat16 [8192, 1024], P(('gen', 'learn')), may hold values from -0.29882812 to 0.29882812
- importance: float32 [8192], P(('gen', 'learn')), may hold values from 0.25 to 4
- block_len: int32 [1024], P(('gen', 'learn')), may hold values from 1 to 8
- version: int32 [1024], P(('gen', 'learn')), may hold values from 0 to 3
- destination: int32 [1024, 1], P(('gen', 'learn')), may hold values from 0 to 15; in each aligned block of 32 rows (0 to 31, 32 to 63, ...) at most 4 rows name the same one
- w_key: bfloat16 [5120, 1024], replicated, may hold values from -0.078125 to 0.078125
- in_gain: float32 [5120], replicated, may hold values from 0.5 to 1.5
- key_gain: float32 [128], replicated, may hold values from 0.5 to 1.5
Outputs:
- grad_slots: bfloat16 [16384, 5120], P(('gen', 'learn'))
- w_grad: float32 [5120, 1024], P('gen')
- gain_grad: float32 [5120], replicated
- kgain_grad: float32 [128], replicated
Inputs may be any that keep to these rules, and one draw needn't show every extreme that they name: `destination`: the 32 blocks of one device name each learner at most 4 times.
All inputs are finite; a program needn't handle non-finite values.
Results may differ from a plain program's by a relative error of at most 0.0075.
Values may be sent and summed in bfloat16 or wider, within the bound.
No kernel may reach another device: no remote copies, remote signals or barrier semaphores. Data moves between devices by JAX's collectives and lax.ppermute only.
A program may use at most 128 MiB of HBM per device.

v0:
```python
import jax
import jax.numpy as jnp
from jax import lax
from jax.sharding import PartitionSpec as P

TILE = 8
VERSIONS = 4
SLOTS = 64


epsilon = 1e-06
clip_ratio = 2.0
staleness = 0.5


def token_weights(importance, block_len, version):
    tile_count = block_len.shape[0]
    inside = (lax.broadcasted_iota(jnp.int32, (tile_count, TILE), 1) < block_len[:, None]).astype(
        jnp.float32
    )
    stale_age = (VERSIONS - 1 - version).astype(jnp.float32)
    decay_factor = jnp.power(jnp.float32(staleness), stale_age)
    return jnp.minimum(importance, clip_ratio) * (decay_factor[:, None] * inside).reshape(-1)


def layer_pass(hidden, upstream_rows, w_key, in_gain, key_gain):
    row_count = hidden.shape[0]
    x_float = hidden.astype(jnp.float32)
    inv_rms = lax.rsqrt(jnp.mean(x_float * x_float, -1, keepdims=True) + epsilon)
    normed = x_float * inv_rms
    h_rows = (normed * in_gain).astype(jnp.bfloat16)
    key_rows = jnp.dot(h_rows, w_key, preferred_element_type=jnp.float32).reshape(
        row_count, -1, key_gain.shape[0]
    )
    key_scale = lax.rsqrt(jnp.mean(key_rows * key_rows, -1, keepdims=True) + epsilon)
    upstream = upstream_rows.astype(jnp.float32).reshape(key_rows.shape)
    kgain_part = jnp.sum(upstream * key_rows * key_scale, axis=(0, 1))
    scaled = upstream * key_gain
    grad_keys = key_scale * scaled - key_rows * key_scale**3 * jnp.mean(
        scaled * key_rows, -1, keepdims=True
    )
    grad_keys = grad_keys.reshape(row_count, -1).astype(jnp.bfloat16)
    grad_h = lax.dot_general(
        grad_keys, w_key, (((1,), (1,)), ((), ())), preferred_element_type=jnp.float32
    )
    gain_part = jnp.sum(grad_h * normed, 0)
    grad_normed = grad_h * in_gain
    grad_input = inv_rms * (
        grad_normed - normed * jnp.mean(grad_normed * normed, -1, keepdims=True)
    )
    return (grad_input.astype(jnp.bfloat16), h_rows, grad_keys, gain_part, kgain_part)


def body(hidden, cotangent, importance, block_len, version, destination, w_key, in_gain, key_gain):
    learners = lax.axis_size("learn")
    capacity = SLOTS // learners
    tile_count = block_len.shape[0]
    weights = token_weights(importance, block_len, version)
    upstream_all = (cotangent.astype(jnp.float32) * weights[:, None]).astype(jnp.bfloat16)
    dest_column = destination[:, 0]
    onehot = (dest_column[:, None] == jnp.arange(learners, dtype=jnp.int32)[None, :]).astype(
        jnp.int32
    )
    slot_rank = jnp.sum((jnp.cumsum(onehot, 0) - onehot) * onehot, 1)
    target = dest_column * capacity + slot_rank
    placing = (target[None, :] == jnp.arange(SLOTS, dtype=jnp.int32)[:, None]).astype(jnp.bfloat16)
    grad_local, h_rows, grad_keys, gain_part, kgain_part = layer_pass(
        hidden, upstream_all, w_key, in_gain, key_gain
    )
    feature_count = grad_local.shape[1]
    spread = jnp.dot(
        placing,
        grad_local.reshape(tile_count, TILE * feature_count),
        preferred_element_type=jnp.float32,
    )
    grad_slots = lax.all_to_all(
        spread.astype(jnp.bfloat16).reshape(SLOTS * TILE, feature_count),
        "learn",
        split_axis=0,
        concat_axis=0,
        tiled=True,
    )
    partial_rows = lax.psum_scatter(
        lax.dot_general(
            h_rows, grad_keys, (((0,), (0,)), ((), ())), preferred_element_type=jnp.float32
        ),
        "gen",
        scatter_dimension=0,
        tiled=True,
    )
    w_grad = lax.psum(partial_rows, "learn")
    gain_grad, kgain_grad = lax.psum((gain_part, kgain_part), ("gen", "learn"))
    return (grad_slots, w_grad, gain_grad, kgain_grad)


def solution(mesh):
    return jax.shard_map(
        body,
        mesh=mesh,
        in_specs=(
            P(("gen", "learn"), None),
            P(("gen", "learn"), None),
            P(("gen", "learn")),
            P(("gen", "learn")),
            P(("gen", "learn")),
            P(("gen", "learn"), None),
            P(),
            P(),
            P(),
        ),
        out_specs=(P(("gen", "learn"), None), P("gen", None), P(), P()),
        check_vma=False,
    )
```

profile of v0, /device:TPU:0, one launch (start us, length us, event | category | flops | bytes accessed | tf_op | source)
XLA Modules:
  0.0 493.8 jit_solution(3641232230139077276)
XLA Ops:
  7.2 0.0 reduce-scatter.2.cloned.1.call-start
  7.2 0.7 convert_power_fusion
  7.9 2.3 fusion.10
  10.2 0.7 broadcast_bitcast_fusion
  10.9 0.7 fusion.22
  11.6 0.1 mul.159
  11.7 0.0 copy-start.7
  11.7 0.0 copy-start.3
  11.7 6.5 %fusion.18 = f32[256,1024]{1,0:T(8,128)S(1)} fusion(bf16[5120,1024]{1,0:T(8,128)(2,1)} %param.15, bf16[256,5120]{1,0:T(8,128)(2,1)} %param.9, f32[5120]{0:T(1024)} %param.16, f32[256]{0:T(256)S(1)} %add_rsqrt_fusion.1), kind=kOutput, calls=%fused_computation.29 | convolution fusion | flops 2689597440 | bytes 14177280 | tf_op jit(solution)/shard_map/dot_general | solution.py:32
  18.3 0.0 copy-start.2
  18.3 0.0 copy-start.5
  18.3 0.2 copy.21
  18.5 0.1 convert_bitcast_fusion
  18.7 0.2 copy.24
  18.9 0.1 copy-done.5
  19.0 0.1 bitcast_multiply_fusion.1
  19.0 0.6 multiply_reduce_fusion.1
  19.7 0.0 copy-start
  19.7 0.0 copy-start.4
  19.7 0.1 copy.16
  19.8 0.1 copy.19
  19.9 0.1 copy.17
  20.0 0.1 copy.20
  20.1 0.1 copy.18
  20.3 0.3 mul.168
  20.6 0.3 mul.174
  20.9 0.3 mul.155
  21.3 2.4 fusion.15
  23.7 8.7 %fusion.16 = f32[5120,1024]{1,0:T(8,128)} fusion(bf16[256,1024]{1,0:T(8,128)(2,1)S(1)} %get-tuple-element.11, bf16[256,5120]{1,0:T(8,128)(2,1)S(1)} %copy-done, f32[5120]{0:T(1024)S(1)} %copy-done.4, f32[256]{0:T(256)S(1)} %add_rsqrt_fusion.1), kind=kOutput, calls=%fused_computation.28 | convolution fusion | flops 2689597440 | bytes 24138752 | tf_op jit(solution)/shard_map/dot_general | solution.py:84
  32.4 0.0 reduce-scatter.2.cloned.1.call-update
  32.4 6.5 %fusion.9 = (f32[5120]{0:T(1024)S(1)}, f32[256]{0:T(256)S(1)}, f32[256,5120]{1,0:T(8,128)S(1)}) fusion(bf16[256,5120]{1,0:T(8,128)(2,1)S(1)} %copy-done, f32[256]{0:T(256)S(1)} %add_rsqrt_fusion.1, f32[5120]{0:T(1024)S(1)} %copy-done.4, bf16[256,1024]{1,0:T(8,128)(2,1)S(1)} %get-tuple-element.11, bf16[5120,1024]{1,0:T(8,128)(2,1)} %param.15), kind=kOutput, calls=%fused_computation.12 | convolution fusion | flops 2693524224 | bytes 18917376 | tf_op jit(solution)/shard_map/dot_general | solution.py:43
  38.9 3.1 fusion.8
  42.0 3.2 reshape.80
  45.2 0.1 fusion.21
  45.3 0.1 reduce_window_sum.11
  45.4 0.2 select_reduce_fusion
  45.6 3.9 convolution_convert_fusion
  49.4 8.1 %all_to_all.8 = bf16[16,32,5120]{2,1,0:T(8,128)(2,1)} reshape(bf16[64,40960]{1,0:T(8,128)(2,1)} %convolution_convert_fusion) | data formatting | bytes 10485760 | tf_op jit(solution)/shard_map/all_to_all | solution.py:76
  57.5 7.3 %all-to-all-start = ((bf16[16,32,5120]{2,1,0:T(8,128)(2,1)}), bf16[16,32,5120]{2,1,0:T(8,128)(2,1)}, u32[]{:S(2)}, u32[]{:S(2)}) async-start(bf16[16,32,5120]{2,1,0:T(8,128)(2,1)} %all_to_all.8), calls=%async_computation | async-start | bytes 10485760 | tf_op jit(solution)/shard_map/all_to_all | solution.py:76
  64.9 0.0 all-reduce.3.cloned.1.call-start
  64.9 204.5 %reduce-scatter.2.cloned.1.call-done = f32[2560,1024]{1,0:T(8,128)} async-done(((f32[5120,1024]{1,0:T(8,128)}), f32[2560,1024]{1,0:T(8,128)}) %reduce-scatter.2.cloned.1.call-update) | async-done | bytes 10485776 | tf_op jit(solution)/shard_map/reduce_scatter | solution.py:83
  269.4 0.0 all-reduce.3.cloned.1.call-update
  269.5 41.3 %all-reduce = (f32[5120]{0:T(1024)}, f32[128]{0:T(128)}) all-reduce(f32[5120]{0:T(1024)S(1)} %get-tuple-element.4, f32[128]{0:T(128)S(1)} %bitcast_reduce_fusion), channel_id=1, replica_groups=mesh['gen'=2,'learn'=16] {'gen','learn'}, use_global_device_ids=true, to_apply=%region_9.10 | all-reduce | flops 5248 | bytes 41984 | tf_op jit(solution)/shard_map/psum | solution.py:92
  310.8 0.0 all-to-all-done
  310.8 164.6 %all-reduce.3.cloned.1.call-done = f32[2560,1024]{1,0:T(8,128)} async-done(((f32[2560,1024]{1,0:T(8,128)}), f32[2560,1024]{1,0:T(8,128)}) %all-reduce.3.cloned.1.call-update) | async-done | bytes 10485776 | tf_op jit(solution)/shard_map/psum | solution.py:91
  475.5 5.6 %copy.32 = bf16[512,5120]{1,0:T(8,128)(2,1)} copy(bf16[512,5120]{1,0:T(8,128)(2,1)} %bitcast.2) | data formatting | bytes 10485760
  481.1 1.8 copy-done.1
  482.9 4.1 copy.33
  (15 shorter events, 0.1 us)
Async XLA Ops:
  7.2 262.3 %reduce-scatter.2.cloned.1.call-start = ((), (), s32[]{:S(2)}) async-start(), calls=%async_computation.2 | async-start | bytes 31457280 | tf_op jit(solution)/shard_map/reduce_scatter | solution.py:83
  11.7 6.8 %copy-start.7 = (f32[256]{0:T(256)S(1)}, f32[256]{0:T(256)}, u32[]{:S(2)}) copy-start(f32[256]{0:T(256)} %param.11) | copy-start | bytes 3076
  11.7 6.8 %copy-start.3 = (bf16[256,1024]{1,0:T(8,128)(2,1)S(1)}, bf16[256,1024]{1,0:T(8,128)(2,1)}, u32[]{:S(2)}) copy-start(bf16[256,1024]{1,0:T(8,128)(2,1)} %param.10) | copy-start | bytes 1572868
  18.3 1.4 copy-start.2
  18.3 0.7 copy-start.5
  19.7 4.0 copy-start
  19.7 4.0 copy-start.4
  42.0 3.2 copy-start.6
  57.5 253.3 %all-to-all-start = ((bf16[16,32,5120]{2,1,0:T(8,128)(2,1)}), bf16[16,32,5120]{2,1,0:T(8,128)(2,1)}, u32[]{:S(2)}, u32[]{:S(2)}) async-start(bf16[16,32,5120]{2,1,0:T(8,128)(2,1)} %all_to_all.8), calls=%async_computation | async-start | bytes 10485760 | tf_op jit(solution)/shard_map/all_to_all | solution.py:76
  64.9 410.6 %all-reduce.3.cloned.1.call-start = ((), (), s32[]{:S(2)}) async-start(), calls=%async_computation.3 | async-start | bytes 20971520 | tf_op jit(solution)/shard_map/psum | solution.py:91
  475.5 7.4 %copy-start.1 = (f32[2560,1024]{1,0:T(8,128)S(1)}, f32[2560,1024]{1,0:T(8,128)}, u32[]{:S(2)}) copy-start(f32[2560,1024]{1,0:T(8,128)} %all-reduce.3.cloned.1.call-done) | copy-start | bytes 31457284
Sparse Core Ops, SparseCore 0:
  32.5 236.8 reduce-scatter.1
  273.2 202.2 all-reduce.2
where the time goes:
time: 494 us
  waiting for transfers between devices  369 us (75%)
  blocking collectives  41.3 us (8%)
  local copies, waits for them, and re-layouts  25.6 us (5%)
  matrix products  25.5 us (5%)
  between operations  14.3 us (3%)
  other arithmetic  10.5 us (2%)
  starting transfers between devices  7.41 us (2%)
    reduce_scatter x1, waiting for transfers between devices, body(): lax.psum_scatter(lax.dot_general(h_rows, grad_keys, (((0,), (0,)), ((), (...  205 us
    psum x1, waiting for transfers between devices, body(): w_grad = lax.psum(partial_rows, 'learn')  165 us
    psum x1, blocking collectives, body(): gain_grad, kgain_grad = lax.psum((gain_part, kgain_part), ('gen', 'learn'))  41.3 us
    unnamed x20, local copies, waits for them, and re-layouts  12 us
  transfers between devices with their start and end apart: 3, of which 2 were waited for; matrix products, arithmetic and copies ran while one was open for 3% of the time, Pallas kernels for 0%

commit v1 on v0

v1 whole, which is shorter than its diff:
```python
import jax
import jax.numpy as jnp
from jax import lax
from jax.sharding import PartitionSpec as P

TILE = 8
VERSIONS = 4
SLOTS = 64


epsilon = 1e-06
clip_ratio = 2.0
staleness = 0.5


def token_weights(importance, block_len, version):
    tile_count = block_len.shape[0]
    inside = (lax.broadcasted_iota(jnp.int32, (tile_count, TILE), 1) < block_len[:, None]).astype(
        jnp.float32
    )
    stale_age = (VERSIONS - 1 - version).astype(jnp.float32)
    decay_factor = jnp.power(jnp.float32(staleness), stale_age)
    return jnp.minimum(importance, clip_ratio) * (decay_factor[:, None] * inside).reshape(-1)


def swap(x, axis, size, bit):
    return lax.ppermute(x, axis, [(i, i ^ bit) for i in range(size)])


def shift(x, axis, size, step):
    return lax.ppermute(x, axis, [(i, (i + step) % size) for i in range(size)])


def butterfly_sum(x, axes):
    for axis, size in axes:
        bit = 1
        while bit < size:
            x = x + swap(x, axis, size, bit)
            bit *= 2
    return x


def join(mine, other, upper):
    place = lax.broadcasted_iota(jnp.int32, (2,) + (1,) * mine.ndim, 0)
    both = jnp.where(place == upper, mine[None], other[None])
    return both.reshape((2 * mine.shape[0],) + mine.shape[1:])


def dot_rows(a, b):
    return lax.dot_general(a, b, (((0,), (0,)), ((), ())), preferred_element_type=jnp.float32)


def weight_gradient(h_rows, grad_keys, gens, learners):
    gen, learn = lax.axis_index("gen"), lax.axis_index("learn")
    width = h_rows.shape[1] // gens
    half = width // 2

    def columns(step):
        return lax.dynamic_slice_in_dim(h_rows, ((gen + step) % gens) * width, width, 1)

    h_all, k_all = [columns(0)], [grad_keys]
    for step in range(1, gens):
        h_all.append(shift(columns(step), "gen", gens, step))
        k_all.append(shift(grad_keys, "gen", gens, step))
    core = learn % 2
    total = 0.0
    for h_part, k_part in zip(h_all, k_all):
        own = lax.dynamic_slice_in_dim(h_part, core * half, half, 1)
        for_other = lax.dynamic_slice_in_dim(h_part, (1 - core) * half, half, 1)
        total = total + dot_rows(own, k_part)
        total = total + dot_rows(
            swap(for_other, "learn", learners, 1), swap(k_part, "learn", learners, 1)
        )
    bits = []
    bit = 2
    while bit < learners:
        upper = (learn // bit) % 2
        rows = total.shape[0] // 2
        sent = lax.dynamic_slice_in_dim(total, (1 - upper) * rows, rows, 0).astype(jnp.bfloat16)
        kept = lax.dynamic_slice_in_dim(total, upper * rows, rows, 0)
        total = kept + swap(sent, "learn", learners, bit).astype(jnp.float32)
        bits.append(bit)
        bit *= 2
    block = total.astype(jnp.bfloat16)
    for bit in reversed(bits):
        block = join(block, swap(block, "learn", learners, bit), (learn // bit) % 2)
    other = swap(block, "learn", learners, 1)
    return join(block.astype(jnp.float32), other.astype(jnp.float32), core)


def body(hidden, cotangent, importance, block_len, version, destination, w_key, in_gain, key_gain):
    learners = lax.axis_size("learn")
    gens = lax.axis_size("gen")
    capacity = SLOTS // learners
    tile_count = block_len.shape[0]
    row_count = hidden.shape[0]
    weights = token_weights(importance, block_len, version)
    upstream_all = (cotangent.astype(jnp.float32) * weights[:, None]).astype(jnp.bfloat16)
    dest_column = destination[:, 0]
    onehot = (dest_column[:, None] == jnp.arange(learners, dtype=jnp.int32)[None, :]).astype(
        jnp.int32
    )
    slot_rank = jnp.sum((jnp.cumsum(onehot, 0) - onehot) * onehot, 1)
    target = dest_column * capacity + slot_rank
    rows_to = (target[:, None] * TILE + jnp.arange(TILE, dtype=jnp.int32)[None, :]).reshape(-1)
    placing = (
        rows_to[None, :] == jnp.arange(SLOTS * TILE, dtype=jnp.int32)[:, None]
    ).astype(jnp.bfloat16)

    x_float = hidden.astype(jnp.float32)
    inv_rms = lax.rsqrt(jnp.mean(x_float * x_float, -1, keepdims=True) + epsilon)
    normed = x_float * inv_rms
    h_rows = (normed * in_gain).astype(jnp.bfloat16)
    key_rows = jnp.dot(h_rows, w_key, preferred_element_type=jnp.float32).reshape(
        row_count, -1, key_gain.shape[0]
    )
    key_scale = lax.rsqrt(jnp.mean(key_rows * key_rows, -1, keepdims=True) + epsilon)
    upstream = upstream_all.astype(jnp.float32).reshape(key_rows.shape)
    kgain_part = jnp.sum(upstream * key_rows * key_scale, axis=(0, 1))
    scaled = upstream * key_gain
    grad_keys = key_scale * scaled - key_rows * key_scale**3 * jnp.mean(
        scaled * key_rows, -1, keepdims=True
    )
    grad_keys = grad_keys.reshape(row_count, -1).astype(jnp.bfloat16)
    grad_h = lax.dot_general(
        grad_keys, w_key, (((1,), (1,)), ((), ())), preferred_element_type=jnp.float32
    )
    gain_part = jnp.sum(grad_h * normed, 0)
    grad_normed = grad_h * in_gain
    grad_input = inv_rms * (
        grad_normed - normed * jnp.mean(grad_normed * normed, -1, keepdims=True)
    )
    spread = jnp.dot(
        placing, grad_input.astype(jnp.bfloat16), preferred_element_type=jnp.float32
    ).astype(jnp.bfloat16)
    grad_slots = lax.all_to_all(spread, "learn", split_axis=0, concat_axis=0, tiled=True)
    w_grad = weight_gradient(h_rows, grad_keys, gens, learners)
    features = hidden.shape[1]
    sums = butterfly_sum(
        jnp.concatenate([gain_part, kgain_part]), (("gen", gens), ("learn", learners))
    )
    return (grad_slots, w_grad, sums[:features], sums[features:])


def solution(mesh):
    return jax.shard_map(
        body,
        mesh=mesh,
        in_specs=(
            P(("gen", "learn"), None),
            P(("gen", "learn"), None),
            P(("gen", "learn")),
            P(("gen", "learn")),
            P(("gen", "learn")),
            P(("gen", "learn"), None),
            P(),
            P(),
            P(),
        ),
        out_specs=(P(("gen", "learn"), None), P("gen", None), P(), P()),
        check_vma=False,
    )
```

time: 494 us -> 289 us (0.59)
  waiting for transfers between devices: 369 us -> 183 us
  blocking collectives: 41.3 us -> 0 us
  other arithmetic: 10.5 us -> 31.6 us
  starting transfers between devices: 7.41 us -> 24.1 us
  between operations: 14.3 us -> 1.16 us
    reduce_scatter x1 -> x0, waiting for transfers between devices: 205 us -> none  [body(): lax.psum_scatter(lax.dot_general(h_rows, grad_keys, (((0,), (0,)), ((), (...]
    ppermute x0 -> x18, waiting for transfers between devices: none -> 183 us  [the longest x16 175 us: swap(): return lax.ppermute(x, axis, [(i, i ^ bit) for i in range(size)])]
    psum x1 -> x0, waiting for transfers between devices: 165 us -> none  [body(): w_grad = lax.psum(partial_rows, 'learn')]
    psum x1 -> x0, blocking collectives: 41.3 us -> none  [body(): gain_grad, kgain_grad = lax.psum((gain_part, kgain_part), ('gen', 'learn'))]
    ppermute x0 -> x18, starting transfers between devices: none -> 17.7 us  [the longest x16 14.6 us: swap(): return lax.ppermute(x, axis, [(i, i ^ bit) for i in range(size)])]
    select_n x0 -> x3, other arithmetic: none -> 9.55 us  [join(): both = jnp.where(place == upper, mine[None], other[None])]
    all_to_all x1 -> x0, local copies, waits for them, and re-layouts: 8.12 us -> none  [body(): lax.all_to_all(spread.astype(jnp.bfloat16).reshape(SLOTS * TILE, feature_...]
    dynamic_slice x0 -> x3, local copies, waits for them, and re-layouts: none -> 5.88 us  [the longest x2 3.37 us: weight_gradient(): for_other = lax.dynamic_slice_in_dim(h_part, (1 - core) * half, half, 1)]
  transfers between devices with their start and end apart: 3 -> 19, of which waited for: 2 -> 12; matrix products, arithmetic and copies ran while one was open for 3% -> 19% of each run, Pallas kernels for 0% -> 0%
where the time goes in v1:
time: 289 us; the launch traced here: 288 us
  waiting for transfers between devices  183 us (63%)
  other arithmetic  31.6 us (11%)
  matrix products  27.2 us (9%)
  starting transfers between devices  24.1 us (8%)
  local copies, waits for them, and re-layouts  21.1 us (7%)
    ppermute x16, waiting for transfers between devices, swap(): return lax.ppermute(x, axis, [(i, i ^ bit) for i in range(size)])  175 us
    ppermute x16, starting transfers between devices, swap(): return lax.ppermute(x, axis, [(i, i ^ bit) for i in range(size)])  14.6 us
    unnamed x21, local copies, waits for them, and re-layouts  10.8 us
    dot_general x1, matrix products, body(): lax.dot_general(grad_keys, w_key, (((1,), (1,)), ((), ())), preferred_ele...  9.97 us
    select_n x3, other arithmetic, join(): both = jnp.where(place == upper, mine[None], other[None])  9.55 us
    ppermute x2, waiting for transfers between devices, shift(): return lax.ppermute(x, axis, [(i, (i + step) % size) for i in range(size)])  8.26 us
    dot_general x4, matrix products, dot_rows(): lax.dot_general(a, b, (((0,), (0,)), ((), ())), preferred_element_type=jn...  7.48 us
    dot_general x1, matrix products, body(): jnp.dot(placing, grad_input.astype(jnp.bfloat16), preferred_element_type=...  6.88 us
  transfers between devices with their start and end apart: 19, of which 12 were waited for; matrix products, arithmetic and copies ran while one was open for 19% of the time, Pallas kernels for 0%

profile of v1, /device:TPU:0, one launch (start us, length us, event | category | flops | bytes accessed | tf_op | source)
XLA Modules:
  0.0 288.4 jit_solution(1166343632442982509)
XLA Ops:
  0.7 0.8 convert_power_fusion
  1.5 2.3 fusion.10
  3.8 0.7 broadcast_bitcast_fusion
  4.5 0.7 fusion.26
  5.3 0.7 minimum_multiply_fusion
  6.0 1.3 convert_bitcast_fusion
  7.7 0.8 fusion.4
  8.4 1.7 copy-done.8
  10.1 2.9 fusion.33
  13.2 0.6 multiply_reduce_fusion.1
  15.6 2.4 fusion.19
  18.0 3.0 %collective-permute-start.3 = (bf16[256,1024]{1,0:T(8,128)(2,1)S(1)}, bf16[256,1024]{1,0:T(8,128)(2,1)}, u32[]{:S(2)}, u32[]{:S(2)}) collective-permute-start(bf16[256,1024]{1,0:T(8,128)(2,1)S(1)} %get-tuple-element.11), channel_id=1, source_target_pairs={{0,16},{16,0},{1,17},{17,1},{2,18},{18,2},{3,19},{19,3},{4,20},{20... | collective-permute-start | bytes 1572872 | tf_op jit(solution)/shard_map/ppermute | solution.py:31
  21.0 2.2 constant_dynamic-slice_fusion.2
  23.7 2.5 constant_dynamic-slice_fusion.1
  26.3 10.0 %fusion.9 = (f32[5120]{0:T(1024)S(1)}, f32[256]{0:T(256)S(1)}, f32[256,5120]{1,0:T(8,128)}) fusion(bf16[256,5120]{1,0:T(8,128)(2,1)S(1)} %copy-done, f32[256]{0:T(256)S(1)} %add_rsqrt_fusion.1, f32[5120]{0:T(1024)S(1)} %copy-done.5, bf16[256,1024]{1,0:T(8,128)(2,1)S(1)} %get-tuple-element.11, bf16[5120,1024]{1,0:T(8,128)(2,1)} %param.15), kind=kOutput, calls=%fused_computation.13 | convolution fusion | flops 2693524224 | bytes 18917376 | tf_op jit(solution)/shard_map/dot_general | solution.py:125
  36.8 6.9 %convolution_convert_fusion = bf16[512,5120]{1,0:T(8,128)(2,1)} fusion(bf16[256,5120]{1,0:T(8,128)(2,1)S(1)} %copy-done, f32[256,5120]{1,0:T(8,128)} %get-tuple-element.14, f32[256]{0:T(256)S(1)} %broadcast_multiply_fusion.1, f32[5120]{0:T(1024)S(1)} %copy-done.5, f32[256]{0:T(256)S(1)} %add_rsqrt_fusion.1, s32[256]{0:T(256)S(1)} %add.155), kind=kOutput, calls=%fused_computation.1 | convolution fusion | flops 1354104832 | bytes 13130752 | tf_op jit(solution)/shard_map/dot_general | solution.py:133
  43.7 6.4 %all-to-all-start = ((bf16[16,32,5120]{2,1,0:T(8,128)(2,1)}), bf16[16,32,5120]{2,1,0:T(8,128)(2,1)}, u32[]{:S(2)}, u32[]{:S(2)}) async-start(bf16[16,32,5120]{2,1,0:T(8,128)(2,1)} %bitcast.63), calls=%async_computation | async-start | bytes 10485760 | tf_op jit(solution)/shard_map/all_to_all | solution.py:136
  50.1 2.3 fusion.22
  52.8 8.3 %collective-permute-done.2 = bf16[256,2560]{1,0:T(8,128)(2,1)} collective-permute-done((bf16[256,2560]{1,0:T(8,128)(2,1)}, bf16[256,2560]{1,0:T(8,128)(2,1)}, u32[]{:S(2)}, u32[]{:S(2)}) %collective-permute-start.2) | collective-permute-done | bytes 1310752 | tf_op jit(solution)/shard_map/ppermute | solution.py:31
  61.1 1.1 constant_dynamic-slice_fusion
  62.3 2.1 fusion.34
  64.4 2.1 fusion.20
  66.6 0.9 add_add_fusion
  67.5 2.3 copy-done.1
  70.1 1.8 collective-permute-start.6
  71.9 56.8 %collective-permute-done.6 = bf16[640,1024]{1,0:T(8,128)(2,1)} collective-permute-done((bf16[640,1024]{1,0:T(8,128)(2,1)S(1)}, bf16[640,1024]{1,0:T(8,128)(2,1)}, u32[]{:S(2)}, u32[]{:S(2)}) %collective-permute-start.6) | collective-permute-done | bytes 1310752 | tf_op jit(solution)/shard_map/ppermute | solution.py:27
  128.7 2.5 convert_add_fusion
  131.5 30.4 %collective-permute-done.7 = bf16[320,1024]{1,0:T(8,128)(2,1)} collective-permute-done((bf16[320,1024]{1,0:T(8,128)(2,1)S(1)}, bf16[320,1024]{1,0:T(8,128)(2,1)}, u32[]{:S(2)}, u32[]{:S(2)}) %collective-permute-start.7) | collective-permute-done | bytes 655392 | tf_op jit(solution)/shard_map/ppermute | solution.py:27
  161.9 1.2 convert_add_fusion.1
  163.2 1.0 copy-done.4
  164.3 18.4 %collective-permute-done.8 = bf16[160,1024]{1,0:T(8,128)(2,1)S(1)} collective-permute-done((bf16[160,1024]{1,0:T(8,128)(2,1)S(1)}, bf16[160,1024]{1,0:T(8,128)(2,1)S(1)}, u32[]{:S(2)}, u32[]{:S(2)}) %collective-permute-start.8) | collective-permute-done | bytes 327712 | tf_op jit(solution)/shard_map/ppermute | solution.py:27
  182.7 1.2 add_convert_fusion
  184.2 14.1 %collective-permute-done.9 = bf16[160,1024]{1,0:T(8,128)(2,1)S(1)} collective-permute-done((bf16[160,1024]{1,0:T(8,128)(2,1)S(1)}, bf16[160,1024]{1,0:T(8,128)(2,1)S(1)}, u32[]{:S(2)}, u32[]{:S(2)}) %collective-permute-start.9) | collective-permute-done | bytes 327712 | tf_op jit(solution)/shard_map/ppermute | solution.py:27
  198.7 13.6 %collective-permute-done.10 = bf16[320,1024]{1,0:T(8,128)(2,1)S(1)} collective-permute-done((bf16[320,1024]{1,0:T(8,128)(2,1)S(1)}, bf16[320,1024]{1,0:T(8,128)(2,1)S(1)}, u32[]{:S(2)}, u32[]{:S(2)}) %collective-permute-start.10) | collective-permute-done | bytes 655392 | tf_op jit(solution)/shard_map/ppermute | solution.py:27
  212.5 7.6 %collective-permute-start.11 = (bf16[640,1024]{1,0:T(8,128)(2,1)S(1)}, bf16[640,1024]{1,0:T(8,128)(2,1)S(1)}, u32[]{:S(2)}, u32[]{:S(2)}) collective-permute-start(bf16[640,1024]{1,0:T(8,128)(2,1)S(1)} %bitcast_select_fusion.2), channel_id=1, source_target_pairs={{0,2},{1,3},{2,0},{3,1},{4,6},{5,7},{6,4},{7,5},{8,10},{9,11},{10,... | collective-permute-start | bytes 3932168 | tf_op jit(solution)/shard_map/ppermute | solution.py:27
  220.2 28.0 %collective-permute-done.11 = bf16[640,1024]{1,0:T(8,128)(2,1)S(1)} collective-permute-done((bf16[640,1024]{1,0:T(8,128)(2,1)S(1)}, bf16[640,1024]{1,0:T(8,128)(2,1)S(1)}, u32[]{:S(2)}, u32[]{:S(2)}) %collective-permute-start.11) | collective-permute-done | bytes 1310752 | tf_op jit(solution)/shard_map/ppermute | solution.py:27
  248.2 3.8 %fusion.32 = (f32[1280,1024]{1,0:T(8,128)}, bf16[1280,1024]{1,0:T(8,128)(2,1)}) fusion(bf16[640,1024]{1,0:T(8,128)(2,1)S(1)} %collective-permute-done.11, bf16[640,1024]{1,0:T(8,128)(2,1)S(1)} %bitcast_select_fusion.2, pred[1280]{0:T(1024)(128)(4,1)S(1)} %broadcast_in_dim.152), kind=kLoop, calls=%fused_computation.77 | loop fusion | flops 2621440 | bytes 10487040 | tf_op jit(solution)/shard_map/convert_element_type | solution.py:88
  252.1 1.6 collective-permute-start.13
  253.6 2.3 collective-permute-done.13
  256.0 1.2 collective-permute-done.14
  257.2 1.7 collective-permute-start.15
  258.9 2.1 collective-permute-done.15
  261.6 3.2 %collective-permute-done.16 = f32[5248]{0:T(1024)S(1)} collective-permute-done((f32[5248]{0:T(1024)S(1)}, f32[5248]{0:T(1024)S(1)}, u32[]{:S(2)}, u32[]{:S(2)}) %collective-permute-start.16) | collective-permute-done | bytes 21024 | tf_op jit(solution)/shard_map/ppermute | solution.py:27
  264.9 4.9 %collective-permute-done.17 = f32[5248]{0:T(1024)S(1)} collective-permute-done((f32[5248]{0:T(1024)S(1)}, f32[5248]{0:T(1024)S(1)}, u32[]{:S(2)}, u32[]{:S(2)}) %collective-permute-start.17) | collective-permute-done | bytes 21024 | tf_op jit(solution)/shard_map/ppermute | solution.py:27
  270.3 0.6 slice.8
  271.0 3.0 %convert_element_type.81 = f32[1280,1024]{1,0:T(8,128)} convert(bf16[1280,1024]{1,0:T(8,128)(2,1)S(1)} %collective-permute-done.12) | non-fusion elementwise | flops 1310720 | bytes 7864320 | tf_op jit(solution)/shard_map/convert_element_type | solution.py:88
  274.0 9.2 %bitcast_select_fusion = f32[2560,1024]{1,0:T(8,128)} fusion(f32[1280,1024]{1,0:T(8,128)} %convert_element_type.81, f32[1280,1024]{1,0:T(8,128)} %get-tuple-element.8, pred[2560]{0:T(1024)(128)(4,1)S(1)} %broadcast_in_dim.149), kind=kLoop, calls=%fused_computation | loop fusion | flops 2621440 | bytes 20974080 | tf_op jit(solution)/shard_map/jit(_where)/select_n | solution.py:45
  283.2 5.2 %copy.31 = bf16[512,5120]{1,0:T(8,128)(2,1)} copy(bf16[512,5120]{1,0:T(8,128)(2,1)} %bitcast.5) | data formatting | bytes 10485760
  (82 shorter events, 6.5 us)
Async XLA Ops:
  0.6 7.0 %copy-start = (bf16[256,5120]{1,0:T(8,128)(2,1)S(1)}, bf16[256,5120]{1,0:T(8,128)(2,1)}, u32[]{:S(2)}) copy-start(bf16[256,5120]{1,0:T(8,128)(2,1)} %param.9) | copy-start | bytes 7864324
  0.6 6.9 %copy-start.6 = (f32[128]{0:T(128)S(1)}, f32[128]{0:T(128)}, u32[]{:S(2)}) copy-start(f32[128]{0:T(128)} %param.17) | copy-start | bytes 1540
  0.7 7.0 %copy-start.5 = (f32[5120]{0:T(1024)S(1)}, f32[5120]{0:T(1024)}, u32[]{:S(2)}) copy-start(f32[5120]{0:T(1024)} %param.16) | copy-start | bytes 61444
  6.0 4.1 %copy-start.8 = (bf16[5120,1024]{1,0:T(8,128)(2,1)S(1)}, bf16[5120,1024]{1,0:T(8,128)(2,1)}, u32[]{:S(2)}) copy-start(bf16[5120,1024]{1,0:T(8,128)(2,1)} %param.15) | copy-start | bytes 31457284
  10.1 2.9 copy-start.2
  13.0 1.0 copy-start.3
  18.0 34.5 %collective-permute-start.3 = (bf16[256,1024]{1,0:T(8,128)(2,1)S(1)}, bf16[256,1024]{1,0:T(8,128)(2,1)}, u32[]{:S(2)}, u32[]{:S(2)}) collective-permute-start(bf16[256,1024]{1,0:T(8,128)(2,1)S(1)} %get-tuple-element.11), channel_id=1, source_target_pairs={{0,16},{16,0},{1,17},{17,1},{2,18},{18,2},{3,19},{19,3},{4,20},{20... | collective-permute-start | bytes 1572872 | tf_op jit(solution)/shard_map/ppermute | solution.py:31
  21.0 41.3 %collective-permute-start.1 = (bf16[256,1024]{1,0:T(8,128)(2,1)S(1)}, bf16[256,1024]{1,0:T(8,128)(2,1)}, u32[]{:S(2)}, u32[]{:S(2)}) collective-permute-start(bf16[256,1024]{1,0:T(8,128)(2,1)S(1)} %get-tuple-element.11), channel_id=1, source_target_pairs={{0,1},{1,0},{2,3},{3,2},{4,5},{5,4},{6,7},{7,6},{8,9},{9,8},{10,11... | collective-permute-start | bytes 1572872 | tf_op jit(solution)/shard_map/ppermute | solution.py:27
  23.2 39.1 %collective-permute-start = (bf16[256,1280]{1,0:T(8,128)(2,1)}, bf16[256,1280]{1,0:T(8,128)(2,1)}, u32[]{:S(2)}, u32[]{:S(2)}) collective-permute-start(bf16[256,1280]{1,0:T(8,128)(2,1)} %constant_dynamic-slice_fusion.2), channel_id=1, source_target_pairs={{0,1},{1,0},{2,3},{3,2},{4,5},{5,4},{6,7},{7,6},{8,9},{9,8},{10,11... | collective-permute-start | bytes 1966088 | tf_op jit(solution)/shard_map/ppermute | solution.py:27
  26.2 10.1 %copy-start.7 = (s32[32,1]{0,1:T(1,128)S(1)}, s32[32,1]{0,1:T(1,128)}, u32[]{:S(2)}) copy-start(s32[32,1]{0,1:T(1,128)} %param.14) | copy-start | bytes 388
  26.2 34.9 %collective-permute-start.2 = (bf16[256,2560]{1,0:T(8,128)(2,1)}, bf16[256,2560]{1,0:T(8,128)(2,1)}, u32[]{:S(2)}, u32[]{:S(2)}) collective-permute-start(bf16[256,2560]{1,0:T(8,128)(2,1)} %constant_dynamic-slice_fusion.1), channel_id=1, source_target_pairs={{0,16},{16,0},{1,17},{17,1},{2,18},{18,2},{3,19},{19,3},{4,20},{20... | collective-permute-start | bytes 3932168 | tf_op jit(solution)/shard_map/ppermute | solution.py:31
  43.7 239.5 %all-to-all-start = ((bf16[16,32,5120]{2,1,0:T(8,128)(2,1)}), bf16[16,32,5120]{2,1,0:T(8,128)(2,1)}, u32[]{:S(2)}, u32[]{:S(2)}) async-start(bf16[16,32,5120]{2,1,0:T(8,128)(2,1)} %bitcast.63), calls=%async_computation | async-start | bytes 10485760 | tf_op jit(solution)/shard_map/all_to_all | solution.py:136
  52.5 14.1 %collective-permute-start.5 = (bf16[256,1024]{1,0:T(8,128)(2,1)}, bf16[256,1024]{1,0:T(8,128)(2,1)S(1)}, u32[]{:S(2)}, u32[]{:S(2)}) collective-permute-start(bf16[256,1024]{1,0:T(8,128)(2,1)} %collective-permute-done.3), channel_id=1, source_target_pairs={{0,1},{1,0},{2,3},{3,2},{4,5},{5,4},{6,7},{7,6},{8,9},{9,8},{10,11... | collective-permute-start | bytes 1572872 | tf_op jit(solution)/shard_map/ppermute | solution.py:27
  62.2 4.4 %collective-permute-start.4 = (bf16[256,1280]{1,0:T(8,128)(2,1)S(1)}, bf16[256,1280]{1,0:T(8,128)(2,1)S(1)}, u32[]{:S(2)}, u32[]{:S(2)}) collective-permute-start(bf16[256,1280]{1,0:T(8,128)(2,1)S(1)} %constant_dynamic-slice_fusion), channel_id=1, source_target_pairs={{0,1},{1,0},{2,3},{3,2},{4,5},{5,4},{6,7},{7,6},{8,9},{9,8},{10,11... | collective-permute-start | bytes 1966088 | tf_op jit(solution)/shard_map/ppermute | solution.py:27
  67.5 2.4 copy-start.1
  70.1 58.6 %collective-permute-start.6 = (bf16[640,1024]{1,0:T(8,128)(2,1)S(1)}, bf16[640,1024]{1,0:T(8,128)(2,1)}, u32[]{:S(2)}, u32[]{:S(2)}) collective-permute-start(bf16[640,1024]{1,0:T(8,128)(2,1)S(1)} %dynamic-slice_convert_fusion), channel_id=1, source_target_pairs={{0,2},{1,3},{2,0},{3,1},{4,6},{5,7},{6,4},{7,5},{8,10},{9,11},{10,... | collective-permute-start | bytes 3932168 | tf_op jit(solution)/shard_map/ppermute | solution.py:27
  131.3 30.5 %collective-permute-start.7 = (bf16[320,1024]{1,0:T(8,128)(2,1)S(1)}, bf16[320,1024]{1,0:T(8,128)(2,1)}, u32[]{:S(2)}, u32[]{:S(2)}) collective-permute-start(bf16[320,1024]{1,0:T(8,128)(2,1)S(1)} %dynamic-slice_convert_fusion.1), channel_id=1, source_target_pairs={{0,4},{1,5},{2,6},{3,7},{4,0},{5,1},{6,2},{7,3},{8,12},{9,13},{10,... | collective-permute-start | bytes 1966088 | tf_op jit(solution)/shard_map/ppermute | solution.py:27
  163.1 1.1 copy-start.4
  164.2 18.5 %collective-permute-start.8 = (bf16[160,1024]{1,0:T(8,128)(2,1)S(1)}, bf16[160,1024]{1,0:T(8,128)(2,1)S(1)}, u32[]{:S(2)}, u32[]{:S(2)}) collective-permute-start(bf16[160,1024]{1,0:T(8,128)(2,1)S(1)} %dynamic-slice_convert_fusion.2), channel_id=1, source_target_pairs={{0,8},{1,9},{2,10},{3,11},{4,12},{5,13},{6,14},{7,15},{8,0},{9,1},... | collective-permute-start | bytes 983048 | tf_op jit(solution)/shard_map/ppermute | solution.py:27
  183.9 14.4 %collective-permute-start.9 = (bf16[160,1024]{1,0:T(8,128)(2,1)S(1)}, bf16[160,1024]{1,0:T(8,128)(2,1)S(1)}, u32[]{:S(2)}, u32[]{:S(2)}) collective-permute-start(bf16[160,1024]{1,0:T(8,128)(2,1)S(1)} %add_convert_fusion), channel_id=1, source_target_pairs={{0,8},{1,9},{2,10},{3,11},{4,12},{5,13},{6,14},{7,15},{8,0},{9,1},... | collective-permute-start | bytes 983048 | tf_op jit(solution)/shard_map/ppermute | solution.py:27
  198.4 13.9 %collective-permute-start.10 = (bf16[320,1024]{1,0:T(8,128)(2,1)S(1)}, bf16[320,1024]{1,0:T(8,128)(2,1)S(1)}, u32[]{:S(2)}, u32[]{:S(2)}) collective-permute-start(bf16[320,1024]{1,0:T(8,128)(2,1)S(1)} %bitcast_select_fusion.3), channel_id=1, source_target_pairs={{0,4},{1,5},{2,6},{3,7},{4,0},{5,1},{6,2},{7,3},{8,12},{9,13},{10,... | collective-permute-start | bytes 1966088 | tf_op jit(solution)/shard_map/ppermute | solution.py:27
  212.5 35.8 %collective-permute-start.11 = (bf16[640,1024]{1,0:T(8,128)(2,1)S(1)}, bf16[640,1024]{1,0:T(8,128)(2,1)S(1)}, u32[]{:S(2)}, u32[]{:S(2)}) collective-permute-start(bf16[640,1024]{1,0:T(8,128)(2,1)S(1)} %bitcast_select_fusion.2), channel_id=1, source_target_pairs={{0,2},{1,3},{2,0},{3,1},{4,6},{5,7},{6,4},{7,5},{8,10},{9,11},{10,... | collective-permute-start | bytes 3932168 | tf_op jit(solution)/shard_map/ppermute | solution.py:27
  252.0 18.9 %collective-permute-start.12 = (bf16[1280,1024]{1,0:T(8,128)(2,1)}, bf16[1280,1024]{1,0:T(8,128)(2,1)S(1)}, u32[]{:S(2)}, u32[]{:S(2)}) collective-permute-start(bf16[1280,1024]{1,0:T(8,128)(2,1)} %get-tuple-element.9), channel_id=1, source_target_pairs={{0,1},{1,0},{2,3},{3,2},{4,5},{5,4},{6,7},{7,6},{8,9},{9,8},{10,11... | collective-permute-start | bytes 7864328 | tf_op jit(solution)/shard_map/ppermute | solution.py:27
  252.1 3.9 %collective-permute-start.13 = (f32[5248]{0:T(1024)S(1)}, f32[5248]{0:T(1024)S(1)}, u32[]{:S(2)}, u32[]{:S(2)}) collective-permute-start(f32[5248]{0:T(1024)S(1)} %pad_maximum_fusion), channel_id=1, source_target_pairs={{0,16},{16,0},{1,17},{17,1},{2,18},{18,2},{3,19},{19,3},{4,20},{20... | collective-permute-start | bytes 62984 | tf_op jit(solution)/shard_map/ppermute | solution.py:27
  256.0 1.2 collective-permute-start.14
  257.2 3.8 %collective-permute-start.15 = (f32[5248]{0:T(1024)S(1)}, f32[5248]{0:T(1024)S(1)}, u32[]{:S(2)}, u32[]{:S(2)}) collective-permute-start(f32[5248]{0:T(1024)S(1)} %add.185), channel_id=1, source_target_pairs={{0,2},{1,3},{2,0},{3,1},{4,6},{5,7},{6,4},{7,5},{8,10},{9,11},{10,... | collective-permute-start | bytes 62984 | tf_op jit(solution)/shard_map/ppermute | solution.py:27
  261.0 3.8 %collective-permute-start.16 = (f32[5248]{0:T(1024)S(1)}, f32[5248]{0:T(1024)S(1)}, u32[]{:S(2)}, u32[]{:S(2)}) collective-permute-start(f32[5248]{0:T(1024)S(1)} %add.186), channel_id=1, source_target_pairs={{0,4},{1,5},{2,6},{3,7},{4,0},{5,1},{6,2},{7,3},{8,12},{9,13},{10,... | collective-permute-start | bytes 62984 | tf_op jit(solution)/shard_map/ppermute | solution.py:27
  264.8 5.0 %collective-permute-start.17 = (f32[5248]{0:T(1024)S(1)}, f32[5248]{0:T(1024)S(1)}, u32[]{:S(2)}, u32[]{:S(2)}) collective-permute-start(f32[5248]{0:T(1024)S(1)} %add.187), channel_id=1, source_target_pairs={{0,8},{1,9},{2,10},{3,11},{4,12},{5,13},{6,14},{7,15},{8,0},{9,1},... | collective-permute-start | bytes 62984 | tf_op jit(solution)/shard_map/ppermute | solution.py:27

commit v2 on v1

--- a/solution.py
+++ b/solution.py
@@ -6,6 +6,9 @@
 TILE = 8
 VERSIONS = 4
 SLOTS = 64
+PACKET = 72
+PASSED_ON = 48
+TAGS = 128
 
 
 epsilon = 1e-06
@@ -88,6 +91,80 @@
     return join(block.astype(jnp.float32), other.astype(jnp.float32), core)
 
 
+def swap_dense(grad_input, target, learners):
+    rows_to = (target[:, None] * TILE + jnp.arange(TILE, dtype=jnp.int32)[None, :]).reshape(-1)
+    place = jnp.arange(SLOTS * TILE, dtype=jnp.int32)[:, None]
+    spread = jnp.dot(
+        (rows_to[None, :] == place).astype(jnp.bfloat16),
+        grad_input,
+        preferred_element_type=jnp.float32,
+    )
+    return lax.all_to_all(
+        spread.astype(jnp.bfloat16), "learn", split_axis=0, concat_axis=0, tiled=True
+    )
+
+
+def packet_plan(block_len, dest_column, slot_rank, learners):
+    learn = lax.axis_index("learn")
+    planes = learners // 4
+    capacity = SLOTS // learners
+    packet = min(PACKET, 4 * capacity * TILE)
+    passed_on = min(PASSED_ON, 2 * capacity * TILE)
+    rows = block_len.shape[0] * TILE
+    row = jnp.arange(rows, dtype=jnp.int32)
+    dest = jnp.repeat(dest_column, TILE)
+    valid = row % TILE < jnp.repeat(block_len, TILE)
+    apart = dest ^ learn
+    plane = jnp.where(valid, apart // 4, planes)
+    other_y = (apart // 2) % 2
+    kinds = jnp.arange(2 * planes, dtype=jnp.int32)
+    member = (plane * 2 + other_y)[None, :] == kinds[:, None]
+    before = (row[:, None] < row[None, :]).astype(jnp.bfloat16)
+    ahead = jnp.dot(
+        member.astype(jnp.bfloat16), before, preferred_element_type=jnp.float32
+    ).astype(jnp.int32)
+    count = jnp.sum(member.astype(jnp.int32), 1)
+    start = (kinds // 2) * packet + jnp.where(kinds % 2 == 1, packet - count, 0)
+    position = jnp.sum(jnp.where(member, ahead + start[:, None], 0), 0)
+    position = jnp.where(valid, position, -1)
+    count = count.reshape(planes, 2)
+    over = jnp.any((count[:, 0] + count[:, 1] > packet) | (count[:, 1] > passed_on))
+    slot = learn * capacity + jnp.repeat(slot_rank, TILE)
+    tags = jnp.stack([dest + 1, slot, row % TILE], 1)
+    tags = jnp.pad(tags, ((0, 0), (0, TAGS - 3))).astype(jnp.bfloat16)
+    return position, tags, over, packet, passed_on
+
+
+def swap_packets(rows_with_tags, position, packet, passed_on, learners):
+    planes = learners // 4
+    place = jnp.arange(planes * packet, dtype=jnp.int32)[:, None]
+    packed = jnp.dot(
+        (position[None, :] == place).astype(jnp.bfloat16),
+        rows_with_tags,
+        preferred_element_type=jnp.float32,
+    ).astype(jnp.bfloat16)
+    held = []
+    for k in range(planes):
+        part = packed[k * packet : (k + 1) * packet]
+        if k:
+            part = swap(part, "learn", learners, 4 * k)
+        held.append(part)
+    held += [swap(part[packet - passed_on :], "learn", learners, 2) for part in held]
+    held += [swap(part, "learn", learners, 1) for part in held]
+    return held
+
+
+def place_packets(held, features):
+    everything = jnp.concatenate(held, 0)
+    tags = everything[:, features : features + 3].astype(jnp.int32)
+    mine = tags[:, 0] == lax.axis_index("learn") + 1
+    target = jnp.where(mine, tags[:, 1] * TILE + tags[:, 2], -1)
+    place = jnp.arange(SLOTS * TILE, dtype=jnp.int32)[None, :]
+    return dot_rows(
+        (target[:, None] == place).astype(jnp.bfloat16), everything[:, :features]
+    ).astype(jnp.bfloat16)
+
+
 def body(hidden, cotangent, importance, block_len, version, destination, w_key, in_gain, key_gain):
     learners = lax.axis_size("learn")
     gens = lax.axis_size("gen")
@@ -102,10 +179,9 @@
     )
     slot_rank = jnp.sum((jnp.cumsum(onehot, 0) - onehot) * onehot, 1)
     target = dest_column * capacity + slot_rank
-    rows_to = (target[:, None] * TILE + jnp.arange(TILE, dtype=jnp.int32)[None, :]).reshape(-1)
-    placing = (
-        rows_to[None, :] == jnp.arange(SLOTS * TILE, dtype=jnp.int32)[:, None]
-    ).astype(jnp.bfloat16)
+    position, tags, over, packet, passed_on = packet_plan(
+        block_len, dest_column, slot_rank, learners
+    )
 
     x_float = hidden.astype(jnp.float32)
     inv_rms = lax.rsqrt(jnp.mean(x_float * x_float, -1, keepdims=True) + epsilon)
@@ -130,16 +206,23 @@
     grad_input = inv_rms * (
         grad_normed - normed * jnp.mean(grad_normed * normed, -1, keepdims=True)
     )
-    spread = jnp.dot(
-        placing, grad_input.astype(jnp.bfloat16), preferred_element_type=jnp.float32
-    ).astype(jnp.bfloat16)
-    grad_slots = lax.all_to_all(spread, "learn", split_axis=0, concat_axis=0, tiled=True)
+    grad_input = grad_input.astype(jnp.bfloat16)
+    held = swap_packets(
+        jnp.concatenate([grad_input, tags], 1), position, packet, passed_on, learners
+    )
     w_grad = weight_gradient(h_rows, grad_keys, gens, learners)
     features = hidden.shape[1]
+    flag = jnp.where(over, 1.0, 0.0) * jnp.ones((key_gain.shape[0],), jnp.float32)
     sums = butterfly_sum(
-        jnp.concatenate([gain_part, kgain_part]), (("gen", gens), ("learn", learners))
-    )
-    return (grad_slots, w_grad, sums[:features], sums[features:])
+        jnp.concatenate([gain_part, kgain_part, flag]), (("gen", gens), ("learn", learners))
+    )
+    grad_slots = lax.cond(
+        sums[-1] > 0.5,
+        lambda: swap_dense(grad_input, target, learners),
+        lambda: place_packets(held, features),
+    )
+    heads_end = features + key_gain.shape[0]
+    return (grad_slots, w_grad, sums[:features], sums[features:heads_end])
 
 
 def solution(mesh):

time: 289 us -> 387 us (1.34)
  local copies, waits for them, and re-layouts: 21.1 us -> 89.8 us
  matrix products: 27.2 us -> 38.5 us
  starting transfers between devices: 24.1 us -> 34.1 us
  other arithmetic: 31.6 us -> 36.9 us
    another operation x0 -> x17, local copies, waits for them, and re-layouts: none -> 36.6 us
    concatenate x0 -> x1, local copies, waits for them, and re-layouts: none -> 24.6 us  [place_packets(): everything = jnp.concatenate(held, 0)]
    ppermute x16 -> x31, starting transfers between devices: 14.6 us -> 31.1 us  [swap(): return lax.ppermute(x, axis, [(i, i ^ bit) for i in range(size)])]
    dot_general x4 -> x5, matrix products: 7.48 us -> 20.7 us  [dot_rows(): lax.dot_general(a, b, (((0,), (0,)), ((), ())), preferred_element_type=jn...]
    ppermute x16 -> x31, waiting for transfers between devices: 175 us -> 162 us  [swap(): return lax.ppermute(x, axis, [(i, i ^ bit) for i in range(size)])]
    ppermute x2, waiting for transfers between devices: 8.26 us -> 20 us  [shift(): return lax.ppermute(x, axis, [(i, (i + step) % size) for i in range(size)])]
    slice x2 -> x8, local copies, waits for them, and re-layouts: 1.12 us -> 7.94 us  [the longest x1 3.26 us: swap_packets(): part = packed[k * packet:(k + 1) * packet]]
    all_to_all x1 -> x0, starting transfers between devices: 6.41 us -> none  [body(): lax.all_to_all(spread, 'learn', split_axis=0, concat_axis=0, tiled=True)]
  transfers between devices with their start and end apart: 19 -> 33, of which waited for: 12 -> 14; matrix products, arithmetic and copies ran while one was open for 19% -> 31% of each run, Pallas kernels for 0% -> 0%
where the time goes in v2:
time: 387 us; the launch traced here: 384 us
  waiting for transfers between devices  182 us (47%)
  local copies, waits for them, and re-layouts  89.8 us (23%)
  matrix products  38.5 us (10%)
  other arithmetic  36.9 us (10%)
  starting transfers between devices  34.1 us (9%)
    ppermute x31, waiting for transfers between devices, swap(): return lax.ppermute(x, axis, [(i, i ^ bit) for i in range(size)])  162 us
    another operation x16, local copies, waits for them, and re-layouts  36.4 us
    ppermute x31, starting transfers between devices, swap(): return lax.ppermute(x, axis, [(i, i ^ bit) for i in range(size)])  31.1 us
    concatenate x1, local copies, waits for them, and re-layouts, place_packets(): everything = jnp.concatenate(held, 0)  24.6 us
    dot_general x5, matrix products, dot_rows(): lax.dot_general(a, b, (((0,), (0,)), ((), ())), preferred_element_type=jn...  20.7 us
    ppermute x2, waiting for transfers between devices, shift(): return lax.ppermute(x, axis, [(i, (i + step) % size) for i in range(size)])  20 us
    select_n x3, other arithmetic, join(): both = jnp.where(place == upper, mine[None], other[None])  11.7 us
    convert_element_type x2, other arithmetic, weight_gradient(): return join(block.astype(jnp.float32), other.astype(jnp.float32), core)  10.2 us
  transfers between devices with their start and end apart: 33, of which 14 were waited for; matrix products, arithmetic and copies ran while one was open for 31% of the time, Pallas kernels for 0%

profile of v2, /device:TPU:0, one launch (start us, length us, event | category | flops | bytes accessed | tf_op | source)
XLA Modules:
  0.0 383.9 jit_solution(3682089832034687263)
XLA Ops:
  1.4 2.4 fusion.20
  7.6 6.7 %fusion.59 = f32[256,1024]{1,0:T(8,128)S(1)} fusion(bf16[256,5120]{1,0:T(8,128)(2,1)S(1)} %fusion.14, bf16[5120,1024]{1,0:T(8,128)(2,1)} %param.17), kind=kOutput, calls=%fused_computation.136 | convolution fusion | flops 2684354560 | bytes 14155776 | tf_op jit(solution)/shard_map/dot_general | solution.py:190
  19.2 3.0 collective-permute-start.23
  22.2 2.2 constant_dynamic-slice_fusion.2
  24.9 2.5 constant_dynamic-slice_fusion.1
  27.5 9.9 %fusion.16 = (f32[256]{0:T(256)S(1)}, f32[5120]{0:T(1024)S(1)}, f32[256,5120]{1,0:T(8,128)}) fusion(bf16[256,5120]{1,0:T(8,128)(2,1)S(1)} %copy-done, f32[5120]{0:T(1024)S(1)} %copy-done.12, f32[256]{0:T(256)S(1)} %add_rsqrt_fusion.1, bf16[256,1024]{1,0:T(8,128)(2,1)S(1)} %get-tuple-element.158, bf16[5120,1024]{1,0:T(8,128)(2,1)} %param.17), kind=kOutput, calls=%fused_computation.27 | convolution fusion | flops 2693524224 | bytes 18917376 | tf_op jit(solution)/shard_map/dot_general | solution.py:201
  37.4 4.7 %fusion.37 = f32[1280,1024]{1,0:T(8,128)} fusion(bf16[256,1024]{1,0:T(8,128)(2,1)S(1)} %get-tuple-element.158, bf16[256,5120]{1,0:T(8,128)(2,1)} %copy-done.1, s32[]{:T(128)S(6)} %dynamic_slice.40), kind=kOutput, calls=%fused_computation.67 | convolution fusion | flops 671088640 | bytes 6422532 | tf_op jit(solution)/shard_map/dot_general | solution.py:53
  42.3 20.0 %collective-permute-done.22 = bf16[256,2560]{1,0:T(8,128)(2,1)} collective-permute-done((bf16[256,2560]{1,0:T(8,128)(2,1)}, bf16[256,2560]{1,0:T(8,128)(2,1)}, u32[]{:S(2)}, u32[]{:S(2)}) %collective-permute-start.22) | collective-permute-done | bytes 1310752 | tf_op jit(solution)/shard_map/ppermute | solution.py:34
  63.7 2.3 fusion.60
  66.1 2.3 fusion.35
  71.4 3.3 fusion.19
  74.7 25.9 %collective-permute-done.26 = bf16[640,1024]{1,0:T(8,128)(2,1)S(1)} collective-permute-done((bf16[640,1024]{1,0:T(8,128)(2,1)S(1)}, bf16[640,1024]{1,0:T(8,128)(2,1)S(1)}, u32[]{:S(2)}, u32[]{:S(2)}) %collective-permute-start.26) | collective-permute-done | bytes 1310752 | tf_op jit(solution)/shard_map/ppermute | solution.py:30
  105.6 13.3 %collective-permute-done.27 = bf16[320,1024]{1,0:T(8,128)(2,1)} collective-permute-done((bf16[320,1024]{1,0:T(8,128)(2,1)S(1)}, bf16[320,1024]{1,0:T(8,128)(2,1)}, u32[]{:S(2)}, u32[]{:S(2)}) %collective-permute-start.27) | collective-permute-done | bytes 655392 | tf_op jit(solution)/shard_map/ppermute | solution.py:30
  120.6 2.8 collective-permute-start.28
  123.6 13.3 %collective-permute-done.28 = bf16[160,1024]{1,0:T(8,128)(2,1)S(1)} collective-permute-done((bf16[160,1024]{1,0:T(8,128)(2,1)S(1)}, bf16[160,1024]{1,0:T(8,128)(2,1)S(1)}, u32[]{:S(2)}, u32[]{:S(2)}) %collective-permute-start.28) | collective-permute-done | bytes 327712 | tf_op jit(solution)/shard_map/ppermute | solution.py:30
  137.2 16.2 %collective-permute-done.29 = bf16[160,1024]{1,0:T(8,128)(2,1)S(1)} collective-permute-done((bf16[160,1024]{1,0:T(8,128)(2,1)S(1)}, bf16[160,1024]{1,0:T(8,128)(2,1)S(1)}, u32[]{:S(2)}, u32[]{:S(2)}) %collective-permute-start.29) | collective-permute-done | bytes 327712 | tf_op jit(solution)/shard_map/ppermute | solution.py:30
  158.9 9.5 %collective-permute-done.30 = bf16[320,1024]{1,0:T(8,128)(2,1)} collective-permute-done((bf16[320,1024]{1,0:T(8,128)(2,1)S(1)}, bf16[320,1024]{1,0:T(8,128)(2,1)}, u32[]{:S(2)}, u32[]{:S(2)}) %collective-permute-start.30) | collective-permute-done | bytes 655392 | tf_op jit(solution)/shard_map/ppermute | solution.py:30
  168.4 2.4 bitcast_select_fusion.2
  172.5 3.3 fusion.58
  175.7 3.2 collective-permute-start.7
  179.1 19.8 %collective-permute-done.31 = bf16[640,1024]{1,0:T(8,128)(2,1)} collective-permute-done((bf16[640,1024]{1,0:T(8,128)(2,1)}, bf16[640,1024]{1,0:T(8,128)(2,1)}, u32[]{:S(2)}, u32[]{:S(2)}) %collective-permute-start.31) | collective-permute-done | bytes 1310752 | tf_op jit(solution)/shard_map/ppermute | solution.py:30
  198.8 5.5 %fusion.57 = (f32[1280,1024]{1,0:T(8,128)}, bf16[1280,1024]{1,0:T(8,128)(2,1)}) fusion(bf16[640,1024]{1,0:T(8,128)(2,1)} %collective-permute-done.31, bf16[640,1024]{1,0:T(8,128)(2,1)} %bitcast_select_fusion.2, pred[1280]{0:T(1024)(128)(4,1)S(1)} %broadcast_in_dim.187), kind=kLoop, calls=%fused_computation.134 | loop fusion | flops 2621440 | bytes 10487040 | tf_op jit(solution)/shard_map/convert_element_type | solution.py:91
  207.6 4.3 %collective-permute-start.6 = (bf16[72,5248]{1,0:T(8,128)(2,1)}, bf16[72,5248]{1,0:T(8,128)(2,1)S(1)}, u32[]{:S(2)}, u32[]{:S(2)}) collective-permute-start(bf16[72,5248]{1,0:T(8,128)(2,1)} %get-tuple-element.155), channel_id=1, source_target_pairs={{0,8},{1,9},{2,10},{3,11},{4,12},{5,13},{6,14},{7,15},{8,0},{9,1},... | collective-permute-start | bytes 2267144 | tf_op jit(solution)/shard_map/ppermute | solution.py:30
  214.7 2.3 collective-permute-done.2
  218.4 10.8 %collective-permute-done.3 = f32[5376]{0:T(1024)S(1)} collective-permute-done((f32[5376]{0:T(1024)S(1)}, f32[5376]{0:T(1024)S(1)}, u32[]{:S(2)}, u32[]{:S(2)}) %collective-permute-start.3) | collective-permute-done | bytes 21536 | tf_op jit(solution)/shard_map/ppermute | solution.py:30
  231.4 15.2 %collective-permute-done.4 = f32[5376]{0:T(1024)S(1)} collective-permute-done((f32[5376]{0:T(1024)S(1)}, f32[5376]{0:T(1024)S(1)}, u32[]{:S(2)}, u32[]{:S(2)}) %collective-permute-start.4) | collective-permute-done | bytes 21536 | tf_op jit(solution)/shard_map/ppermute | solution.py:30
  250.5 14.9 %collective-permute-done.5 = bf16[72,5248]{1,0:T(8,128)(2,1)} collective-permute-done((bf16[72,5248]{1,0:T(8,128)(2,1)}, bf16[72,5248]{1,0:T(8,128)(2,1)}, u32[]{:S(2)}, u32[]{:S(2)}) %collective-permute-start.5) | collective-permute-done | bytes 755744 | tf_op jit(solution)/shard_map/ppermute | solution.py:30
  269.2 10.8 %collective-permute-done.10 = bf16[48,5248]{1,0:T(8,128)(2,1)} collective-permute-done((bf16[48,5248]{1,0:T(8,128)(2,1)S(1)}, bf16[48,5248]{1,0:T(8,128)(2,1)}, u32[]{:S(2)}, u32[]{:S(2)}) %collective-permute-start.10) | collective-permute-done | bytes 503840 | tf_op jit(solution)/shard_map/ppermute | solution.py:30
  280.0 8.6 %collective-permute-done.9 = bf16[48,5248]{1,0:T(8,128)(2,1)} collective-permute-done((bf16[48,5248]{1,0:T(8,128)(2,1)S(1)}, bf16[48,5248]{1,0:T(8,128)(2,1)}, u32[]{:S(2)}, u32[]{:S(2)}) %collective-permute-start.9) | collective-permute-done | bytes 503840 | tf_op jit(solution)/shard_map/ppermute | solution.py:30
  292.5 72.2 %conditional.1 = (bf16[512,5120]{1,0:T(8,128)(2,1)}) conditional(s32[]{:T(128)} %bitcast.6, (bf16[72,5248]{1,0:T(8,128)(2,1)S(1)}, bf16[72,5248]{1,0:T(8,128)(2,1)}, bf16[72,5248]{1,0:T(8,128)(2,1)}, bf16[72,5248]{1,0:T(8,128)(2,1)}, bf16[48,5248]{1,0:T(8,128)(2,1)}, /*index=5*/bf16[48,5248]{1,0:T(8,128)(2,1)}, bf16[48,5248]{1,0:T(8,128)(2,1)}, ...), branch_computations={%region_12.13_spmd, %region_13.14_spmd} | conditional | flops 5036775936 | bytes 56069804 | solution.py:219
  296.3 2.4 copy.104
  298.7 2.4 copy.103
  301.1 2.4 copy.102
  303.5 2.4 copy.101
  305.9 2.4 copy.100
  308.3 2.4 copy.99
  310.7 2.4 copy.98
  313.1 2.3 copy.97
  315.5 2.4 copy.96
  317.8 2.4 copy.95
  320.2 2.4 copy.94
  322.6 2.4 copy.93
  325.0 2.4 copy.92
  328.9 24.6 %concatenate.6 = bf16[960,5248]{0,1:T(8,128)(2,1)} concatenate(bf16[72,5248]{0,1:T(8,128)(2,1)} %copy.91, bf16[72,5248]{0,1:T(8,128)(2,1)} %copy.92, bf16[72,5248]{0,1:T(8,128)(2,1)} %copy.93, bf16[72,5248]{0,1:T(8,128)(2,1)} %copy.94, bf16[48,5248]{0,1:T(8,128)(2,1)} %copy.95, bf16[48,5248]{0,1:T(8,128)(2,1)} %copy.96, bf16[48,5248]{0,1:T(8,128)(2,1)} %copy.97, ...), dimensions={0} | concatenate | bytes 20152320 | tf_op jit(solution)/shard_map/cond/branch_0_fun/concatenate | solution.py:158
  354.3 10.5 %fusion.2 = bf16[512,5120]{1,0:T(8,128)(2,1)} fusion(bf16[960,5248]{0,1:T(8,128)(2,1)} %concatenate.6, s32[960]{0:T(1024)S(1)} %bitcast.74), kind=kOutput, calls=%fused_computation.2 | convolution fusion | flops 5036769280 | bytes 15732480 | tf_op jit(solution)/shard_map/cond/branch_0_fun/dot_general | solution.py:53
  364.7 4.7 %convert_element_type.111 = f32[1280,1024]{1,0:T(8,128)} convert(bf16[1280,1024]{1,0:T(8,128)(2,1)} %collective-permute-done.32) | non-fusion elementwise | flops 1310720 | bytes 7864320 | tf_op jit(solution)/shard_map/convert_element_type | solution.py:91
  369.4 9.2 %bitcast_select_fusion = f32[2560,1024]{1,0:T(8,128)} fusion(f32[1280,1024]{1,0:T(8,128)} %convert_element_type.111, f32[1280,1024]{1,0:T(8,128)} %get-tuple-element.152, pred[2560]{0:T(1024)(128)(4,1)S(1)} %broadcast_in_dim.184), kind=kLoop, calls=%fused_computation.15 | loop fusion | flops 2621440 | bytes 20974080 | tf_op jit(solution)/shard_map/jit(_where)/select_n | solution.py:48
  378.7 5.2 %copy.119 = bf16[512,5120]{1,0:T(8,128)(2,1)} copy(bf16[512,5120]{1,0:T(8,128)(2,1)} %get-tuple-element.173) | data formatting | bytes 10485760
  (180 shorter events, 54.6 us)
Async XLA Ops:
  0.6 5.7 %copy-start.8 = (bf16[256,1024]{1,0:T(8,128)(2,1)S(1)}, bf16[256,1024]{1,0:T(8,128)(2,1)}, u32[]{:S(2)}) copy-start(bf16[256,1024]{1,0:T(8,128)(2,1)} %param.12) | copy-start | bytes 1572868
  1.4 5.3 %copy-start.14 = (f32[128]{0:T(128)S(1)}, f32[128]{0:T(128)}, u32[]{:S(2)}) copy-start(f32[128]{0:T(128)} %param.19) | copy-start | bytes 1540
  3.7 3.0 copy-start
  3.7 3.1 copy-start.12
  7.6 6.7 %copy-start.1 = (bf16[256,5120]{1,0:T(8,128)(2,1)}, bf16[256,5120]{1,0:T(8,128)(2,1)S(1)}, u32[]{:S(2)}) copy-start(bf16[256,5120]{1,0:T(8,128)(2,1)S(1)} %fusion.14) | copy-start | bytes 7864324
  19.2 23.1 %collective-permute-start.23 = (bf16[256,1024]{1,0:T(8,128)(2,1)S(1)}, bf16[256,1024]{1,0:T(8,128)(2,1)}, u32[]{:S(2)}, u32[]{:S(2)}) collective-permute-start(bf16[256,1024]{1,0:T(8,128)(2,1)S(1)} %get-tuple-element.158), channel_id=1, source_target_pairs={{0,16},{16,0},{1,17},{17,1},{2,18},{18,2},{3,19},{19,3},{4,20},{20... | collective-permute-start | bytes 1572872 | tf_op jit(solution)/shard_map/ppermute | solution.py:34
  22.2 41.5 %collective-permute-start.21 = (bf16[256,1024]{1,0:T(8,128)(2,1)S(1)}, bf16[256,1024]{1,0:T(8,128)(2,1)}, u32[]{:S(2)}, u32[]{:S(2)}) collective-permute-start(bf16[256,1024]{1,0:T(8,128)(2,1)S(1)} %get-tuple-element.158), channel_id=1, source_target_pairs={{0,1},{1,0},{2,3},{3,2},{4,5},{5,4},{6,7},{7,6},{8,9},{9,8},{10,11... | collective-permute-start | bytes 1572872 | tf_op jit(solution)/shard_map/ppermute | solution.py:30
  24.4 39.3 %collective-permute-start.20 = (bf16[256,1280]{1,0:T(8,128)(2,1)}, bf16[256,1280]{1,0:T(8,128)(2,1)}, u32[]{:S(2)}, u32[]{:S(2)}) collective-permute-start(bf16[256,1280]{1,0:T(8,128)(2,1)} %constant_dynamic-slice_fusion.2), channel_id=1, source_target_pairs={{0,1},{1,0},{2,3},{3,2},{4,5},{5,4},{6,7},{7,6},{8,9},{9,8},{10,11... | collective-permute-start | bytes 1966088 | tf_op jit(solution)/shard_map/ppermute | solution.py:30
  27.4 34.9 %collective-permute-start.22 = (bf16[256,2560]{1,0:T(8,128)(2,1)}, bf16[256,2560]{1,0:T(8,128)(2,1)}, u32[]{:S(2)}, u32[]{:S(2)}) collective-permute-start(bf16[256,2560]{1,0:T(8,128)(2,1)} %constant_dynamic-slice_fusion.1), channel_id=1, source_target_pairs={{0,16},{16,0},{1,17},{17,1},{2,18},{18,2},{3,19},{19,3},{4,20},{20... | collective-permute-start | bytes 3932168 | tf_op jit(solution)/shard_map/ppermute | solution.py:34
  37.4 4.7 %copy-start.13 = (s32[32,1]{0,1:T(1,128)S(1)}, s32[32,1]{0,1:T(1,128)}, u32[]{:S(2)}) copy-start(s32[32,1]{0,1:T(1,128)} %param.16) | copy-start | bytes 388
  42.3 26.1 %collective-permute-start.25 = (bf16[256,1024]{1,0:T(8,128)(2,1)}, bf16[256,1024]{1,0:T(8,128)(2,1)S(1)}, u32[]{:S(2)}, u32[]{:S(2)}) collective-permute-start(bf16[256,1024]{1,0:T(8,128)(2,1)} %collective-permute-done.23), channel_id=1, source_target_pairs={{0,1},{1,0},{2,3},{3,2},{4,5},{5,4},{6,7},{7,6},{8,9},{9,8},{10,11... | collective-permute-start | bytes 1572872 | tf_op jit(solution)/shard_map/ppermute | solution.py:30
  62.3 6.1 %slice-start = ((s8[5242880]{0:T(1024)(128)(4,1)}), s8[4194304]{0:T(1024)(128)(4,1)S(1)}, s32[]{:S(2)}) async-start(s8[5242880]{0:T(1024)(128)(4,1)} %bitcast.60), calls=%async_computation.1 | async-start | bytes 8388608
  63.6 4.8 %slice-start.1 = ((s8[5242880]{0:T(1024)(128)(4,1)}), s8[1048576]{0:T(1024)(128)(4,1)S(1)}, s32[]{:S(2)}) async-start(s8[5242880]{0:T(1024)(128)(4,1)} %bitcast.60), calls=%async_computation.2 | async-start | bytes 2097152
  63.6 4.7 %collective-permute-start.24 = (bf16[256,1280]{1,0:T(8,128)(2,1)S(1)}, bf16[256,1280]{1,0:T(8,128)(2,1)S(1)}, u32[]{:S(2)}, u32[]{:S(2)}) collective-permute-start(bf16[256,1280]{1,0:T(8,128)(2,1)S(1)} %constant_dynamic-slice_fusion), channel_id=1, source_target_pairs={{0,1},{1,0},{2,3},{3,2},{4,5},{5,4},{6,7},{7,6},{8,9},{9,8},{10,11... | collective-permute-start | bytes 1966088 | tf_op jit(solution)/shard_map/ppermute | solution.py:30
  66.0 5.3 %slice-start.2 = ((s8[5242880]{0:T(1024)(128)(4,1)}), s8[4194304]{0:T(1024)(128)(4,1)S(1)}, s32[]{:S(2)}) async-start(s8[5242880]{0:T(1024)(128)(4,1)} %bitcast.64), calls=%async_computation.3 | async-start | bytes 8388608
  68.3 3.1 slice-start.3
  69.6 31.0 %collective-permute-start.26 = (bf16[640,1024]{1,0:T(8,128)(2,1)S(1)}, bf16[640,1024]{1,0:T(8,128)(2,1)S(1)}, u32[]{:S(2)}, u32[]{:S(2)}) collective-permute-start(bf16[640,1024]{1,0:T(8,128)(2,1)S(1)} %dynamic-slice_convert_fusion), channel_id=1, source_target_pairs={{0,2},{1,3},{2,0},{3,1},{4,6},{5,7},{6,4},{7,5},{8,10},{9,11},{10,... | collective-permute-start | bytes 3932168 | tf_op jit(solution)/shard_map/ppermute | solution.py:30
  101.0 1.5 copy-start.3
  102.6 16.3 %collective-permute-start.27 = (bf16[320,1024]{1,0:T(8,128)(2,1)S(1)}, bf16[320,1024]{1,0:T(8,128)(2,1)}, u32[]{:S(2)}, u32[]{:S(2)}) collective-permute-start(bf16[320,1024]{1,0:T(8,128)(2,1)S(1)} %dynamic-slice_convert_fusion.1), channel_id=1, source_target_pairs={{0,4},{1,5},{2,6},{3,7},{4,0},{5,1},{6,2},{7,3},{8,12},{9,13},{10,... | collective-permute-start | bytes 1966088 | tf_op jit(solution)/shard_map/ppermute | solution.py:30
  105.6 48.1 %copy-start.2 = (bf16[256,5120]{1,0:T(8,128)(2,1)S(1)}, bf16[256,5120]{1,0:T(8,128)(2,1)}, u32[]{:S(2)}) copy-start(bf16[256,5120]{1,0:T(8,128)(2,1)} %fusion.19) | copy-start | bytes 7864324
  120.6 16.2 %collective-permute-start.28 = (bf16[160,1024]{1,0:T(8,128)(2,1)S(1)}, bf16[160,1024]{1,0:T(8,128)(2,1)S(1)}, u32[]{:S(2)}, u32[]{:S(2)}) collective-permute-start(bf16[160,1024]{1,0:T(8,128)(2,1)S(1)} %dynamic-slice_convert_fusion.2), channel_id=1, source_target_pairs={{0,8},{1,9},{2,10},{3,11},{4,12},{5,13},{6,14},{7,15},{8,0},{9,1},... | collective-permute-start | bytes 983048 | tf_op jit(solution)/shard_map/ppermute | solution.py:30
  137.0 16.5 %collective-permute-start.29 = (bf16[160,1024]{1,0:T(8,128)(2,1)S(1)}, bf16[160,1024]{1,0:T(8,128)(2,1)S(1)}, u32[]{:S(2)}, u32[]{:S(2)}) collective-permute-start(bf16[160,1024]{1,0:T(8,128)(2,1)S(1)} %add_convert_fusion), channel_id=1, source_target_pairs={{0,8},{1,9},{2,10},{3,11},{4,12},{5,13},{6,14},{7,15},{8,0},{9,1},... | collective-permute-start | bytes 983048 | tf_op jit(solution)/shard_map/ppermute | solution.py:30
  153.6 14.8 %collective-permute-start.30 = (bf16[320,1024]{1,0:T(8,128)(2,1)S(1)}, bf16[320,1024]{1,0:T(8,128)(2,1)}, u32[]{:S(2)}, u32[]{:S(2)}) collective-permute-start(bf16[320,1024]{1,0:T(8,128)(2,1)S(1)} %bitcast_select_fusion.3), channel_id=1, source_target_pairs={{0,4},{1,5},{2,6},{3,7},{4,0},{5,1},{6,2},{7,3},{8,12},{9,13},{10,... | collective-permute-start | bytes 1966088 | tf_op jit(solution)/shard_map/ppermute | solution.py:30
  154.7 1.6 copy-start.6
  157.1 90.2 %collective-permute-start.8 = (bf16[48,5248]{1,0:T(8,128)(2,1)}, bf16[48,5248]{1,0:T(8,128)(2,1)}, u32[]{:S(2)}, u32[]{:S(2)}) collective-permute-start(bf16[48,5248]{1,0:T(8,128)(2,1)} %slice.79), channel_id=1, source_target_pairs={{0,2},{1,3},{2,0},{3,1},{4,6},{5,7},{6,4},{7,5},{8,10},{9,11},{10,... | collective-permute-start | bytes 1511432 | tf_op jit(solution)/shard_map/ppermute | solution.py:30
  170.8 28.1 %collective-permute-start.31 = (bf16[640,1024]{1,0:T(8,128)(2,1)}, bf16[640,1024]{1,0:T(8,128)(2,1)}, u32[]{:S(2)}, u32[]{:S(2)}) collective-permute-start(bf16[640,1024]{1,0:T(8,128)(2,1)} %bitcast_select_fusion.2), channel_id=1, source_target_pairs={{0,2},{1,3},{2,0},{3,1},{4,6},{5,7},{6,4},{7,5},{8,10},{9,11},{10,... | collective-permute-start | bytes 3932168 | tf_op jit(solution)/shard_map/ppermute | solution.py:30
  175.7 71.6 %collective-permute-start.7 = (bf16[72,5248]{1,0:T(8,128)(2,1)}, bf16[72,5248]{1,0:T(8,128)(2,1)}, u32[]{:S(2)}, u32[]{:S(2)}) collective-permute-start(bf16[72,5248]{1,0:T(8,128)(2,1)} %get-tuple-element.154), channel_id=1, source_target_pairs={{0,12},{1,13},{2,14},{3,15},{4,8},{5,9},{6,10},{7,11},{8,4},{9,5},... | collective-permute-start | bytes 2267144 | tf_op jit(solution)/shard_map/ppermute | solution.py:30
  204.3 160.4 %collective-permute-start.32 = (bf16[1280,1024]{1,0:T(8,128)(2,1)}, bf16[1280,1024]{1,0:T(8,128)(2,1)}, u32[]{:S(2)}, u32[]{:S(2)}) collective-permute-start(bf16[1280,1024]{1,0:T(8,128)(2,1)} %get-tuple-element.153), channel_id=1, source_target_pairs={{0,1},{1,0},{2,3},{3,2},{4,5},{5,4},{6,7},{7,6},{8,9},{9,8},{10,11... | collective-permute-start | bytes 7864328 | tf_op jit(solution)/shard_map/ppermute | solution.py:30
  205.8 6.2 %collective-permute-start = (f32[5376]{0:T(1024)S(1)}, f32[5376]{0:T(1024)S(1)}, u32[]{:S(2)}, u32[]{:S(2)}) collective-permute-start(f32[5376]{0:T(1024)S(1)} %pad_maximum_fusion), channel_id=1, source_target_pairs={{0,16},{16,0},{1,17},{17,1},{2,18},{18,2},{3,19},{19,3},{4,20},{20... | collective-permute-start | bytes 64520 | tf_op jit(solution)/shard_map/ppermute | solution.py:30
  207.6 41.3 %collective-permute-start.6 = (bf16[72,5248]{1,0:T(8,128)(2,1)}, bf16[72,5248]{1,0:T(8,128)(2,1)S(1)}, u32[]{:S(2)}, u32[]{:S(2)}) collective-permute-start(bf16[72,5248]{1,0:T(8,128)(2,1)} %get-tuple-element.155), channel_id=1, source_target_pairs={{0,8},{1,9},{2,10},{3,11},{4,12},{5,13},{6,14},{7,15},{8,0},{9,1},... | collective-permute-start | bytes 2267144 | tf_op jit(solution)/shard_map/ppermute | solution.py:30
  211.9 1.3 collective-permute-start.1
  213.2 3.8 collective-permute-start.2
  217.0 12.2 %collective-permute-start.3 = (f32[5376]{0:T(1024)S(1)}, f32[5376]{0:T(1024)S(1)}, u32[]{:S(2)}, u32[]{:S(2)}) collective-permute-start(f32[5376]{0:T(1024)S(1)} %add.280), channel_id=1, source_target_pairs={{0,4},{1,5},{2,6},{3,7},{4,0},{5,1},{6,2},{7,3},{8,12},{9,13},{10,... | collective-permute-start | bytes 64520 | tf_op jit(solution)/shard_map/ppermute | solution.py:30
  229.2 17.4 %collective-permute-start.4 = (f32[5376]{0:T(1024)S(1)}, f32[5376]{0:T(1024)S(1)}, u32[]{:S(2)}, u32[]{:S(2)}) collective-permute-start(f32[5376]{0:T(1024)S(1)} %add.281), channel_id=1, source_target_pairs={{0,8},{1,9},{2,10},{3,11},{4,12},{5,13},{6,14},{7,15},{8,0},{9,1},... | collective-permute-start | bytes 64520 | tf_op jit(solution)/shard_map/ppermute | solution.py:30
  246.6 18.8 %collective-permute-start.5 = (bf16[72,5248]{1,0:T(8,128)(2,1)}, bf16[72,5248]{1,0:T(8,128)(2,1)}, u32[]{:S(2)}, u32[]{:S(2)}) collective-permute-start(bf16[72,5248]{1,0:T(8,128)(2,1)} %get-tuple-element.156), channel_id=1, source_target_pairs={{0,4},{1,5},{2,6},{3,7},{4,0},{5,1},{6,2},{7,3},{8,12},{9,13},{10,... | collective-permute-start | bytes 2267144 | tf_op jit(solution)/shard_map/ppermute | solution.py:30
  247.3 19.7 %collective-permute-start.12 = (bf16[72,5248]{1,0:T(8,128)(2,1)S(1)}, bf16[72,5248]{1,0:T(8,128)(2,1)S(1)}, u32[]{:S(2)}, u32[]{:S(2)}) collective-permute-start(bf16[72,5248]{1,0:T(8,128)(2,1)S(1)} %get-tuple-element.157), channel_id=1, source_target_pairs={{0,1},{1,0},{2,3},{3,2},{4,5},{5,4},{6,7},{7,6},{8,9},{9,8},{10,11... | collective-permute-start | bytes 2267144 | tf_op jit(solution)/shard_map/ppermute | solution.py:30
  247.3 19.7 %collective-permute-start.16 = (bf16[48,5248]{1,0:T(8,128)(2,1)}, bf16[48,5248]{1,0:T(8,128)(2,1)}, u32[]{:S(2)}, u32[]{:S(2)}) collective-permute-start(bf16[48,5248]{1,0:T(8,128)(2,1)} %collective-permute-done.8), channel_id=1, source_target_pairs={{0,1},{1,0},{2,3},{3,2},{4,5},{5,4},{6,7},{7,6},{8,9},{9,8},{10,11... | collective-permute-start | bytes 1511432 | tf_op jit(solution)/shard_map/ppermute | solution.py:30
  248.9 18.1 %copy-start.7 = (bf16[72,5248]{1,0:T(8,128)(2,1)}, bf16[72,5248]{1,0:T(8,128)(2,1)S(1)}, u32[]{:S(2)}) copy-start(bf16[72,5248]{1,0:T(8,128)(2,1)S(1)} %collective-permute-done.6) | copy-start | bytes 2267140
  248.9 19.6 %collective-permute-start.11 = (bf16[48,5248]{1,0:T(8,128)(2,1)S(1)}, bf16[48,5248]{1,0:T(8,128)(2,1)}, u32[]{:S(2)}, u32[]{:S(2)}) collective-permute-start(bf16[48,5248]{1,0:T(8,128)(2,1)S(1)} %slice.82), channel_id=1, source_target_pairs={{0,2},{1,3},{2,0},{3,1},{4,6},{5,7},{6,4},{7,5},{8,10},{9,11},{10,... | collective-permute-start | bytes 1511432 | tf_op jit(solution)/shard_map/ppermute | solution.py:30
  265.5 14.5 %collective-permute-start.10 = (bf16[48,5248]{1,0:T(8,128)(2,1)S(1)}, bf16[48,5248]{1,0:T(8,128)(2,1)}, u32[]{:S(2)}, u32[]{:S(2)}) collective-permute-start(bf16[48,5248]{1,0:T(8,128)(2,1)S(1)} %slice.81), channel_id=1, source_target_pairs={{0,2},{1,3},{2,0},{3,1},{4,6},{5,7},{6,4},{7,5},{8,10},{9,11},{10,... | collective-permute-start | bytes 1511432 | tf_op jit(solution)/shard_map/ppermute | solution.py:30
  267.0 22.1 %copy-start.9 = (bf16[72,5248]{1,0:T(8,128)(2,1)}, bf16[72,5248]{1,0:T(8,128)(2,1)S(1)}, u32[]{:S(2)}) copy-start(bf16[72,5248]{1,0:T(8,128)(2,1)S(1)} %collective-permute-done.12) | copy-start | bytes 2267140
  267.0 21.6 %collective-permute-start.15 = (bf16[72,5248]{1,0:T(8,128)(2,1)}, bf16[72,5248]{1,0:T(8,128)(2,1)S(1)}, u32[]{:S(2)}, u32[]{:S(2)}) collective-permute-start(bf16[72,5248]{1,0:T(8,128)(2,1)} %collective-permute-done.7), channel_id=1, source_target_pairs={{0,1},{1,0},{2,3},{3,2},{4,5},{5,4},{6,7},{7,6},{8,9},{9,8},{10,11... | collective-permute-start | bytes 2267144 | tf_op jit(solution)/shard_map/ppermute | solution.py:30
  267.0 22.1 %collective-permute-start.14 = (bf16[72,5248]{1,0:T(8,128)(2,1)S(1)}, bf16[72,5248]{1,0:T(8,128)(2,1)S(1)}, u32[]{:S(2)}, u32[]{:S(2)}) collective-permute-start(bf16[72,5248]{1,0:T(8,128)(2,1)S(1)} %collective-permute-done.6), channel_id=1, source_target_pairs={{0,1},{1,0},{2,3},{3,2},{4,5},{5,4},{6,7},{7,6},{8,9},{9,8},{10,11... | collective-permute-start | bytes 2267144 | tf_op jit(solution)/shard_map/ppermute | solution.py:30
  268.6 20.0 %collective-permute-start.9 = (bf16[48,5248]{1,0:T(8,128)(2,1)S(1)}, bf16[48,5248]{1,0:T(8,128)(2,1)}, u32[]{:S(2)}, u32[]{:S(2)}) collective-permute-start(bf16[48,5248]{1,0:T(8,128)(2,1)S(1)} %slice.80), channel_id=1, source_target_pairs={{0,2},{1,3},{2,0},{3,1},{4,6},{5,7},{6,4},{7,5},{8,10},{9,11},{10,... | collective-permute-start | bytes 1511432 | tf_op jit(solution)/shard_map/ppermute | solution.py:30
  280.0 12.5 %collective-permute-start.13 = (bf16[72,5248]{1,0:T(8,128)(2,1)}, bf16[72,5248]{1,0:T(8,128)(2,1)}, u32[]{:S(2)}, u32[]{:S(2)}) collective-permute-start(bf16[72,5248]{1,0:T(8,128)(2,1)} %collective-permute-done.5), channel_id=1, source_target_pairs={{0,1},{1,0},{2,3},{3,2},{4,5},{5,4},{6,7},{7,6},{8,9},{9,8},{10,11... | collective-permute-start | bytes 2267144 | tf_op jit(solution)/shard_map/ppermute | solution.py:30
  288.6 3.9 %collective-permute-start.19 = (bf16[48,5248]{1,0:T(8,128)(2,1)}, bf16[48,5248]{1,0:T(8,128)(2,1)}, u32[]{:S(2)}, u32[]{:S(2)}) collective-permute-start(bf16[48,5248]{1,0:T(8,128)(2,1)} %collective-permute-done.11), channel_id=1, source_target_pairs={{0,1},{1,0},{2,3},{3,2},{4,5},{5,4},{6,7},{7,6},{8,9},{9,8},{10,11... | collective-permute-start | bytes 1511432 | tf_op jit(solution)/shard_map/ppermute | solution.py:30
  288.6 3.9 %collective-permute-start.18 = (bf16[48,5248]{1,0:T(8,128)(2,1)}, bf16[48,5248]{1,0:T(8,128)(2,1)}, u32[]{:S(2)}, u32[]{:S(2)}) collective-permute-start(bf16[48,5248]{1,0:T(8,128)(2,1)} %collective-permute-done.10), channel_id=1, source_target_pairs={{0,1},{1,0},{2,3},{3,2},{4,5},{5,4},{6,7},{7,6},{8,9},{9,8},{10,11... | collective-permute-start | bytes 1511432 | tf_op jit(solution)/shard_map/ppermute | solution.py:30
  289.1 3.4 collective-permute-start.17
  (4 other events, 4.0 us)

commit v3 on v0

v3 whole, which is shorter than its diff:
```python
import functools

import jax
import jax.numpy as jnp
from jax import lax
from jax.experimental import pallas as pl
from jax.experimental.pallas import tpu as pltpu
from jax.sharding import PartitionSpec as P

TILE = 8
VERSIONS = 4
SLOTS = 64
PACKET = 72
PASSED_ON = 48
TAGS = 128
STRIP = 512
UNROLL = 5
KEYS_MIB, STACK_MIB, PLACE_MIB, SLOTS_MIB = 36, 20, 30, 44


epsilon = 1e-06
clip_ratio = 2.0
staleness = 0.5
BOTH = ("gen", "learn")
F32 = jnp.float32
BF16 = jnp.bfloat16


def to_column(row, size):
    same = lax.broadcasted_iota(jnp.int32, (size, size), 0) == lax.broadcasted_iota(
        jnp.int32, (size, size), 1
    )
    return jnp.sum(jnp.where(same, row, jnp.zeros_like(row)), 1, keepdims=True)


def row_values(per_block, rows):
    shape = (rows, per_block.shape[1])
    own = lax.broadcasted_iota(jnp.int32, shape, 0) // TILE == lax.broadcasted_iota(
        jnp.int32, shape, 1
    )
    return jnp.sum(jnp.where(own, per_block, jnp.zeros_like(per_block)), 1, keepdims=True)


def token_weights(importance_row, len_row, version_row):
    rows = importance_row.shape[1]
    stale_age = VERSIONS - 1 - version_row
    decay_row = jnp.zeros(stale_age.shape, F32)
    for age in range(VERSIONS):
        decay_row = jnp.where(stale_age == age, staleness**age, decay_row)
    inside = lax.broadcasted_iota(jnp.int32, (rows, 1), 0) % TILE < row_values(len_row, rows)
    importance = jnp.minimum(to_column(importance_row, rows), clip_ratio)
    return importance * (row_values(decay_row, rows) * jnp.where(inside, 1.0, 0.0))


def swap(x, axis, size, bit):
    return lax.ppermute(x, axis, [(i, i ^ bit) for i in range(size)])


def butterfly_sum(x, axes, learners=None):
    for axis, size in axes:
        bit = 1
        while bit < size:
            x = x + swap(x, axis, learners or size, bit)
            bit *= 2
    return x


def join_at(mine, other, upper, axis):
    place = lax.broadcasted_iota(jnp.int32, (2,) + (1,) * (mine.ndim - axis), 0)
    return jnp.where(
        place == upper, jnp.expand_dims(mine, axis), jnp.expand_dims(other, axis)
    )


def join(mine, other, upper):
    return join_at(mine, other, upper, 0).reshape((2 * mine.shape[0],) + mine.shape[1:])


def dot_rows(a, b):
    return lax.dot_general(a, b, (((0,), (0,)), ((), ())), preferred_element_type=F32)


VMEM = pl.BlockSpec(memory_space=pltpu.VMEM)
SMEM = pl.BlockSpec(memory_space=pltpu.SMEM)
ANY = pl.BlockSpec(memory_space=pl.ANY)


def keys_kernel(blocks, plan, pieces, index_ref, *refs):
    sources, outs, refs = refs[:9], refs[9 : 9 + blocks], refs[9 + blocks :]
    planes, packet = plan[:2]
    packs, refs = refs[: len(pieces)], refs[len(pieces) :]
    (keys_out, sums_out), held, (w_all, h_all, keys, sems) = refs[:2], refs[2:10], refs[10:]

    def spread(packed, first):
        for pack, (low, high) in zip(packs, pieces):
            pack[:, first] = packed[low:high]

    w_ref = sources[8]
    copies = [
        pltpu.make_async_copy(source, place, sems.at[i])
        for i, (source, place) in enumerate(zip(sources[:8], held))
    ]
    for copy in copies:
        copy.start()
    hidden_ref, len_ref, dest_ref, importance_ref, version_ref, gain_ref, key_gain_ref = held[:7]
    cotangent_ref = held[7]
    rows, features = hidden_ref.shape
    strips = features // STRIP

    def strip(i):
        return pl.ds(pl.multiple_of(i * STRIP, STRIP), STRIP)

    def fetch(i):
        return pltpu.make_async_copy(w_ref.at[strip(i)], w_all.at[strip(i)], sems.at[8 + i])

    for i in range(strips):
        fetch(i).start()
    for copy in copies[1:3]:
        copy.wait()
    place, tags, over = packet_plan(index_ref[blocks], len_ref[...], dest_ref[...], rows, *plan)
    places = lax.broadcasted_iota(jnp.int32, (planes * packet, rows), 0)
    onehot = (places == place).astype(F32).astype(BF16)
    for copy in copies[3:]:
        copy.wait()
    weight = token_weights(importance_ref[...], len_ref[...], version_ref[...])
    copies[0].wait()

    def squares(i, total):
        part = hidden_ref[:, strip(i)]
        packed = jnp.dot(onehot, part, preferred_element_type=F32).astype(BF16)
        spread(packed, strip(i))
        x = part.astype(F32)
        return total + jnp.sum(x * x, 1, keepdims=True)

    square_sum = lax.fori_loop(
        0, strips, squares, jnp.zeros((rows, 1), F32), unroll=UNROLL
    )
    packed = jnp.dot(onehot, tags, preferred_element_type=F32).astype(BF16)
    spread(packed, slice(features, features + TAGS))
    inv = lax.rsqrt(square_sum / features + epsilon)
    keys[...] = jnp.zeros_like(keys)

    def project(i, carry):
        h = (hidden_ref[:, strip(i)].astype(F32) * inv * gain_ref[:, strip(i)]).astype(BF16)
        h_all[:, strip(i)] = h
        fetch(i).wait()
        keys[...] += jnp.dot(h, w_all[strip(i), :], preferred_element_type=F32)
        return carry

    lax.fori_loop(0, strips, project, 0, unroll=UNROLL)
    width = outs[0].shape[1] - keys.shape[1]
    for k in range(blocks):
        outs[k][:, :width] = h_all[:, pl.ds(pl.multiple_of(index_ref[k] * width, width), width)]
    head = key_gain_ref.shape[1]
    kgain = jnp.zeros((1, head), F32)
    for a in range(keys.shape[1] // head):
        span = slice(a * head, (a + 1) * head)
        key = keys[:, span]
        scale = lax.rsqrt(jnp.mean(key * key, 1, keepdims=True) + epsilon)
        upstream = (cotangent_ref[:, span].astype(F32) * weight).astype(BF16).astype(F32)
        kgain = kgain + jnp.sum(upstream * key * scale, 0, keepdims=True)
        scaled = upstream * key_gain_ref[...]
        grad = scale * scaled - key * (scale * scale * scale) * jnp.mean(
            scaled * key, 1, keepdims=True
        )
        grad = grad.astype(BF16)
        keys_out[:, span] = grad
        for k in range(blocks):
            outs[k][:, width + a * head : width + (a + 1) * head] = grad
    sums_out[:, :head] = kgain
    sums_out[:, head:] = jnp.broadcast_to(over, (1, head))
    packed = jnp.dot(onehot, keys_out[...], preferred_element_type=F32).astype(BF16)
    spread(packed, slice(features + TAGS, features + TAGS + keys.shape[1]))


def packet_plan(learn, len_row, dest_row, rows, planes, packet, passed_on, capacity):
    tiles = dest_row.shape[1]
    dest_column = to_column(dest_row, tiles)
    shape = (tiles, tiles)
    earlier = lax.broadcasted_iota(jnp.int32, shape, 0) < lax.broadcasted_iota(jnp.int32, shape, 1)
    alike = earlier & (dest_column == dest_row)
    rank_row = jnp.sum(jnp.where(alike, 1, 0), 0, keepdims=True)
    shape = (tiles, rows)
    token = lax.broadcasted_iota(jnp.int32, shape, 1)
    own = token // TILE == lax.broadcasted_iota(jnp.int32, shape, 0)
    dest = jnp.sum(jnp.where(own, dest_column, 0), 0, keepdims=True)
    length = jnp.sum(jnp.where(own, to_column(len_row, tiles), 0), 0, keepdims=True)
    valid = token[:1] % TILE < length
    apart = dest ^ learn
    kind = jnp.where(valid, (apart // 4) * 2 + (apart // 2) % 2, 2 * planes)
    kinds = lax.broadcasted_iota(jnp.int32, (2 * planes, 1), 0)
    member = kind == kinds
    shape = (rows, rows)
    before = lax.broadcasted_iota(jnp.int32, shape, 0) < lax.broadcasted_iota(jnp.int32, shape, 1)
    counted = jnp.where(member, 1.0, 0.0)
    ahead = jnp.dot(
        counted.astype(BF16),
        jnp.where(before, 1.0, 0.0).astype(BF16),
        preferred_element_type=F32,
    ).astype(jnp.int32)
    count = jnp.sum(counted, 1, keepdims=True).astype(jnp.int32)
    start = (kinds // 2) * packet + jnp.where(kinds % 2 == 1, packet - count, 0)
    position = jnp.sum(jnp.where(member, ahead + start, 0), 0, keepdims=True)
    position = jnp.where(valid, position, -1)
    plane_of = lax.broadcasted_iota(jnp.int32, (2 * planes, planes), 0) // 2
    same_plane = plane_of == lax.broadcasted_iota(jnp.int32, (2 * planes, planes), 1)
    together = jnp.sum(jnp.where(same_plane, count, 0), 0, keepdims=True)
    too_many = jnp.where((kinds % 2 == 1) & (count > passed_on), 1.0, 0.0)
    over = jnp.max(jnp.where(together > packet, 1.0, 0.0), 1, keepdims=True) + jnp.max(
        too_many, 0, keepdims=True
    )
    lane = lax.broadcasted_iota(jnp.int32, (rows, TAGS), 1)
    line = lax.broadcasted_iota(jnp.int32, (rows, TAGS), 0) % TILE
    slot = learn * capacity + row_values(rank_row, rows)
    tags = jnp.where(lane == 0, row_values(dest_row, rows) + 1, jnp.where(lane == 1, slot, line))
    tags = jnp.where(lane < 3, tags, 0)
    return position, tags.astype(F32).astype(BF16), over


def stack_kernel(*refs):
    out, used = refs[-1], 0
    for part in refs[:-1]:
        out[used : used + part.shape[0], :] = part[...]
        used += part.shape[0]
    if used < out.shape[0]:
        out[used:, :] = jnp.zeros((out.shape[0] - used, out.shape[1]), BF16)


def place_kernel(me_ref, own_ref, other_ref, rows_out, keys_out, chosen):
    slots, features = rows_out.shape
    count = own_ref.shape[0]
    tag = slice(features, features + TAGS)
    tags = jnp.concatenate([own_ref[:, tag], other_ref[:, tag]], 0)
    tags = tags.astype(F32).T.astype(jnp.int32)
    target = jnp.where(tags[0:1] == me_ref[0] + 1, tags[1:2] * TILE + tags[2:3], -1)
    places = lax.broadcasted_iota(jnp.int32, (slots, 2 * count), 0)
    chosen[...] = (places == target).astype(F32).astype(BF16)

    def pick(columns):
        rows = jnp.dot(chosen[:, :count], own_ref[:, columns], preferred_element_type=F32)
        rows += jnp.dot(chosen[:, count:], other_ref[:, columns], preferred_element_type=F32)
        return rows.astype(BF16)

    def put(i, carry):
        strip = pl.ds(pl.multiple_of(i * STRIP, STRIP), STRIP)
        rows_out[:, strip] = pick(strip)
        return carry

    lax.fori_loop(0, features // STRIP, put, 0, unroll=UNROLL)
    keys_out[...] = pick(slice(features + TAGS, features + TAGS + keys_out.shape[1]))


def slots_kernel(over_ref, rows_ref, keys_ref, w_ref, gain_ref, out_ref, w_all, grad, sems):
    slots, features = out_ref.shape
    strips = features // STRIP

    def strip(i):
        return pl.ds(pl.multiple_of(i * STRIP, STRIP), STRIP)

    def fetch(i):
        return pltpu.make_async_copy(w_ref.at[strip(i)], w_all.at[strip(i)], sems.at[i])

    for i in range(strips):
        fetch(i).start()

    def back(i, total):
        rows = rows_ref[:, strip(i)].astype(F32)
        fetch(i).wait()
        g = gain_ref[:, strip(i)] * lax.dot_general(
            keys_ref[...], w_all[strip(i), :], (((1,), (1,)), ((), ())), preferred_element_type=F32
        )
        grad[:, strip(i)] = g
        squares, products = total
        return (
            squares + jnp.sum(rows * rows, 1, keepdims=True),
            products + jnp.sum(g * rows, 1, keepdims=True),
        )

    zero = jnp.zeros((slots, 1), F32)
    squares, products = lax.fori_loop(0, strips, back, (zero, zero), unroll=UNROLL)
    inv = lax.rsqrt(squares / features + epsilon)
    mean = products * inv / features

    def finish(i, carry):
        normed = rows_ref[:, strip(i)].astype(F32) * inv
        out_ref[:, strip(i)] = (inv * (grad[:, strip(i)] - normed * mean)).astype(BF16)
        return carry

    lax.fori_loop(0, strips, finish, 0, unroll=UNROLL)

    @pl.when(over_ref[0] > 0.5)
    def _():
        out_ref[...] = rows_ref[...]


def output_kernel(sizes, index_ref, *refs):
    count = len(sizes)
    mine, others, out_ref = refs[:count], refs[count : 2 * count], refs[-1]
    half = mine[0].shape[1]
    step = pl.program_id(0)
    core = index_ref[sum(sizes)]
    columns = pl.ds(pl.multiple_of(core * half, half), half)
    other_columns = pl.ds(pl.multiple_of((1 - core) * half, half), half)
    first = 0
    for k, size in enumerate(sizes):

        @pl.when((step >= first) & (step < first + size))
        def _():
            out_ref[:, columns] = mine[k][...].astype(F32)
            out_ref[:, other_columns] = others[k][...].astype(F32)

        first += size


def lay_out(index, mine, others, tall, rows, filled=None):
    half = mine[0].shape[1]
    sizes = [part.shape[0] // tall for part in mine]

    def spec(k):
        first, size = sum(sizes[:k]), sizes[k]
        return pl.BlockSpec((tall, half), lambda i, ids: (jnp.clip(i - first, 0, size - 1), 0))

    specs = [spec(k) for k in range(len(sizes))]
    more = [] if filled is None else [filled]
    return pl.pallas_call(
        functools.partial(output_kernel, sizes),
        out_shape=jax.ShapeDtypeStruct((rows, 2 * half), F32),
        grid_spec=pltpu.PrefetchScalarGridSpec(
            num_scalar_prefetch=1,
            grid=(sum(sizes),),
            in_specs=specs + specs + [ANY] * len(more),
            out_specs=pl.BlockSpec((tall, 2 * half), lambda i, ids: (ids[i], 0)),
        ),
        input_output_aliases={1 + 2 * len(sizes): 0} if more else {},
        compiler_params=pltpu.CompilerParams(vmem_limit_bytes=24 << 20),
    )(index, *mine, *others, *more)


def swap_dense(hidden, grad_keys, w_key, in_gain, dest_column, learners):
    x_float = hidden.astype(F32)
    inv_rms = lax.rsqrt(jnp.mean(x_float * x_float, -1, keepdims=True) + epsilon)
    normed = x_float * inv_rms
    grad_normed = in_gain * lax.dot_general(
        grad_keys, w_key, (((1,), (1,)), ((), ())), preferred_element_type=F32
    )
    grad_input = inv_rms * (
        grad_normed - normed * jnp.mean(grad_normed * normed, -1, keepdims=True)
    )
    onehot = (dest_column[:, None] == jnp.arange(learners, dtype=jnp.int32)[None, :]).astype(
        jnp.int32
    )
    slot_rank = jnp.sum((jnp.cumsum(onehot, 0) - onehot) * onehot, 1)
    target = dest_column * (SLOTS // learners) + slot_rank
    rows_to = (target[:, None] * TILE + jnp.arange(TILE, dtype=jnp.int32)[None, :]).reshape(-1)
    place = jnp.arange(SLOTS * TILE, dtype=jnp.int32)[:, None]
    spread = jnp.dot(
        (rows_to[None, :] == place).astype(BF16),
        grad_input.astype(BF16),
        preferred_element_type=F32,
    )
    return lax.all_to_all(spread.astype(BF16), "learn", split_axis=0, concat_axis=0, tiled=True)


def body(hidden, cotangent, importance, block_len, version, destination, w_key, in_gain, key_gain):
    learners, gens = lax.axis_size("learn"), lax.axis_size("gen")
    gen, learn = lax.axis_index("gen"), lax.axis_index("learn")
    core, across = learn % 2, (learn // 2) % 2
    capacity = SLOTS // learners
    planes = learners // 4
    packet = min(PACKET, 4 * capacity * TILE)
    passed_on = min(PASSED_ON, 2 * capacity * TILE)
    rows, features = hidden.shape
    key_count = cotangent.shape[1]
    head = key_gain.shape[0]
    strips = features // STRIP
    blocks = 2 * gens
    width = features // blocks
    half = key_count // 2

    def limit(mebibytes):
        return pltpu.CompilerParams(vmem_limit_bytes=mebibytes << 20)


    front = packet - passed_on
    pieces = []
    for k in range(planes):
        cuts = (0, front, packet) if k in (0, planes - 1) else (0, packet)
        pieces += [(k * packet + low, k * packet + high) for low, high in zip(cuts, cuts[1:])]
    packed_width = features + TAGS + key_count
    steps = [(step, dy) for step in range(gens) for dy in range(2)]
    wanted = [((gen + step) % gens) * 2 + (across ^ dy) for step, dy in steps]
    in_gain_row = in_gain[None, :]
    tiles = block_len.shape[0]
    made = pl.pallas_call(
        functools.partial(
            keys_kernel, blocks, (planes, packet, passed_on, capacity), pieces
        ),
        out_shape=[jax.ShapeDtypeStruct((rows, width + key_count), BF16)] * blocks
        + [jax.ShapeDtypeStruct((high - low, packed_width), BF16) for low, high in pieces]
        + [
            jax.ShapeDtypeStruct((rows, key_count), BF16),
            jax.ShapeDtypeStruct((1, 2 * head), F32),
        ],
        in_specs=[SMEM] + [ANY] * 9,
        out_specs=[VMEM] * (blocks + len(pieces) + 2),
        scratch_shapes=[
            pltpu.VMEM((rows, features), BF16),
            pltpu.VMEM((1, tiles), jnp.int32),
            pltpu.VMEM((1, tiles), jnp.int32),
            pltpu.VMEM((1, rows), F32),
            pltpu.VMEM((1, tiles), jnp.int32),
            pltpu.VMEM((1, features), F32),
            pltpu.VMEM((1, head), F32),
            pltpu.VMEM((rows, key_count), BF16),
            pltpu.VMEM((features, key_count), BF16),
            pltpu.VMEM((rows, features), BF16),
            pltpu.VMEM((rows, key_count), F32),
            pltpu.SemaphoreType.DMA((8 + strips,)),
        ],
        compiler_params=limit(KEYS_MIB),
        cost_estimate=pl.CostEstimate(
            flops=2 * rows * features * key_count, bytes_accessed=16 << 20, transcendentals=0
        ),
    )(
        jnp.stack(wanted + [learn]),
        hidden,
        block_len[None, :],
        destination[:, 0][None, :],
        importance[None, :],
        version[None, :],
        in_gain_row,
        key_gain[None, :],
        cotangent,
        w_key,
    )
    operands, packs, (grad_keys, sums) = (
        made[:blocks],
        made[blocks : blocks + len(pieces)],
        made[blocks + len(pieces) :],
    )

    def gather(k):
        step, dy = steps[k]
        pairs = [
            (p * learners + j, ((p + step) % gens) * learners + (j ^ (2 * dy)))
            for p in range(gens)
            for j in range(learners)
        ]
        return lax.ppermute(operands[k], BOTH, pairs)

    def across_learn(part, bit):
        return swap(part, "learn", learners, bit)

    def over_y(part):
        return across_learn(part[part.shape[0] - passed_on :], 2)

    def products(part):
        keys = lax.dynamic_slice_in_dim(part, width + core * half, half, 1)
        return dot_rows(part[:, :width], keys)

    barrier = lax.optimization_barrier
    direct = [k for k, (step, dy) in enumerate(steps) if (step > 0) + dy == 1]
    diagonal = [k for k, (step, dy) in enumerate(steps) if (step > 0) + dy == 2]
    last = planes - 1
    held, passed = {0: packs[1], planes: packs[0]}, {}

    gathered = [gather(k) for k in direct + diagonal]
    for k in range(2, last):
        held[k] = across_learn(packs[1 + k], 4 * k)
    held[planes + 1] = across_learn(packs[-2], 4 * last)
    gathered, held, packs = barrier((gathered, held, packs))

    total = products(operands[0]) + products(across_learn(operands[0], 1))
    for part in gathered:
        total = total + products(part) + products(across_learn(part, 1))
    held[1] = across_learn(packs[2], 4)
    held[last] = across_learn(packs[-1], 4 * last)
    for k in (0, *range(2, last)):
        passed[k] = over_y(held[k])
    total, held, passed = barrier((total, held, passed))

    bits = [4 << b for b in range(planes.bit_length() - 1)]
    for n, bit in enumerate(bits):
        upper = (learn // bit) % 2
        tall = total.shape[0] // 2
        sent = lax.dynamic_slice_in_dim(total, (1 - upper) * tall, tall, 0).astype(BF16)
        kept = lax.dynamic_slice_in_dim(total, upper * tall, tall, 0)
        total = kept + across_learn(sent, bit).astype(F32)
        if n == 0:
            passed[1] = over_y(held[1])
            sums = butterfly_sum(sums, (("gen", gens),))
            sums = butterfly_sum(sums, (("learn", 4),), learners)
        if n == 1:
            passed[last] = over_y(held[last])
            sums = sums + across_learn(sums, bits[0])
        total, passed, held, sums = barrier((total, passed, held, sums))

    tall = total.shape[0]
    first = (gen * 2 + across) * width
    for n, bit in enumerate(bits):
        first = first + ((learn // bit) % 2) * (width >> (n + 1))
    w_part = lax.dynamic_slice(w_key, (first, core * half), (tall, half)).astype(F32)
    gains = jnp.sum(w_part * total, 1) / lax.dynamic_slice_in_dim(in_gain, first, tall)

    parts, y_parts, offsets = [total.astype(BF16)], [], [0]
    order = list(held.values()) + list(passed.values())
    used = sum(part.shape[0] for part in order)
    place = -(-used // 128) * 128
    for n, bit in enumerate(reversed(bits)):
        block = parts[0] if n == 0 else jnp.concatenate(parts, 0)
        received = across_learn(block, bit)
        y_parts.append(across_learn(parts[-1], 2))
        if n == 0:
            all_rows = pl.pallas_call(
                stack_kernel,
                out_shape=jax.ShapeDtypeStruct((place, packed_width), BF16),
                in_specs=[VMEM] * len(order),
                out_specs=VMEM,
                compiler_params=limit(STACK_MIB),
            )(*order)
            other_rows = across_learn(all_rows, 1)
            gains = gains + across_learn(gains, 1)
            gains = gains[None]
            step = 1
            while step < gens:
                gains = join(gains, swap(gains, "gen", gens, step), (gen // step) % 2)
                step *= 2
            for other_bit in bits[1:]:
                sums = sums + across_learn(sums, other_bit)
            received, y_parts, all_rows, other_rows, gains, sums = barrier(
                (received, y_parts, all_rows, other_rows, gains, sums)
            )
        parts = parts + [received]
        weight = planes >> (bits.index(bit) + 1)
        offsets = offsets + [o ^ weight for o in offsets]
        if n:
            wide = bits[-n]
            gains = join_at(gains, across_learn(gains, wide), (learn // wide) % 2, 1)
    rows_placed, keys_placed = pl.pallas_call(
        place_kernel,
        out_shape=[
            jax.ShapeDtypeStruct((SLOTS * TILE, features), BF16),
            jax.ShapeDtypeStruct((SLOTS * TILE, key_count), BF16),
        ],
        in_specs=[SMEM, VMEM, VMEM],
        out_specs=[VMEM] * 2,
        scratch_shapes=[pltpu.VMEM((SLOTS * TILE, 2 * place), BF16)],
        compiler_params=limit(PLACE_MIB),
    )(learn[None], all_rows, other_rows)
    parts, y_parts, gains, sums, rows_placed, keys_placed = barrier(
        (parts, y_parts, gains, sums, rows_placed, keys_placed)
    )

    y_parts.append(across_learn(parts[-1], 2))
    _, rows_placed = lax.while_loop(
        lambda state: state[0] > 0.5,
        lambda state: (
            jnp.zeros((), F32),
            swap_dense(hidden, grad_keys, w_key, in_gain, destination[:, 0], learners),
        ),
        (sums[0, -1], rows_placed),
    )
    grad_slots = pl.pallas_call(
        slots_kernel,
        out_shape=jax.ShapeDtypeStruct((SLOTS * TILE, features), BF16),
        in_specs=[SMEM, VMEM, VMEM, ANY, VMEM],
        out_specs=VMEM,
        scratch_shapes=[
            pltpu.VMEM((features, key_count), BF16),
            pltpu.VMEM((SLOTS * TILE, features), F32),
            pltpu.SemaphoreType.DMA((strips,)),
        ],
        compiler_params=limit(SLOTS_MIB),
    )(sums[0, -1:], rows_placed, keys_placed, w_key, in_gain_row)
    core_parts = [across_learn(part, 1) for part in parts]
    core_y = [across_learn(part, 1) for part in y_parts[:-1]]
    first = sum(((learn // bit) % 2) * (planes >> (n + 1)) for n, bit in enumerate(bits))
    first = first ^ jnp.asarray(offsets, jnp.int32)
    w_rows = 2 * width
    w_grad = lay_out(
        jnp.concatenate([across * planes + first, core[None]]), parts, core_parts, tall, w_rows
    )
    near = [across_learn(gains, bit) for bit in (bits[0], 2, bits[0] + 2)]
    upper = (learn // bits[0]) % 2
    gains = join_at(
        join_at(gains, near[0], upper, 1), join_at(near[1], near[2], upper, 1), across, 1
    )
    w_grad, y_parts, core_y, gains, sums, grad_slots = barrier(
        (w_grad, y_parts, core_y, gains, sums, grad_slots)
    )
    core_y.append(across_learn(y_parts[-1], 1))
    w_grad = lay_out(
        jnp.concatenate([(1 - across) * planes + first, core[None]]),
        y_parts,
        core_y,
        tall,
        w_rows,
        w_grad,
    )
    return (grad_slots, w_grad, gains.reshape(-1), sums[0, :head])


def solution(mesh):
    return jax.shard_map(
        body,
        mesh=mesh,
        in_specs=(
            P(("gen", "learn"), None),
            P(("gen", "learn"), None),
            P(("gen", "learn")),
            P(("gen", "learn")),
            P(("gen", "learn")),
            P(("gen", "learn"), None),
            P(),
            P(),
            P(),
        ),
        out_specs=(P(("gen", "learn"), None), P("gen", None), P(), P()),
        check_vma=False,
    )
```

time: 494 us -> 244 us (0.49)
  waiting for transfers between devices: 369 us -> 115 us
  Pallas kernels: 0 us -> 57 us
  blocking collectives: 41.3 us -> 0 us
  starting transfers between devices: 7.41 us -> 36.5 us
  matrix products: 25.5 us -> 10.2 us
  between operations: 14.3 us -> 1.7 us
  local copies, waits for them, and re-layouts: 25.6 us -> 16.8 us
    reduce_scatter x1 -> x0, waiting for transfers between devices: 205 us -> none  [body(): lax.psum_scatter(lax.dot_general(h_rows, grad_keys, (((0,), (0,)), ((), (...]
    psum x1 -> x0, waiting for transfers between devices: 165 us -> none  [body(): w_grad = lax.psum(partial_rows, 'learn')]
    ppermute x0 -> x40, waiting for transfers between devices: none -> 115 us  [the longest x37 115 us: swap(): return lax.ppermute(x, axis, [(i, i ^ bit) for i in range(size)])]
    pallas_call x0 -> x6, Pallas kernels: none -> 57 us  [the longest x1 18.2 us: body(): pl.pallas_call(slots_kernel, out_shape=jax.ShapeDtypeStruct((SLOTS * TILE...]
    psum x1 -> x0, blocking collectives: 41.3 us -> none  [body(): gain_grad, kgain_grad = lax.psum((gain_part, kgain_part), ('gen', 'learn'))]
    ppermute x0 -> x40, starting transfers between devices: none -> 36.5 us  [the longest x37 32 us: swap(): return lax.ppermute(x, axis, [(i, i ^ bit) for i in range(size)])]
    dot_general x4 -> x8, matrix products: 25.5 us -> 10.2 us  [dot_rows(): lax.dot_general(a, b, (((0,), (0,)), ((), ())), preferred_element_type=F32)]
    all_to_all x1 -> x0, local copies, waits for them, and re-layouts: 8.12 us -> none  [body(): lax.all_to_all(spread.astype(jnp.bfloat16).reshape(SLOTS * TILE, feature_...]
  transfers between devices with their start and end apart: 3 -> 40, of which waited for: 2 -> 16; matrix products, arithmetic and copies ran while one was open for 3% -> 8% of each run, Pallas kernels for 0% -> 15%
where the time goes in v3:
time: 244 us; the launch traced here: 243 us
  waiting for transfers between devices  115 us (47%)
  Pallas kernels  57 us (23%)
  starting transfers between devices  36.5 us (15%)
  local copies, waits for them, and re-layouts  16.8 us (7%)
  matrix products  10.2 us (4%)
  other arithmetic  6.02 us (2%)
    ppermute x37, waiting for transfers between devices, swap(): return lax.ppermute(x, axis, [(i, i ^ bit) for i in range(size)])  115 us
    ppermute x37, starting transfers between devices, swap(): return lax.ppermute(x, axis, [(i, i ^ bit) for i in range(size)])  32 us
    pallas_call x1, Pallas kernels, body(): pl.pallas_call(slots_kernel, out_shape=jax.ShapeDtypeStruct((SLOTS * TILE...  18.2 us
    pallas_call x1, Pallas kernels, body(): pl.pallas_call(place_kernel, out_shape=[jax.ShapeDtypeStruct((SLOTS * TIL...  13.5 us
    pallas_call x1, Pallas kernels, body(): pl.pallas_call(functools.partial(keys_kernel, blocks, (planes, packet, pa...  12.5 us
    unnamed x54, local copies, waits for them, and re-layouts  12.4 us
    dot_general x8, matrix products, dot_rows(): lax.dot_general(a, b, (((0,), (0,)), ((), ())), preferred_element_type=F32)  10.2 us
    pallas_call x2, Pallas kernels, lay_out(): pl.pallas_call(functools.partial(output_kernel, sizes), out_shape=jax.Sha...  8.1 us
  transfers between devices with their start and end apart: 40, of which 16 were waited for; matrix products, arithmetic and copies ran while one was open for 8% of the time, Pallas kernels for 15%

profile of v3, /device:TPU:0, one launch (start us, length us, event | category | flops | bytes accessed | tf_op | source)
XLA Modules:
  0.0 243.2 jit_solution(5130087520200929241)
XLA Ops:
  0.8 1.0 copy-done.2
  4.5 12.5 %shard_map.129 = (bf16[256,2304]{1,0:T(8,128)(2,1)}, bf16[256,2304]{1,0:T(8,128)(2,1)}, bf16[256,2304]{1,0:T(8,128)(2,1)}, bf16[256,2304]{1,0:T(8,128)(2,1)}, bf...) custom-call(s32[5]{0:T(128)S(1)} %stack.23.index_ref, ...), custom_call_target="tpu_custom_call" | custom-call | flops 2684354560 | bytes 16777216 | tf_op jit(solution)/shard_map/pallas_call | solution.py:394
  17.0 1.0 copy-done.19
  18.9 3.0 %collective-permute-start.1 = (bf16[256,2304]{1,0:T(8,128)(2,1)}, bf16[256,2304]{1,0:T(8,128)(2,1)}, u32[]{:S(2)}, u32[]{:S(2)}) collective-permute-start(bf16[256,2304]{1,0:T(8,128)(2,1)} %get-tuple-element.119), channel_id=1, source_target_pairs={{0,2},{1,3},{2,0},{3,1},{4,6},{5,7},{6,4},{7,5},{8,10},{9,11},{10,... | collective-permute-start | bytes 3538952 | tf_op jit(solution)/shard_map/ppermute | solution.py:449
  21.9 1.5 collective-permute-start.2
  23.4 4.1 %collective-permute-start.5 = (bf16[24,6272]{1,0:T(8,128)(2,1)S(1)}, bf16[24,6272]{1,0:T(8,128)(2,1)S(1)}, u32[]{:S(2)}, u32[]{:S(2)}) collective-permute-start(bf16[24,6272]{1,0:T(8,128)(2,1)S(1)} %get-tuple-element.125), channel_id=1, source_target_pairs={{0,12},{1,13},{2,14},{3,15},{4,8},{5,9},{6,10},{7,11},{8,4},{9,5},... | collective-permute-start | bytes 903176 | tf_op jit(solution)/shard_map/ppermute | solution.py:56
  27.4 8.1 %collective-permute-done.5.refs_5_ = bf16[24,6272]{1,0:T(8,128)(2,1)S(1)} collective-permute-done((bf16[24,6272]{1,0:T(8,128)(2,1)S(1)}, bf16[24,6272]{1,0:T(8,128)(2,1)S(1)}, u32[]{:S(2)}, u32[]{:S(2)}) %collective-permute-start.5) | collective-permute-done | bytes 301088 | tf_op jit(solution)/shard_map/ppermute | solution.py:56
  35.5 1.8 fusion.23
  37.3 40.7 %collective-permute-done.4.refs_2_ = bf16[72,6272]{1,0:T(8,128)(2,1)S(1)} collective-permute-done((bf16[72,6272]{1,0:T(8,128)(2,1)S(1)}, bf16[72,6272]{1,0:T(8,128)(2,1)S(1)}, u32[]{:S(2)}, u32[]{:S(2)}) %collective-permute-start.4) | collective-permute-done | bytes 903200 | tf_op jit(solution)/shard_map/ppermute | solution.py:56
  78.6 1.7 fusion.20
  80.4 1.6 collective-permute-start.12
  82.0 2.5 %collective-permute-start.10 = (bf16[48,6272]{1,0:T(8,128)(2,1)S(1)}, bf16[48,6272]{1,0:T(8,128)(2,1)}, u32[]{:S(2)}, u32[]{:S(2)}) collective-permute-start(bf16[48,6272]{1,0:T(8,128)(2,1)S(1)} %copy-done.22), channel_id=1, source_target_pairs={{0,12},{1,13},{2,14},{3,15},{4,8},{5,9},{6,10},{7,11},{8,4},{9,5},... | collective-permute-start | bytes 1806344 | tf_op jit(solution)/shard_map/ppermute | solution.py:56
  84.4 1.7 convolution_add_fusion.4
  86.1 1.7 convolution_add_fusion.3
  87.8 1.8 fusion.18
  92.0 4.9 %collective-permute-done.12.refs_8_ = bf16[48,6272]{1,0:T(8,128)(2,1)S(1)} collective-permute-done((bf16[48,6272]{1,0:T(8,128)(2,1)S(1)}, bf16[48,6272]{1,0:T(8,128)(2,1)S(1)}, u32[]{:S(2)}, u32[]{:S(2)}) %collective-permute-start.12) | collective-permute-done | bytes 602144 | tf_op jit(solution)/shard_map/ppermute | solution.py:56
  96.9 3.5 %collective-permute-done.10.refs_3_ = bf16[48,6272]{1,0:T(8,128)(2,1)} collective-permute-done((bf16[48,6272]{1,0:T(8,128)(2,1)S(1)}, bf16[48,6272]{1,0:T(8,128)(2,1)}, u32[]{:S(2)}, u32[]{:S(2)}) %collective-permute-start.10) | collective-permute-done | bytes 602144 | tf_op jit(solution)/shard_map/ppermute | solution.py:56
  100.4 8.5 %collective-permute-done.11.refs_6_ = bf16[48,6272]{1,0:T(8,128)(2,1)S(1)} collective-permute-done((bf16[48,6272]{1,0:T(8,128)(2,1)S(1)}, bf16[48,6272]{1,0:T(8,128)(2,1)S(1)}, u32[]{:S(2)}, u32[]{:S(2)}) %collective-permute-start.11) | collective-permute-done | bytes 602144 | tf_op jit(solution)/shard_map/ppermute | solution.py:56
  109.8 8.8 %collective-permute-done.9.refs_1_ = bf16[72,6272]{1,0:T(8,128)(2,1)S(1)} collective-permute-done((bf16[72,6272]{1,0:T(8,128)(2,1)S(1)}, bf16[72,6272]{1,0:T(8,128)(2,1)S(1)}, u32[]{:S(2)}, u32[]{:S(2)}) %collective-permute-start.9) | collective-permute-done | bytes 903200 | tf_op jit(solution)/shard_map/ppermute | solution.py:56
  118.5 0.9 dynamic-slice_convert_fusion
  121.5 1.5 collective-permute-start.15
  123.0 2.1 collective-permute-done.15
  125.1 1.1 collective-permute-done.16
  126.2 1.5 collective-permute-start.17
  127.7 8.5 %collective-permute-done.17 = f32[1,256]{1,0:T(1,128)S(1)} collective-permute-done((f32[1,256]{1,0:T(1,128)S(1)}, f32[1,256]{1,0:T(1,128)S(1)}, u32[]{:S(2)}, u32[]{:S(2)}) %collective-permute-start.17) | collective-permute-done | bytes 1056 | tf_op jit(solution)/shard_map/ppermute | solution.py:56
  136.5 1.7 convert_add_fusion
  140.0 2.5 %collective-permute-start.18 = (bf16[320,512]{1,0:T(8,128)(2,1)}, bf16[320,512]{1,0:T(8,128)(2,1)}, u32[]{:S(2)}, u32[]{:S(2)}) collective-permute-start(bf16[320,512]{1,0:T(8,128)(2,1)} %dynamic-slice_convert_fusion.1), channel_id=1, source_target_pairs={{0,8},{1,9},{2,10},{3,11},{4,12},{5,13},{6,14},{7,15},{8,0},{9,1},... | collective-permute-start | bytes 983048 | tf_op jit(solution)/shard_map/ppermute | solution.py:56
  143.1 5.9 %collective-permute-done.20 = f32[1,256]{1,0:T(1,128)S(1)} collective-permute-done((f32[1,256]{1,0:T(1,128)S(1)}, f32[1,256]{1,0:T(1,128)S(1)}, u32[]{:S(2)}, u32[]{:S(2)}) %collective-permute-start.20) | collective-permute-done | bytes 1056 | tf_op jit(solution)/shard_map/ppermute | solution.py:56
  148.9 8.2 %collective-permute-done.18 = bf16[320,512]{1,0:T(8,128)(2,1)} collective-permute-done((bf16[320,512]{1,0:T(8,128)(2,1)}, bf16[320,512]{1,0:T(8,128)(2,1)}, u32[]{:S(2)}, u32[]{:S(2)}) %collective-permute-start.18) | collective-permute-done | bytes 327712 | tf_op jit(solution)/shard_map/ppermute | solution.py:56
  157.1 2.1 convert_add_fusion.1
  159.2 1.1 copy-done.1
  160.3 1.0 copy-done.14
  161.3 4.6 %shard_map.130.own_ref = bf16[512,6272]{1,0:T(8,128)(2,1)} custom-call(bf16[48,6272]{1,0:T(8,128)(2,1)S(1)} %get-tuple-element.159.refs_0_, bf16[72,6272]{1,0:T(8,128)(2,1)S(1)} %collective-permute-done.9.refs_1_, bf16[72,6272]{1,0:T(8,128)(2,1)S(1)} %collective-permute-done.4.refs_2_, bf16[48,6272]{1,0:T(8,128)(2,1)} %collective-permute-done.10.refs_3_, ...), custom_call_target="tpu_custom_call" | custom-call | tf_op jit(solution)/shard_map/pallas_call | solution.py:514
  165.9 1.5 multiply_reduce_fusion
  168.8 2.9 %collective-permute-start.26 = (f32[1,256]{1,0:T(1,128)S(1)}, f32[1,256]{1,0:T(1,128)S(1)}, u32[]{:S(2)}, u32[]{:S(2)}) collective-permute-start(f32[1,256]{1,0:T(1,128)S(1)} %add.225), channel_id=1, source_target_pairs={{0,8},{1,9},{2,10},{3,11},{4,12},{5,13},{6,14},{7,15},{8,0},{9,1},... | collective-permute-start | bytes 3080 | tf_op jit(solution)/shard_map/ppermute | solution.py:56
  171.7 4.5 %collective-permute-done.24 = f32[320]{0:T(512)S(1)} collective-permute-done((f32[320]{0:T(512)S(1)}, f32[320]{0:T(512)S(1)}, u32[]{:S(2)}, u32[]{:S(2)}) %collective-permute-start.24) | collective-permute-done | bytes 1312 | tf_op jit(solution)/shard_map/ppermute | solution.py:56
  176.2 1.5 collective-permute-start.25
  177.7 8.3 %collective-permute-done.26 = f32[1,256]{1,0:T(1,128)S(1)} collective-permute-done((f32[1,256]{1,0:T(1,128)S(1)}, f32[1,256]{1,0:T(1,128)S(1)}, u32[]{:S(2)}, u32[]{:S(2)}) %collective-permute-start.26) | collective-permute-done | bytes 1056 | tf_op jit(solution)/shard_map/ppermute | solution.py:56
  186.3 1.3 collective-permute-start.28
  187.6 1.9 collective-permute-start.29
  189.6 13.5 %shard_map.131 = (bf16[512,5120]{1,0:T(8,128)(2,1)}, bf16[512,1024]{1,0:T(8,128)(2,1)S(1)}) custom-call(s32[1]{0:T(128)} %bitcast.8.me_ref, bf16[512,6272]{1,0:T(8,128)(2,1)} %shard_map.130.own_ref, bf16[512,6272]{1,0:T(8,128)(2,1)} %collective-permute-done.23.other_ref), custom_call_target="tpu_custom_call" | custom-call | tf_op jit(solution)/shard_map/pallas_call | solution.py:539
  204.9 1.9 collective-permute-start.36
  206.8 1.0 collective-permute-start.33
  209.6 18.2 %shard_map.133 = bf16[512,5120]{1,0:T(8,128)(2,1)} custom-call(f32[1]{0:T(128)} %bitcast.15.over_ref, bf16[512,5120]{1,0:T(8,128)(2,1)} %get-tuple-element.187.rows_ref, bf16[512,1024]{1,0:T(8,128)(2,1)S(1)} %get-tuple-element.188.keys_ref, bf16[5120,1024]{1,0:T(8,128)(2,1)} %get-tuple-element.279, f32[1,5120]{1,0:T(1,128)S(1)} %bitcast.28), custom_call_target="tpu_custom_call" | custom-call | tf_op jit(solution)/shard_map/pallas_call | solution.py:563
  229.5 4.8 %shard_map.132.refs_6_ = f32[2560,1024]{1,0:T(8,128)} custom-call(s32[5]{0:T(128)S(1)} %pad_add_fusion.index_ref, bf16[320,512]{1,0:T(8,128)(2,1)S(1)} %get-tuple-element.178.refs_0_, bf16[320,512]{1,0:T(8,128)(2,1)S(1)} %collective-permute-done.21.refs_1_, bf16[640,512]{1,0:T(8,128)(2,1)S(1)} %collective-permute-done.27.refs_2_, ...), custom_call_target="tpu_custom_call" | custom-call | tf_op jit(solution)/shard_map/pallas_call | solution.py:325
  237.9 1.0 copy-done.10
  238.9 1.0 copy-done.12
  239.9 3.3 %shard_map.134 = f32[2560,1024]{1,0:T(8,128)} custom-call(s32[5]{0:T(128)S(1)} %pad_add_fusion.1.index_ref, bf16[320,512]{1,0:T(8,128)(2,1)S(1)} %copy-done.5, bf16[320,512]{1,0:T(8,128)(2,1)S(1)} %copy-done.8, bf16[640,512]{1,0:T(8,128)(2,1)S(1)} %collective-permute-done.33.refs_2_, ...), custom_call_target="tpu_custom_call", output_to_operand_aliasing={{}: (7, {})} | custom-call | tf_op jit(solution)/shard_map/pallas_call | solution.py:325
  (134 shorter events, 21.9 us)
Async XLA Ops:
  18.9 59.2 %collective-permute-start.1 = (bf16[256,2304]{1,0:T(8,128)(2,1)}, bf16[256,2304]{1,0:T(8,128)(2,1)}, u32[]{:S(2)}, u32[]{:S(2)}) collective-permute-start(bf16[256,2304]{1,0:T(8,128)(2,1)} %get-tuple-element.119), channel_id=1, source_target_pairs={{0,2},{1,3},{2,0},{3,1},{4,6},{5,7},{6,4},{7,5},{8,10},{9,11},{10,... | collective-permute-start | bytes 3538952 | tf_op jit(solution)/shard_map/ppermute | solution.py:449
  21.9 56.2 %collective-permute-start.2 = (bf16[256,2304]{1,0:T(8,128)(2,1)}, bf16[256,2304]{1,0:T(8,128)(2,1)}, u32[]{:S(2)}, u32[]{:S(2)}) collective-permute-start(bf16[256,2304]{1,0:T(8,128)(2,1)} %get-tuple-element.120), channel_id=1, source_target_pairs={{0,16},{1,17},{2,18},{3,19},{4,20},{5,21},{6,22},{7,23},{8,24},{9,... | collective-permute-start | bytes 3538952 | tf_op jit(solution)/shard_map/ppermute | solution.py:449
  23.4 54.7 %collective-permute-start.3 = (bf16[256,2304]{1,0:T(8,128)(2,1)}, bf16[256,2304]{1,0:T(8,128)(2,1)}, u32[]{:S(2)}, u32[]{:S(2)}) collective-permute-start(bf16[256,2304]{1,0:T(8,128)(2,1)} %get-tuple-element.121), channel_id=1, source_target_pairs={{0,18},{1,19},{2,16},{3,17},{4,22},{5,23},{6,20},{7,21},{8,26},{9,... | collective-permute-start | bytes 3538952 | tf_op jit(solution)/shard_map/ppermute | solution.py:449
  23.4 12.2 %collective-permute-start.5 = (bf16[24,6272]{1,0:T(8,128)(2,1)S(1)}, bf16[24,6272]{1,0:T(8,128)(2,1)S(1)}, u32[]{:S(2)}, u32[]{:S(2)}) collective-permute-start(bf16[24,6272]{1,0:T(8,128)(2,1)S(1)} %get-tuple-element.125), channel_id=1, source_target_pairs={{0,12},{1,13},{2,14},{3,15},{4,8},{5,9},{6,10},{7,11},{8,4},{9,5},... | collective-permute-start | bytes 903176 | tf_op jit(solution)/shard_map/ppermute | solution.py:56
  27.4 50.6 %collective-permute-start.4 = (bf16[72,6272]{1,0:T(8,128)(2,1)S(1)}, bf16[72,6272]{1,0:T(8,128)(2,1)S(1)}, u32[]{:S(2)}, u32[]{:S(2)}) collective-permute-start(bf16[72,6272]{1,0:T(8,128)(2,1)S(1)} %get-tuple-element.123), channel_id=1, source_target_pairs={{0,8},{1,9},{2,10},{3,11},{4,12},{5,13},{6,14},{7,15},{8,0},{9,1},... | collective-permute-start | bytes 2709512 | tf_op jit(solution)/shard_map/ppermute | solution.py:56
  35.5 44.8 %copy-start.13 = (bf16[24,6272]{1,0:T(8,128)(2,1)}, bf16[24,6272]{1,0:T(8,128)(2,1)S(1)}, u32[]{:S(2)}) copy-start(bf16[24,6272]{1,0:T(8,128)(2,1)S(1)} %collective-permute-done.5.refs_5_) | copy-start | bytes 903172
  35.5 48.9 %collective-permute-start = (bf16[256,2304]{1,0:T(8,128)(2,1)}, bf16[256,2304]{1,0:T(8,128)(2,1)}, u32[]{:S(2)}, u32[]{:S(2)}) collective-permute-start(bf16[256,2304]{1,0:T(8,128)(2,1)} %get-tuple-element.118), channel_id=1, source_target_pairs={{0,1},{1,0},{2,3},{3,2},{4,5},{5,4},{6,7},{7,6},{8,9},{9,8},{10,11... | collective-permute-start | bytes 3538952 | tf_op jit(solution)/shard_map/ppermute | solution.py:56
  37.3 44.6 %copy-start.22 = (bf16[48,6272]{1,0:T(8,128)(2,1)S(1)}, bf16[48,6272]{1,0:T(8,128)(2,1)}, u32[]{:S(2)}) copy-start(bf16[48,6272]{1,0:T(8,128)(2,1)} %copy-done.21) | copy-start | bytes 1806340
  78.1 11.5 %collective-permute-start.6 = (bf16[256,2304]{1,0:T(8,128)(2,1)}, bf16[256,2304]{1,0:T(8,128)(2,1)S(1)}, u32[]{:S(2)}, u32[]{:S(2)}) collective-permute-start(bf16[256,2304]{1,0:T(8,128)(2,1)} %collective-permute-done.1), channel_id=1, source_target_pairs={{0,1},{1,0},{2,3},{3,2},{4,5},{5,4},{6,7},{7,6},{8,9},{9,8},{10,11... | collective-permute-start | bytes 3538952 | tf_op jit(solution)/shard_map/ppermute | solution.py:56
  78.1 12.1 %collective-permute-start.7 = (bf16[256,2304]{1,0:T(8,128)(2,1)}, bf16[256,2304]{1,0:T(8,128)(2,1)S(1)}, u32[]{:S(2)}, u32[]{:S(2)}) collective-permute-start(bf16[256,2304]{1,0:T(8,128)(2,1)} %collective-permute-done.2), channel_id=1, source_target_pairs={{0,1},{1,0},{2,3},{3,2},{4,5},{5,4},{6,7},{7,6},{8,9},{9,8},{10,11... | collective-permute-start | bytes 3538952 | tf_op jit(solution)/shard_map/ppermute | solution.py:56
  80.4 16.5 %collective-permute-start.12 = (bf16[48,6272]{1,0:T(8,128)(2,1)S(1)}, bf16[48,6272]{1,0:T(8,128)(2,1)S(1)}, u32[]{:S(2)}, u32[]{:S(2)}) collective-permute-start(bf16[48,6272]{1,0:T(8,128)(2,1)S(1)} %slice.45), channel_id=1, source_target_pairs={{0,2},{1,3},{2,0},{3,1},{4,6},{5,7},{6,4},{7,5},{8,10},{9,11},{10,... | collective-permute-start | bytes 1806344 | tf_op jit(solution)/shard_map/ppermute | solution.py:56
  82.0 18.4 %collective-permute-start.10 = (bf16[48,6272]{1,0:T(8,128)(2,1)S(1)}, bf16[48,6272]{1,0:T(8,128)(2,1)}, u32[]{:S(2)}, u32[]{:S(2)}) collective-permute-start(bf16[48,6272]{1,0:T(8,128)(2,1)S(1)} %copy-done.22), channel_id=1, source_target_pairs={{0,12},{1,13},{2,14},{3,15},{4,8},{5,9},{6,10},{7,11},{8,4},{9,5},... | collective-permute-start | bytes 1806344 | tf_op jit(solution)/shard_map/ppermute | solution.py:56
  84.4 6.9 %collective-permute-start.8 = (bf16[256,2304]{1,0:T(8,128)(2,1)}, bf16[256,2304]{1,0:T(8,128)(2,1)S(1)}, u32[]{:S(2)}, u32[]{:S(2)}) collective-permute-start(bf16[256,2304]{1,0:T(8,128)(2,1)} %collective-permute-done.3), channel_id=1, source_target_pairs={{0,1},{1,0},{2,3},{3,2},{4,5},{5,4},{6,7},{7,6},{8,9},{9,8},{10,11... | collective-permute-start | bytes 3538952 | tf_op jit(solution)/shard_map/ppermute | solution.py:56
  89.6 28.9 %collective-permute-start.9 = (bf16[72,6272]{1,0:T(8,128)(2,1)S(1)}, bf16[72,6272]{1,0:T(8,128)(2,1)S(1)}, u32[]{:S(2)}, u32[]{:S(2)}) collective-permute-start(bf16[72,6272]{1,0:T(8,128)(2,1)S(1)} %copy-done.20), channel_id=1, source_target_pairs={{0,4},{1,5},{2,6},{3,7},{4,0},{5,1},{6,2},{7,3},{8,12},{9,13},{10,... | collective-permute-start | bytes 2709512 | tf_op jit(solution)/shard_map/ppermute | solution.py:56
  90.3 18.7 %collective-permute-start.11 = (bf16[48,6272]{1,0:T(8,128)(2,1)S(1)}, bf16[48,6272]{1,0:T(8,128)(2,1)S(1)}, u32[]{:S(2)}, u32[]{:S(2)}) collective-permute-start(bf16[48,6272]{1,0:T(8,128)(2,1)S(1)} %get-tuple-element.159.refs_0_), channel_id=1, source_target_pairs={{0,2},{1,3},{2,0},{3,1},{4,6},{5,7},{6,4},{7,5},{8,10},{9,11},{10,... | collective-permute-start | bytes 1806344 | tf_op jit(solution)/shard_map/ppermute | solution.py:56
  91.9 33.1 %copy-start.24 = (f32[1280,512]{1,0:T(8,128)}, f32[1280,512]{1,0:T(8,128)S(1)}, u32[]{:S(2)}) copy-start(f32[1280,512]{1,0:T(8,128)S(1)} %convolution_add_fusion) | copy-start | bytes 7864324
  119.4 17.0 %collective-permute-start.13 = (bf16[640,512]{1,0:T(8,128)(2,1)}, bf16[640,512]{1,0:T(8,128)(2,1)}, u32[]{:S(2)}, u32[]{:S(2)}) collective-permute-start(bf16[640,512]{1,0:T(8,128)(2,1)} %dynamic-slice_convert_fusion), channel_id=1, source_target_pairs={{0,4},{1,5},{2,6},{3,7},{4,0},{5,1},{6,2},{7,3},{8,12},{9,13},{10,... | collective-permute-start | bytes 1966088 | tf_op jit(solution)/shard_map/ppermute | solution.py:56
  121.0 17.2 %collective-permute-start.14 = (bf16[48,6272]{1,0:T(8,128)(2,1)}, bf16[48,6272]{1,0:T(8,128)(2,1)}, u32[]{:S(2)}, u32[]{:S(2)}) collective-permute-start(bf16[48,6272]{1,0:T(8,128)(2,1)} %slice.46), channel_id=1, source_target_pairs={{0,2},{1,3},{2,0},{3,1},{4,6},{5,7},{6,4},{7,5},{8,10},{9,11},{10,... | collective-permute-start | bytes 1806344 | tf_op jit(solution)/shard_map/ppermute | solution.py:56
  121.5 3.6 %collective-permute-start.15 = (f32[1,256]{1,0:T(1,128)S(1)}, f32[1,256]{1,0:T(1,128)S(1)}, u32[]{:S(2)}, u32[]{:S(2)}) collective-permute-start(f32[1,256]{1,0:T(1,128)S(1)} %get-tuple-element.146), channel_id=1, source_target_pairs={{0,16},{16,0},{1,17},{17,1},{2,18},{18,2},{3,19},{19,3},{4,20},{20... | collective-permute-start | bytes 3080 | tf_op jit(solution)/shard_map/ppermute | solution.py:56
  125.0 1.1 collective-permute-start.16
  126.2 10.0 %collective-permute-start.17 = (f32[1,256]{1,0:T(1,128)S(1)}, f32[1,256]{1,0:T(1,128)S(1)}, u32[]{:S(2)}, u32[]{:S(2)}) collective-permute-start(f32[1,256]{1,0:T(1,128)S(1)} %add.220), channel_id=1, source_target_pairs={{0,2},{1,3},{2,0},{3,1},{4,6},{5,7},{6,4},{7,5},{8,10},{9,11},{10,... | collective-permute-start | bytes 3080 | tf_op jit(solution)/shard_map/ppermute | solution.py:56
  138.2 21.0 %collective-permute-start.19 = (bf16[48,6272]{1,0:T(8,128)(2,1)}, bf16[48,6272]{1,0:T(8,128)(2,1)}, u32[]{:S(2)}, u32[]{:S(2)}) collective-permute-start(bf16[48,6272]{1,0:T(8,128)(2,1)} %collective-permute-done.10.refs_3_), channel_id=1, source_target_pairs={{0,2},{1,3},{2,0},{3,1},{4,6},{5,7},{6,4},{7,5},{8,10},{9,11},{10,... | collective-permute-start | bytes 1806344 | tf_op jit(solution)/shard_map/ppermute | solution.py:56
  140.0 17.1 %collective-permute-start.18 = (bf16[320,512]{1,0:T(8,128)(2,1)}, bf16[320,512]{1,0:T(8,128)(2,1)}, u32[]{:S(2)}, u32[]{:S(2)}) collective-permute-start(bf16[320,512]{1,0:T(8,128)(2,1)} %dynamic-slice_convert_fusion.1), channel_id=1, source_target_pairs={{0,8},{1,9},{2,10},{3,11},{4,12},{5,13},{6,14},{7,15},{8,0},{9,1},... | collective-permute-start | bytes 983048 | tf_op jit(solution)/shard_map/ppermute | solution.py:56
  142.5 6.4 %collective-permute-start.20 = (f32[1,256]{1,0:T(1,128)S(1)}, f32[1,256]{1,0:T(1,128)S(1)}, u32[]{:S(2)}, u32[]{:S(2)}) collective-permute-start(f32[1,256]{1,0:T(1,128)S(1)} %add.221), channel_id=1, source_target_pairs={{0,4},{1,5},{2,6},{3,7},{4,0},{5,1},{6,2},{7,3},{8,12},{9,13},{10,... | collective-permute-start | bytes 3080 | tf_op jit(solution)/shard_map/ppermute | solution.py:56
  165.9 20.3 %collective-permute-start.23 = (bf16[512,6272]{1,0:T(8,128)(2,1)}, bf16[512,6272]{1,0:T(8,128)(2,1)}, u32[]{:S(2)}, u32[]{:S(2)}) collective-permute-start(bf16[512,6272]{1,0:T(8,128)(2,1)} %shard_map.130.own_ref), channel_id=1, source_target_pairs={{0,1},{1,0},{2,3},{3,2},{4,5},{5,4},{6,7},{7,6},{8,9},{9,8},{10,11... | collective-permute-start | bytes 19267592 | tf_op jit(solution)/shard_map/ppermute | solution.py:56
  167.5 8.7 %collective-permute-start.24 = (f32[320]{0:T(512)S(1)}, f32[320]{0:T(512)S(1)}, u32[]{:S(2)}, u32[]{:S(2)}) collective-permute-start(f32[320]{0:T(512)S(1)} %dynamic-slice_divide_fusion), channel_id=1, source_target_pairs={{0,1},{1,0},{2,3},{3,2},{4,5},{5,4},{6,7},{7,6},{8,9},{9,8},{10,11... | collective-permute-start | bytes 3848 | tf_op jit(solution)/shard_map/ppermute | solution.py:56
  168.0 18.1 %collective-permute-start.22 = (bf16[320,512]{1,0:T(8,128)(2,1)S(1)}, bf16[320,512]{1,0:T(8,128)(2,1)S(1)}, u32[]{:S(2)}, u32[]{:S(2)}) collective-permute-start(bf16[320,512]{1,0:T(8,128)(2,1)S(1)} %get-tuple-element.178.refs_0_), channel_id=1, source_target_pairs={{0,2},{1,3},{2,0},{3,1},{4,6},{5,7},{6,4},{7,5},{8,10},{9,11},{10,... | collective-permute-start | bytes 983048 | tf_op jit(solution)/shard_map/ppermute | solution.py:56
  168.8 17.4 %collective-permute-start.21 = (bf16[320,512]{1,0:T(8,128)(2,1)S(1)}, bf16[320,512]{1,0:T(8,128)(2,1)S(1)}, u32[]{:S(2)}, u32[]{:S(2)}) collective-permute-start(bf16[320,512]{1,0:T(8,128)(2,1)S(1)} %get-tuple-element.178.refs_0_), channel_id=1, source_target_pairs={{0,8},{1,9},{2,10},{3,11},{4,12},{5,13},{6,14},{7,15},{8,0},{9,1},... | collective-permute-start | bytes 983048 | tf_op jit(solution)/shard_map/ppermute | solution.py:56
  168.8 17.2 %collective-permute-start.26 = (f32[1,256]{1,0:T(1,128)S(1)}, f32[1,256]{1,0:T(1,128)S(1)}, u32[]{:S(2)}, u32[]{:S(2)}) collective-permute-start(f32[1,256]{1,0:T(1,128)S(1)} %add.225), channel_id=1, source_target_pairs={{0,8},{1,9},{2,10},{3,11},{4,12},{5,13},{6,14},{7,15},{8,0},{9,1},... | collective-permute-start | bytes 3080 | tf_op jit(solution)/shard_map/ppermute | solution.py:56
  176.2 9.8 %collective-permute-start.25 = (f32[1,320]{1,0:T(1,128)S(1)}, f32[1,320]{1,0:T(1,128)S(1)}, u32[]{:S(2)}, u32[]{:S(2)}) collective-permute-start(f32[1,320]{1,0:T(1,128)S(1)} %broadcast_in_dim.158), channel_id=1, source_target_pairs={{0,16},{16,0},{1,17},{17,1},{2,18},{18,2},{3,19},{19,3},{4,20},{20... | collective-permute-start | bytes 3848 | tf_op jit(solution)/shard_map/ppermute | solution.py:56
  186.2 17.0 %collective-permute-start.27 = (bf16[640,512]{1,0:T(8,128)(2,1)S(1)}, bf16[640,512]{1,0:T(8,128)(2,1)S(1)}, u32[]{:S(2)}, u32[]{:S(2)}) collective-permute-start(bf16[640,512]{1,0:T(8,128)(2,1)S(1)} %pad_maximum_fusion), channel_id=1, source_target_pairs={{0,4},{1,5},{2,6},{3,7},{4,0},{5,1},{6,2},{7,3},{8,12},{9,13},{10,... | collective-permute-start | bytes 1966088 | tf_op jit(solution)/shard_map/ppermute | solution.py:56
  186.3 16.8 %collective-permute-start.28 = (bf16[320,512]{1,0:T(8,128)(2,1)S(1)}, bf16[320,512]{1,0:T(8,128)(2,1)S(1)}, u32[]{:S(2)}, u32[]{:S(2)}) collective-permute-start(bf16[320,512]{1,0:T(8,128)(2,1)S(1)} %collective-permute-done.21.refs_1_), channel_id=1, source_target_pairs={{0,2},{1,3},{2,0},{3,1},{4,6},{5,7},{6,4},{7,5},{8,10},{9,11},{10,... | collective-permute-start | bytes 983048 | tf_op jit(solution)/shard_map/ppermute | solution.py:56
  187.6 15.5 %collective-permute-start.29 = (f32[2,320]{1,0:T(2,128)S(1)}, f32[2,320]{1,0:T(2,128)S(1)}, u32[]{:S(2)}, u32[]{:S(2)}) collective-permute-start(f32[2,320]{1,0:T(2,128)S(1)} %broadcast_select_fusion.4), channel_id=1, source_target_pairs={{0,8},{1,9},{2,10},{3,11},{4,12},{5,13},{6,14},{7,15},{8,0},{9,1},... | collective-permute-start | bytes 7688 | tf_op jit(solution)/shard_map/ppermute | solution.py:56
  189.6 20.0 %copy-start.27 = (s32[32,1]{0,1:T(1,128)S(1)}, s32[32,1]{0,1:T(1,128)}, u32[]{:S(2)}) copy-start(s32[32,1]{0,1:T(1,128)} %param.17) | copy-start | bytes 388
  203.2 5.8 %collective-permute-start.38 = (f32[2,2,320]{2,1,0:T(2,128)S(1)}, f32[2,2,320]{2,1,0:T(2,128)S(1)}, u32[]{:S(2)}, u32[]{:S(2)}) collective-permute-start(f32[2,2,320]{2,1,0:T(2,128)S(1)} %broadcast_select_fusion.3), channel_id=1, source_target_pairs={{0,6},{1,7},{2,4},{3,5},{4,2},{5,3},{6,0},{7,1},{8,14},{9,15},{10,... | collective-permute-start | bytes 15368 | tf_op jit(solution)/shard_map/ppermute | solution.py:56
  204.1 23.8 %collective-permute-start.37 = (f32[2,2,320]{2,1,0:T(2,128)S(1)}, f32[2,2,320]{2,1,0:T(2,128)S(1)}, u32[]{:S(2)}, u32[]{:S(2)}) collective-permute-start(f32[2,2,320]{2,1,0:T(2,128)S(1)} %broadcast_select_fusion.3), channel_id=1, source_target_pairs={{0,2},{1,3},{2,0},{3,1},{4,6},{5,7},{6,4},{7,5},{8,10},{9,11},{10,... | collective-permute-start | bytes 15368 | tf_op jit(solution)/shard_map/ppermute | solution.py:56
  204.9 23.1 %collective-permute-start.36 = (f32[2,2,320]{2,1,0:T(2,128)S(1)}, f32[2,2,320]{2,1,0:T(2,128)S(1)}, u32[]{:S(2)}, u32[]{:S(2)}) collective-permute-start(f32[2,2,320]{2,1,0:T(2,128)S(1)} %broadcast_select_fusion.3), channel_id=1, source_target_pairs={{0,4},{1,5},{2,6},{3,7},{4,0},{5,1},{6,2},{7,3},{8,12},{9,13},{10,... | collective-permute-start | bytes 15368 | tf_op jit(solution)/shard_map/ppermute | solution.py:56
  206.8 29.0 %collective-permute-start.33 = (bf16[640,512]{1,0:T(8,128)(2,1)S(1)}, bf16[640,512]{1,0:T(8,128)(2,1)S(1)}, u32[]{:S(2)}, u32[]{:S(2)}) collective-permute-start(bf16[640,512]{1,0:T(8,128)(2,1)S(1)} %collective-permute-done.27.refs_2_), channel_id=1, source_target_pairs={{0,2},{1,3},{2,0},{3,1},{4,6},{5,7},{6,4},{7,5},{8,10},{9,11},{10,... | collective-permute-start | bytes 1966088 | tf_op jit(solution)/shard_map/ppermute | solution.py:56
  207.8 21.8 %collective-permute-start.32 = (bf16[640,512]{1,0:T(8,128)(2,1)S(1)}, bf16[640,512]{1,0:T(8,128)(2,1)}, u32[]{:S(2)}, u32[]{:S(2)}) collective-permute-start(bf16[640,512]{1,0:T(8,128)(2,1)S(1)} %collective-permute-done.27.refs_2_), channel_id=1, source_target_pairs={{0,1},{1,0},{2,3},{3,2},{4,5},{5,4},{6,7},{7,6},{8,9},{9,8},{10,11... | collective-permute-start | bytes 1966088 | tf_op jit(solution)/shard_map/ppermute | solution.py:56
  209.0 19.4 %collective-permute-start.30 = (bf16[320,512]{1,0:T(8,128)(2,1)S(1)}, bf16[320,512]{1,0:T(8,128)(2,1)S(1)}, u32[]{:S(2)}, u32[]{:S(2)}) collective-permute-start(bf16[320,512]{1,0:T(8,128)(2,1)S(1)} %get-tuple-element.178.refs_0_), channel_id=1, source_target_pairs={{0,1},{1,0},{2,3},{3,2},{4,5},{5,4},{6,7},{7,6},{8,9},{9,8},{10,11... | collective-permute-start | bytes 983048 | tf_op jit(solution)/shard_map/ppermute | solution.py:56
  209.6 18.4 %copy-start.4 = (bf16[320,512]{1,0:T(8,128)(2,1)S(1)}, bf16[320,512]{1,0:T(8,128)(2,1)}, u32[]{:S(2)}) copy-start(bf16[320,512]{1,0:T(8,128)(2,1)} %copy-done.3) | copy-start | bytes 983044
  209.6 18.8 %copy-start.7 = (bf16[320,512]{1,0:T(8,128)(2,1)S(1)}, bf16[320,512]{1,0:T(8,128)(2,1)}, u32[]{:S(2)}) copy-start(bf16[320,512]{1,0:T(8,128)(2,1)} %copy-done.6) | copy-start | bytes 983044
  227.8 1.7 collective-permute-start.31
  227.9 6.4 %collective-permute-start.34 = (bf16[320,512]{1,0:T(8,128)(2,1)S(1)}, bf16[320,512]{1,0:T(8,128)(2,1)S(1)}, u32[]{:S(2)}, u32[]{:S(2)}) collective-permute-start(bf16[320,512]{1,0:T(8,128)(2,1)S(1)} %copy-done.4), channel_id=1, source_target_pairs={{0,1},{1,0},{2,3},{3,2},{4,5},{5,4},{6,7},{7,6},{8,9},{9,8},{10,11... | collective-permute-start | bytes 983048 | tf_op jit(solution)/shard_map/ppermute | solution.py:56
  228.4 6.7 %collective-permute-start.35 = (bf16[320,512]{1,0:T(8,128)(2,1)S(1)}, bf16[320,512]{1,0:T(8,128)(2,1)S(1)}, u32[]{:S(2)}, u32[]{:S(2)}) collective-permute-start(bf16[320,512]{1,0:T(8,128)(2,1)S(1)} %copy-done.7), channel_id=1, source_target_pairs={{0,1},{1,0},{2,3},{3,2},{4,5},{5,4},{6,7},{7,6},{8,9},{9,8},{10,11... | collective-permute-start | bytes 983048 | tf_op jit(solution)/shard_map/ppermute | solution.py:56
  228.7 9.3 %copy-start.5 = (bf16[320,512]{1,0:T(8,128)(2,1)S(1)}, bf16[320,512]{1,0:T(8,128)(2,1)}, u32[]{:S(2)}) copy-start(bf16[320,512]{1,0:T(8,128)(2,1)} %copy-done.3) | copy-start | bytes 983044
  228.7 9.3 %copy-start.8 = (bf16[320,512]{1,0:T(8,128)(2,1)S(1)}, bf16[320,512]{1,0:T(8,128)(2,1)}, u32[]{:S(2)}) copy-start(bf16[320,512]{1,0:T(8,128)(2,1)} %copy-done.6) | copy-start | bytes 983044
  235.8 2.1 collective-permute-start.39
  (19 other events, 27.9 us)

commit v4 on v3

--- a/solution.py
+++ b/solution.py
@@ -15,7 +15,7 @@
 TAGS = 128
 STRIP = 512
 UNROLL = 5
-KEYS_MIB, STACK_MIB, PLACE_MIB, SLOTS_MIB = 36, 20, 30, 44
+KEYS_MIB, STACK_MIB, PLACE_MIB, SLOTS_MIB = 56, 20, 36, 44
 
 
 epsilon = 1e-06
@@ -86,7 +86,9 @@
 
 
 def keys_kernel(blocks, plan, pieces, index_ref, *refs):
-    sources, outs, refs = refs[:9], refs[9 : 9 + blocks], refs[9 + blocks :]
+    sources, outs, rests = refs[:9], refs[9 : 9 + blocks], refs[9 + blocks : 9 + 2 * blocks]
+    refs = refs[9 + 2 * blocks :]
+    main = outs[0].shape[0]
     planes, packet = plan[:2]
     packs, refs = refs[: len(pieces)], refs[len(pieces) :]
     (keys_out, sums_out), held, (w_all, h_all, keys, sems) = refs[:2], refs[2:10], refs[10:]
@@ -117,9 +119,13 @@
         fetch(i).start()
     for copy in copies[1:3]:
         copy.wait()
-    place, tags, over = packet_plan(index_ref[blocks], len_ref[...], dest_ref[...], rows, *plan)
+    place, tags, over, order, many = packet_plan(
+        index_ref[blocks], len_ref[...], dest_ref[...], rows, main, *plan
+    )
     places = lax.broadcasted_iota(jnp.int32, (planes * packet, rows), 0)
     onehot = (places == place).astype(F32).astype(BF16)
+    places = lax.broadcasted_iota(jnp.int32, (rows, rows), 0)
+    squeeze = (places == order).astype(F32).astype(BF16)
     for copy in copies[3:]:
         copy.wait()
     weight = token_weights(importance_ref[...], len_ref[...], version_ref[...])
@@ -142,7 +148,7 @@
 
     def project(i, carry):
         h = (hidden_ref[:, strip(i)].astype(F32) * inv * gain_ref[:, strip(i)]).astype(BF16)
-        h_all[:, strip(i)] = h
+        h_all[:, strip(i)] = jnp.dot(squeeze, h, preferred_element_type=F32).astype(BF16)
         fetch(i).wait()
         keys[...] += jnp.dot(h, w_all[strip(i), :], preferred_element_type=F32)
         return carry
@@ -150,7 +156,9 @@
     lax.fori_loop(0, strips, project, 0, unroll=UNROLL)
     width = outs[0].shape[1] - keys.shape[1]
     for k in range(blocks):
-        outs[k][:, :width] = h_all[:, pl.ds(pl.multiple_of(index_ref[k] * width, width), width)]
+        columns = pl.ds(pl.multiple_of(index_ref[k] * width, width), width)
+        outs[k][:, :width] = h_all[:main, columns]
+        rests[k][:, :width] = h_all[main:, columns]
     head = key_gain_ref.shape[1]
     kgain = jnp.zeros((1, head), F32)
     for a in range(keys.shape[1] // head):
@@ -163,17 +171,19 @@
         grad = scale * scaled - key * (scale * scale * scale) * jnp.mean(
             scaled * key, 1, keepdims=True
         )
-        grad = grad.astype(BF16)
-        keys_out[:, span] = grad
-        for k in range(blocks):
-            outs[k][:, width + a * head : width + (a + 1) * head] = grad
+        keys_out[:, span] = grad.astype(BF16)
     sums_out[:, :head] = kgain
-    sums_out[:, head:] = jnp.broadcast_to(over, (1, head))
+    sums_out[:, head : 2 * head] = jnp.broadcast_to(over, (1, head))
+    sums_out[:, 2 * head :] = jnp.broadcast_to(many, (1, head))
+    packed = jnp.dot(squeeze, keys_out[...], preferred_element_type=F32).astype(BF16)
+    for k in range(blocks):
+        outs[k][:, width:] = packed[:main]
+        rests[k][:, width:] = packed[main:]
     packed = jnp.dot(onehot, keys_out[...], preferred_element_type=F32).astype(BF16)
     spread(packed, slice(features + TAGS, features + TAGS + keys.shape[1]))
 
 
-def packet_plan(learn, len_row, dest_row, rows, planes, packet, passed_on, capacity):
+def packet_plan(learn, len_row, dest_row, rows, main, planes, packet, passed_on, capacity):
     tiles = dest_row.shape[1]
     dest_column = to_column(dest_row, tiles)
     shape = (tiles, tiles)
@@ -202,6 +212,8 @@
     start = (kinds // 2) * packet + jnp.where(kinds % 2 == 1, packet - count, 0)
     position = jnp.sum(jnp.where(member, ahead + start, 0), 0, keepdims=True)
     position = jnp.where(valid, position, -1)
+    order = jnp.where(valid, jnp.sum(ahead, 0, keepdims=True), -1)
+    many = jnp.where(jnp.sum(count, 0, keepdims=True) > main, 1.0, 0.0)
     plane_of = lax.broadcasted_iota(jnp.int32, (2 * planes, planes), 0) // 2
     same_plane = plane_of == lax.broadcasted_iota(jnp.int32, (2 * planes, planes), 1)
     together = jnp.sum(jnp.where(same_plane, count, 0), 0, keepdims=True)
@@ -214,7 +226,7 @@
     slot = learn * capacity + row_values(rank_row, rows)
     tags = jnp.where(lane == 0, row_values(dest_row, rows) + 1, jnp.where(lane == 1, slot, line))
     tags = jnp.where(lane < 3, tags, 0)
-    return position, tags.astype(F32).astype(BF16), over
+    return position, tags.astype(F32).astype(BF16), over, order, many
 
 
 def stack_kernel(*refs):
@@ -222,24 +234,30 @@
     for part in refs[:-1]:
         out[used : used + part.shape[0], :] = part[...]
         used += part.shape[0]
-    if used < out.shape[0]:
-        out[used:, :] = jnp.zeros((out.shape[0] - used, out.shape[1]), BF16)
-
-
-def place_kernel(me_ref, own_ref, other_ref, rows_out, keys_out, chosen):
+
+
+def place_kernel(me_ref, *refs):
+    sources, (rows_out, keys_out, held, chosen, sems) = refs[:4], refs[4:]
     slots, features = rows_out.shape
-    count = own_ref.shape[0]
-    tag = slice(features, features + TAGS)
-    tags = jnp.concatenate([own_ref[:, tag], other_ref[:, tag]], 0)
-    tags = tags.astype(F32).T.astype(jnp.int32)
+    copies, used = [], 0
+    for i, source in enumerate(sources):
+        place = held.at[pl.ds(used, source.shape[0])]
+        copies.append(pltpu.make_async_copy(source, place, sems.at[i]))
+        copies[-1].start()
+        used += source.shape[0]
+    if used < held.shape[0]:
+        held[used:, :] = jnp.zeros((held.shape[0] - used, held.shape[1]), BF16)
+    for copy in copies:
+        copy.wait()
+    tags = held[:, features : features + TAGS].astype(F32).T.astype(jnp.int32)
     target = jnp.where(tags[0:1] == me_ref[0] + 1, tags[1:2] * TILE + tags[2:3], -1)
-    places = lax.broadcasted_iota(jnp.int32, (slots, 2 * count), 0)
+    places = lax.broadcasted_iota(jnp.int32, (slots, held.shape[0]), 0)
     chosen[...] = (places == target).astype(F32).astype(BF16)
 
     def pick(columns):
-        rows = jnp.dot(chosen[:, :count], own_ref[:, columns], preferred_element_type=F32)
-        rows += jnp.dot(chosen[:, count:], other_ref[:, columns], preferred_element_type=F32)
-        return rows.astype(BF16)
+        return jnp.dot(
+            chosen[...], held[:, columns], preferred_element_type=F32
+        ).astype(BF16)
 
     def put(i, carry):
         strip = pl.ds(pl.multiple_of(i * STRIP, STRIP), STRIP)
@@ -370,6 +388,7 @@
     packet = min(PACKET, 4 * capacity * TILE)
     passed_on = min(PASSED_ON, 2 * capacity * TILE)
     rows, features = hidden.shape
+    main = rows * 3 // 4
     key_count = cotangent.shape[1]
     head = key_gain.shape[0]
     strips = features // STRIP
@@ -395,14 +414,15 @@
         functools.partial(
             keys_kernel, blocks, (planes, packet, passed_on, capacity), pieces
         ),
-        out_shape=[jax.ShapeDtypeStruct((rows, width + key_count), BF16)] * blocks
+        out_shape=[jax.ShapeDtypeStruct((main, width + key_count), BF16)] * blocks
+        + [jax.ShapeDtypeStruct((rows - main, width + key_count), BF16)] * blocks
         + [jax.ShapeDtypeStruct((high - low, packed_width), BF16) for low, high in pieces]
         + [
             jax.ShapeDtypeStruct((rows, key_count), BF16),
-            jax.ShapeDtypeStruct((1, 2 * head), F32),
+            jax.ShapeDtypeStruct((1, 3 * head), F32),
         ],
         in_specs=[SMEM] + [ANY] * 9,
-        out_specs=[VMEM] * (blocks + len(pieces) + 2),
+        out_specs=[VMEM] * (2 * blocks + len(pieces) + 2),
         scratch_shapes=[
             pltpu.VMEM((rows, features), BF16),
             pltpu.VMEM((1, tiles), jnp.int32),
@@ -433,13 +453,10 @@
         cotangent,
         w_key,
     )
-    operands, packs, (grad_keys, sums) = (
-        made[:blocks],
-        made[blocks : blocks + len(pieces)],
-        made[blocks + len(pieces) :],
-    )
-
-    def gather(k):
+    operands, rests, made = made[:blocks], made[blocks : 2 * blocks], made[2 * blocks :]
+    packs, (grad_keys, sums) = made[: len(pieces)], made[len(pieces) :]
+
+    def gather(k, operands):
         step, dy = steps[k]
         pairs = [
             (p * learners + j, ((p + step) % gens) * learners + (j ^ (2 * dy)))
@@ -464,36 +481,66 @@
     last = planes - 1
     held, passed = {0: packs[1], planes: packs[0]}, {}
 
-    gathered = [gather(k) for k in direct + diagonal]
-    for k in range(2, last):
-        held[k] = across_learn(packs[1 + k], 4 * k)
-    held[planes + 1] = across_learn(packs[-2], 4 * last)
-    gathered, held, packs = barrier((gathered, held, packs))
-
-    total = products(operands[0]) + products(across_learn(operands[0], 1))
-    for part in gathered:
-        total = total + products(part) + products(across_learn(part, 1))
-    held[1] = across_learn(packs[2], 4)
-    held[last] = across_learn(packs[-1], 4 * last)
-    for k in (0, *range(2, last)):
-        passed[k] = over_y(held[k])
-    total, held, passed = barrier((total, held, passed))
+    def add_products(total, parts):
+        for part in parts:
+            total = total + products(part) + products(across_learn(part, 1))
+        return total
 
     bits = [4 << b for b in range(planes.bit_length() - 1)]
-    for n, bit in enumerate(bits):
+
+    def halve(total, bit):
         upper = (learn // bit) % 2
         tall = total.shape[0] // 2
         sent = lax.dynamic_slice_in_dim(total, (1 - upper) * tall, tall, 0).astype(BF16)
         kept = lax.dynamic_slice_in_dim(total, upper * tall, tall, 0)
-        total = kept + across_learn(sent, bit).astype(F32)
+        return kept + across_learn(sent, bit).astype(F32)
+
+    def stack(parts):
+        return pl.pallas_call(
+            stack_kernel,
+            out_shape=jax.ShapeDtypeStruct(
+                (sum(part.shape[0] for part in parts), packed_width), BF16
+            ),
+            in_specs=[VMEM] * len(parts),
+            out_specs=VMEM,
+            compiler_params=limit(STACK_MIB),
+        )(*parts)
+
+    gathered = [gather(k, operands) for k in direct + diagonal]
+    for k in range(1, last):
+        held[k] = across_learn(packs[1 + k], 4 * k)
+    gathered, held, packs = barrier((gathered, held, packs))
+
+    total = add_products(0.0, [operands[0], *gathered])
+    held[last] = across_learn(packs[-1], 4 * last)
+    passed[0] = over_y(held[0])
+    passed[1] = over_y(held[1])
+    total, held, passed, packs = barrier((total, held, passed, packs))
+
+    for n, bit in enumerate(bits):
+        total = halve(total, bit)
         if n == 0:
-            passed[1] = over_y(held[1])
+            held[planes + 1] = across_learn(packs[-2], 4 * last)
+            for k in range(2, last):
+                passed[k] = over_y(held[k])
             sums = butterfly_sum(sums, (("gen", gens),))
             sums = butterfly_sum(sums, (("learn", 4),), learners)
         if n == 1:
+            stacked = stack(list(held.values()) + list(passed.values()))
             passed[last] = over_y(held[last])
-            sums = sums + across_learn(sums, bits[0])
-        total, passed, held, sums = barrier((total, passed, held, sums))
+            for other_bit in bits:
+                sums = sums + across_learn(sums, other_bit)
+            total, passed, stacked, sums = barrier((total, passed, stacked, sums))
+        else:
+            total, passed, held, sums = barrier((total, passed, held, sums))
+
+    def add_rests(state):
+        total = add_products(0.0, [rests[0]] + [gather(k, rests) for k in range(1, blocks)])
+        for bit in bits:
+            total = halve(total, bit)
+        return jnp.zeros((), F32), state[1] + total
+
+    _, total = lax.while_loop(lambda state: state[0] > 0.5, add_rests, (sums[0, -1], total))
 
     tall = total.shape[0]
     first = (gen * 2 + across) * width
@@ -503,32 +550,21 @@
     gains = jnp.sum(w_part * total, 1) / lax.dynamic_slice_in_dim(in_gain, first, tall)
 
     parts, y_parts, offsets = [total.astype(BF16)], [], [0]
-    order = list(held.values()) + list(passed.values())
-    used = sum(part.shape[0] for part in order)
-    place = -(-used // 128) * 128
     for n, bit in enumerate(reversed(bits)):
         block = parts[0] if n == 0 else jnp.concatenate(parts, 0)
         received = across_learn(block, bit)
         y_parts.append(across_learn(parts[-1], 2))
         if n == 0:
-            all_rows = pl.pallas_call(
-                stack_kernel,
-                out_shape=jax.ShapeDtypeStruct((place, packed_width), BF16),
-                in_specs=[VMEM] * len(order),
-                out_specs=VMEM,
-                compiler_params=limit(STACK_MIB),
-            )(*order)
-            other_rows = across_learn(all_rows, 1)
+            other_stacked = across_learn(stacked, 1)
+            other_passed = across_learn(passed[last], 1)
             gains = gains + across_learn(gains, 1)
             gains = gains[None]
             step = 1
             while step < gens:
                 gains = join(gains, swap(gains, "gen", gens, step), (gen // step) % 2)
                 step *= 2
-            for other_bit in bits[1:]:
-                sums = sums + across_learn(sums, other_bit)
-            received, y_parts, all_rows, other_rows, gains, sums = barrier(
-                (received, y_parts, all_rows, other_rows, gains, sums)
+            received, y_parts, other_stacked, other_passed, gains = barrier(
+                (received, y_parts, other_stacked, other_passed, gains)
             )
         parts = parts + [received]
         weight = planes >> (bits.index(bit) + 1)
@@ -536,17 +572,22 @@
         if n:
             wide = bits[-n]
             gains = join_at(gains, across_learn(gains, wide), (learn // wide) % 2, 1)
+    place = -(-2 * (stacked.shape[0] + passed_on) // 128) * 128
     rows_placed, keys_placed = pl.pallas_call(
         place_kernel,
         out_shape=[
             jax.ShapeDtypeStruct((SLOTS * TILE, features), BF16),
             jax.ShapeDtypeStruct((SLOTS * TILE, key_count), BF16),
         ],
-        in_specs=[SMEM, VMEM, VMEM],
+        in_specs=[SMEM] + [ANY] * 4,
         out_specs=[VMEM] * 2,
-        scratch_shapes=[pltpu.VMEM((SLOTS * TILE, 2 * place), BF16)],
+        scratch_shapes=[
+            pltpu.VMEM((place, packed_width), BF16),
+            pltpu.VMEM((SLOTS * TILE, place), BF16),
+            pltpu.SemaphoreType.DMA((4,)),
+        ],
         compiler_params=limit(PLACE_MIB),
-    )(learn[None], all_rows, other_rows)
+    )(learn[None], stacked, passed[last], other_stacked, other_passed)
     parts, y_parts, gains, sums, rows_placed, keys_placed = barrier(
         (parts, y_parts, gains, sums, rows_placed, keys_placed)
     )
@@ -558,7 +599,7 @@
             jnp.zeros((), F32),
             swap_dense(hidden, grad_keys, w_key, in_gain, destination[:, 0], learners),
         ),
-        (sums[0, -1], rows_placed),
+        (sums[0, head], rows_placed),
     )
     grad_slots = pl.pallas_call(
         slots_kernel,
@@ -571,7 +612,7 @@
             pltpu.SemaphoreType.DMA((strips,)),
         ],
         compiler_params=limit(SLOTS_MIB),
-    )(sums[0, -1:], rows_placed, keys_placed, w_key, in_gain_row)
+    )(sums[0, head : head + 1], rows_placed, keys_placed, w_key, in_gain_row)
     core_parts = [across_learn(part, 1) for part in parts]
     core_y = [across_learn(part, 1) for part in y_parts[:-1]]
     first = sum(((learn // bit) % 2) * (planes >> (n + 1)) for n, bit in enumerate(bits))

time: 244 us -> 229 us (0.939)
  waiting for transfers between devices: 115 us -> 86.5 us
  starting transfers between devices: 36.5 us -> 46.8 us
  local copies, waits for them, and re-layouts: 16.8 us -> 25.1 us
  Pallas kernels: 57 us -> 54.5 us
  matrix products: 10.2 us -> 7.72 us
    ppermute x37 -> x38, waiting for transfers between devices: 115 us -> 51.5 us  [swap(): return lax.ppermute(x, axis, [(i, i ^ bit) for i in range(size)])]
    ppermute x3, waiting for transfers between devices: 0.01 us -> 35.1 us  [gather(): return lax.ppermute(operands[k], BOTH, pairs)]
    ppermute x37 -> x38, starting transfers between devices: 32 us -> 43.3 us  [swap(): return lax.ppermute(x, axis, [(i, i ^ bit) for i in range(size)])]
    unnamed x54 -> x65, local copies, waits for them, and re-layouts: 12.4 us -> 18.2 us
    pallas_call x1, Pallas kernels: 4.61 us -> 1.53 us  [stack(): pl.pallas_call(stack_kernel, out_shape=jax.ShapeDtypeStruct((sum((part.sh...]
    dot_general x8, matrix products: 10.2 us -> 7.72 us  [dot_rows(): lax.dot_general(a, b, (((0,), (0,)), ((), ())), preferred_element_type=F32)]
  transfers between devices with their start and end apart: 40 -> 41, of which waited for: 16 -> 15; matrix products, arithmetic and copies ran while one was open for 8% -> 8% of each run, Pallas kernels for 15% -> 16%
where the time goes in v4:
time: 229 us; the launch traced here: 228 us
  waiting for transfers between devices  86.5 us (38%)
  Pallas kernels  54.5 us (24%)
  starting transfers between devices  46.8 us (20%)
  local copies, waits for them, and re-layouts  25.1 us (11%)
  matrix products  7.72 us (3%)
  other arithmetic  4.6 us (2%)
    ppermute x38, waiting for transfers between devices, swap(): return lax.ppermute(x, axis, [(i, i ^ bit) for i in range(size)])  51.5 us
    ppermute x38, starting transfers between devices, swap(): return lax.ppermute(x, axis, [(i, i ^ bit) for i in range(size)])  43.3 us
    ppermute x3, waiting for transfers between devices, gather(): return lax.ppermute(operands[k], BOTH, pairs)  35.1 us
    unnamed x65, local copies, waits for them, and re-layouts  18.2 us
    pallas_call x1, Pallas kernels, body(): pl.pallas_call(slots_kernel, out_shape=jax.ShapeDtypeStruct((SLOTS * TILE...  18.1 us
    pallas_call x1, Pallas kernels, body(): pl.pallas_call(functools.partial(keys_kernel, blocks, (planes, packet, pa...  14.7 us
    pallas_call x1, Pallas kernels, body(): pl.pallas_call(place_kernel, out_shape=[jax.ShapeDtypeStruct((SLOTS * TIL...  12 us
    pallas_call x2, Pallas kernels, lay_out(): pl.pallas_call(functools.partial(output_kernel, sizes), out_shape=jax.Sha...  8.1 us
  transfers between devices with their start and end apart: 41, of which 15 were waited for; matrix products, arithmetic and copies ran while one was open for 8% of the time, Pallas kernels for 16%

profile of v4, /device:TPU:0, one launch (start us, length us, event | category | flops | bytes accessed | tf_op | source)
XLA Modules:
  0.0 227.8 jit_solution(9873195328051711155)
XLA Ops:
  1.3 14.7 %shard_map.129 = (bf16[192,2304]{1,0:T(8,128)(2,1)}, bf16[192,2304]{1,0:T(8,128)(2,1)}, bf16[192,2304]{1,0:T(8,128)(2,1)}, bf16[192,2304]{1,0:T(8,128)(2,1)}, bf...) custom-call(s32[5]{0:T(128)} %stack.23.index_ref, ...), custom_call_target="tpu_custom_call" | custom-call | flops 2684354560 | bytes 16777216 | tf_op jit(solution)/shard_map/pallas_call | solution.py:413
  16.5 2.6 %collective-permute-start.13 = (bf16[72,6272]{1,0:T(8,128)(2,1)}, bf16[72,6272]{1,0:T(8,128)(2,1)S(1)}, u32[]{:S(2)}, u32[]{:S(2)}) collective-permute-start(bf16[72,6272]{1,0:T(8,128)(2,1)} %get-tuple-element.159), channel_id=1, source_target_pairs={{0,4},{1,5},{2,6},{3,7},{4,0},{5,1},{6,2},{7,3},{8,12},{9,13},{10,... | collective-permute-start | bytes 2709512 | tf_op jit(solution)/shard_map/ppermute | solution.py:56
  19.2 2.6 %collective-permute-start.14 = (bf16[72,6272]{1,0:T(8,128)(2,1)}, bf16[72,6272]{1,0:T(8,128)(2,1)S(1)}, u32[]{:S(2)}, u32[]{:S(2)}) collective-permute-start(bf16[72,6272]{1,0:T(8,128)(2,1)} %get-tuple-element.160), channel_id=1, source_target_pairs={{0,8},{1,9},{2,10},{3,11},{4,12},{5,13},{6,14},{7,15},{8,0},{9,1},... | collective-permute-start | bytes 2709512 | tf_op jit(solution)/shard_map/ppermute | solution.py:56
  21.8 1.5 collective-permute-start.10
  23.3 1.5 collective-permute-start.11
  26.2 1.7 fusion.53
  28.5 15.3 %collective-permute-done.10 = bf16[192,2304]{1,0:T(8,128)(2,1)} collective-permute-done((bf16[192,2304]{1,0:T(8,128)(2,1)}, bf16[192,2304]{1,0:T(8,128)(2,1)}, u32[]{:S(2)}, u32[]{:S(2)}) %collective-permute-start.10) | collective-permute-done | bytes 884768 | tf_op jit(solution)/shard_map/ppermute | solution.py:466
  43.8 2.4 %collective-permute-done.11 = bf16[192,2304]{1,0:T(8,128)(2,1)} collective-permute-done((bf16[192,2304]{1,0:T(8,128)(2,1)}, bf16[192,2304]{1,0:T(8,128)(2,1)}, u32[]{:S(2)}, u32[]{:S(2)}) %collective-permute-start.11) | collective-permute-done | bytes 884768 | tf_op jit(solution)/shard_map/ppermute | solution.py:466
  46.2 17.4 %collective-permute-done.12 = bf16[192,2304]{1,0:T(8,128)(2,1)S(1)} collective-permute-done((bf16[192,2304]{1,0:T(8,128)(2,1)}, bf16[192,2304]{1,0:T(8,128)(2,1)S(1)}, u32[]{:S(2)}, u32[]{:S(2)}) %collective-permute-start.12) | collective-permute-done | bytes 884768 | tf_op jit(solution)/shard_map/ppermute | solution.py:466
  63.6 1.6 collective-permute-start.20
  66.3 1.6 convolution_add_fusion.8
  67.9 1.7 fusion.50
  72.7 7.5 %collective-permute-done.20.refs_7_ = bf16[48,6272]{1,0:T(8,128)(2,1)S(1)} collective-permute-done((bf16[48,6272]{1,0:T(8,128)(2,1)S(1)}, bf16[48,6272]{1,0:T(8,128)(2,1)S(1)}, u32[]{:S(2)}, u32[]{:S(2)}) %collective-permute-start.20) | collective-permute-done | bytes 602144 | tf_op jit(solution)/shard_map/ppermute | solution.py:56
  81.1 9.7 %collective-permute-done.19.refs_6_ = bf16[48,6272]{1,0:T(8,128)(2,1)S(1)} collective-permute-done((bf16[48,6272]{1,0:T(8,128)(2,1)S(1)}, bf16[48,6272]{1,0:T(8,128)(2,1)S(1)}, u32[]{:S(2)}, u32[]{:S(2)}) %collective-permute-start.19) | collective-permute-done | bytes 602144 | tf_op jit(solution)/shard_map/ppermute | solution.py:56
  92.6 8.5 %collective-permute-start.21 = (bf16[640,512]{1,0:T(8,128)(2,1)}, bf16[640,512]{1,0:T(8,128)(2,1)}, u32[]{:S(2)}, u32[]{:S(2)}) collective-permute-start(bf16[640,512]{1,0:T(8,128)(2,1)} %dynamic-slice_convert_fusion.2), channel_id=1, source_target_pairs={{0,4},{1,5},{2,6},{3,7},{4,0},{5,1},{6,2},{7,3},{8,12},{9,13},{10,... | collective-permute-start | bytes 1966088 | tf_op jit(solution)/shard_map/ppermute | solution.py:56
  101.9 1.4 collective-permute-start.22
  103.3 1.4 collective-permute-start.23
  104.7 1.5 collective-permute-start.24
  106.2 2.1 collective-permute-done.24
  108.3 1.1 collective-permute-done.25
  110.1 6.9 %collective-permute-done.26 = f32[1,384]{1,0:T(1,128)S(1)} collective-permute-done((f32[1,384]{1,0:T(1,128)S(1)}, f32[1,384]{1,0:T(1,128)S(1)}, u32[]{:S(2)}, u32[]{:S(2)}) %collective-permute-start.26) | collective-permute-done | bytes 1568 | tf_op jit(solution)/shard_map/ppermute | solution.py:56
  117.0 1.8 convert_add_fusion
  118.7 4.5 %collective-permute-done.23.refs_5_ = bf16[24,6272]{1,0:T(8,128)(2,1)S(1)} collective-permute-done((bf16[24,6272]{1,0:T(8,128)(2,1)}, bf16[24,6272]{1,0:T(8,128)(2,1)S(1)}, u32[]{:S(2)}, u32[]{:S(2)}) %collective-permute-start.23) | collective-permute-done | bytes 301088 | tf_op jit(solution)/shard_map/ppermute | solution.py:56
  124.8 1.3 collective-permute-start.28
  126.8 3.0 %collective-permute-start.29 = (f32[1,384]{1,0:T(1,128)S(1)}, f32[1,384]{1,0:T(1,128)S(1)}, u32[]{:S(2)}, u32[]{:S(2)}) collective-permute-start(f32[1,384]{1,0:T(1,128)S(1)} %add.300), channel_id=1, source_target_pairs={{0,4},{1,5},{2,6},{3,7},{4,0},{5,1},{6,2},{7,3},{8,12},{9,13},{10,... | collective-permute-start | bytes 4616 | tf_op jit(solution)/shard_map/ppermute | solution.py:56
  129.8 3.0 %collective-permute-done.29 = f32[1,384]{1,0:T(1,128)S(1)} collective-permute-done((f32[1,384]{1,0:T(1,128)S(1)}, f32[1,384]{1,0:T(1,128)S(1)}, u32[]{:S(2)}, u32[]{:S(2)}) %collective-permute-start.29) | collective-permute-done | bytes 1568 | tf_op jit(solution)/shard_map/ppermute | solution.py:56
  132.8 3.3 %collective-permute-start.30 = (f32[1,384]{1,0:T(1,128)S(1)}, f32[1,384]{1,0:T(1,128)S(1)}, u32[]{:S(2)}, u32[]{:S(2)}) collective-permute-start(f32[1,384]{1,0:T(1,128)S(1)} %add.304), channel_id=1, source_target_pairs={{0,8},{1,9},{2,10},{3,11},{4,12},{5,13},{6,14},{7,15},{8,0},{9,1},... | collective-permute-start | bytes 4616 | tf_op jit(solution)/shard_map/ppermute | solution.py:56
  138.1 1.1 copy-done.3
  139.2 1.1 copy-done.5
  140.2 1.1 copy-done.7
  141.3 1.1 copy-done.9
  143.3 1.5 shard_map.130.refs_0_
  144.9 2.4 %copy-done = bf16[432,6272]{1,0:T(8,128)(2,1)} copy-done((bf16[432,6272]{1,0:T(8,128)(2,1)}, bf16[432,6272]{1,0:T(8,128)(2,1)S(1)}, u32[]{:S(2)}) %copy-start) | copy-done | bytes 5419032
  147.3 1.1 convert_add_fusion.1
  150.7 1.1 multiply_reduce_fusion
  153.2 5.9 %collective-permute-done.35 = f32[320]{0:T(512)S(1)} collective-permute-done((f32[320]{0:T(512)S(1)}, f32[320]{0:T(512)S(1)}, u32[]{:S(2)}, u32[]{:S(2)}) %collective-permute-start.35) | collective-permute-done | bytes 1312 | tf_op jit(solution)/shard_map/ppermute | solution.py:56
  159.1 1.5 collective-permute-start.36
  160.6 2.1 collective-permute-done.36
  162.8 7.2 %collective-permute-done.31.refs_1_ = bf16[320,512]{1,0:T(8,128)(2,1)S(1)} collective-permute-done((bf16[320,512]{1,0:T(8,128)(2,1)S(1)}, bf16[320,512]{1,0:T(8,128)(2,1)S(1)}, u32[]{:S(2)}, u32[]{:S(2)}) %collective-permute-start.31) | collective-permute-done | bytes 327712 | tf_op jit(solution)/shard_map/ppermute | solution.py:56
  170.2 1.1 collective-permute-start.38
  171.3 2.6 %collective-permute-start.39 = (f32[2,320]{1,0:T(2,128)S(1)}, f32[2,320]{1,0:T(2,128)S(1)}, u32[]{:S(2)}, u32[]{:S(2)}) collective-permute-start(f32[2,320]{1,0:T(2,128)S(1)} %broadcast_select_fusion.4), channel_id=1, source_target_pairs={{0,8},{1,9},{2,10},{3,11},{4,12},{5,13},{6,14},{7,15},{8,0},{9,1},... | collective-permute-start | bytes 7688 | tf_op jit(solution)/shard_map/ppermute | solution.py:56
  174.0 2.5 %copy-done.1 = bf16[432,6272]{1,0:T(8,128)(2,1)S(1)} copy-done((bf16[432,6272]{1,0:T(8,128)(2,1)S(1)}, bf16[432,6272]{1,0:T(8,128)(2,1)}, u32[]{:S(2)}) %copy-start.1) | copy-done | bytes 5419032
  177.6 12.0 %shard_map.131 = (bf16[512,5120]{1,0:T(8,128)(2,1)}, bf16[512,1024]{1,0:T(8,128)(2,1)S(1)}) custom-call(s32[1]{0:T(128)} %bitcast.10.me_ref, bf16[432,6272]{1,0:T(8,128)(2,1)S(1)} %copy-done.1, bf16[48,6272]{1,0:T(8,128)(2,1)S(1)} %collective-permute-done.28.refs_1_, bf16[432,6272]{1,0:T(8,128)(2,1)} %collective-permute-done.33.refs_2_, ...), custom_call_target="tpu_custom_call" | custom-call | tf_op jit(solution)/shard_map/pallas_call | solution.py:576
  190.2 1.1 collective-permute-start.47
  191.3 2.0 collective-permute-start.46
  196.0 18.1 %shard_map.133 = bf16[512,5120]{1,0:T(8,128)(2,1)} custom-call(f32[1]{0:T(128)} %bitcast.18.over_ref, bf16[512,5120]{1,0:T(8,128)(2,1)} %get-tuple-element.219.rows_ref, bf16[512,1024]{1,0:T(8,128)(2,1)S(1)} %get-tuple-element.220.keys_ref, bf16[5120,1024]{1,0:T(8,128)(2,1)} %get-tuple-element.373, f32[1,5120]{1,0:T(1,128)S(1)} %bitcast.29), custom_call_target="tpu_custom_call" | custom-call | tf_op jit(solution)/shard_map/pallas_call | solution.py:604
  215.8 4.8 %shard_map.132.refs_6_ = f32[2560,1024]{1,0:T(8,128)} custom-call(s32[5]{0:T(128)S(1)} %pad_add_fusion.index_ref, bf16[320,512]{1,0:T(8,128)(2,1)S(1)} %copy.19.refs_0_, bf16[320,512]{1,0:T(8,128)(2,1)S(1)} %collective-permute-done.31.refs_1_, bf16[640,512]{1,0:T(8,128)(2,1)S(1)} %collective-permute-done.37.refs_2_, ...), custom_call_target="tpu_custom_call" | custom-call | tf_op jit(solution)/shard_map/pallas_call | solution.py:343
  224.5 3.3 %shard_map.134 = f32[2560,1024]{1,0:T(8,128)} custom-call(s32[5]{0:T(128)S(1)} %pad_add_fusion.1.index_ref, bf16[320,512]{1,0:T(8,128)(2,1)S(1)} %copy-done.14, bf16[320,512]{1,0:T(8,128)(2,1)S(1)} %copy-done.17, bf16[640,512]{1,0:T(8,128)(2,1)S(1)} %collective-permute-done.43.refs_2_, ...), custom_call_target="tpu_custom_call", output_to_operand_aliasing={{}: (7, {})} | custom-call | tf_op jit(solution)/shard_map/pallas_call | solution.py:343
  (152 shorter events, 29.7 us)
Async XLA Ops:
  16.0 8.8 %collective-permute-start.9 = (bf16[192,2304]{1,0:T(8,128)(2,1)}, bf16[192,2304]{1,0:T(8,128)(2,1)S(1)}, u32[]{:S(2)}, u32[]{:S(2)}) collective-permute-start(bf16[192,2304]{1,0:T(8,128)(2,1)} %get-tuple-element.154), channel_id=1, source_target_pairs={{0,1},{1,0},{2,3},{3,2},{4,5},{5,4},{6,7},{7,6},{8,9},{9,8},{10,11... | collective-permute-start | bytes 2654216 | tf_op jit(solution)/shard_map/ppermute | solution.py:56
  16.5 47.0 %collective-permute-start.13 = (bf16[72,6272]{1,0:T(8,128)(2,1)}, bf16[72,6272]{1,0:T(8,128)(2,1)S(1)}, u32[]{:S(2)}, u32[]{:S(2)}) collective-permute-start(bf16[72,6272]{1,0:T(8,128)(2,1)} %get-tuple-element.159), channel_id=1, source_target_pairs={{0,4},{1,5},{2,6},{3,7},{4,0},{5,1},{6,2},{7,3},{8,12},{9,13},{10,... | collective-permute-start | bytes 2709512 | tf_op jit(solution)/shard_map/ppermute | solution.py:56
  19.2 44.4 %collective-permute-start.14 = (bf16[72,6272]{1,0:T(8,128)(2,1)}, bf16[72,6272]{1,0:T(8,128)(2,1)S(1)}, u32[]{:S(2)}, u32[]{:S(2)}) collective-permute-start(bf16[72,6272]{1,0:T(8,128)(2,1)} %get-tuple-element.160), channel_id=1, source_target_pairs={{0,8},{1,9},{2,10},{3,11},{4,12},{5,13},{6,14},{7,15},{8,0},{9,1},... | collective-permute-start | bytes 2709512 | tf_op jit(solution)/shard_map/ppermute | solution.py:56
  21.8 22.0 %collective-permute-start.10 = (bf16[192,2304]{1,0:T(8,128)(2,1)}, bf16[192,2304]{1,0:T(8,128)(2,1)}, u32[]{:S(2)}, u32[]{:S(2)}) collective-permute-start(bf16[192,2304]{1,0:T(8,128)(2,1)} %get-tuple-element.155), channel_id=1, source_target_pairs={{0,2},{1,3},{2,0},{3,1},{4,6},{5,7},{6,4},{7,5},{8,10},{9,11},{10,... | collective-permute-start | bytes 2654216 | tf_op jit(solution)/shard_map/ppermute | solution.py:466
  23.3 22.9 %collective-permute-start.11 = (bf16[192,2304]{1,0:T(8,128)(2,1)}, bf16[192,2304]{1,0:T(8,128)(2,1)}, u32[]{:S(2)}, u32[]{:S(2)}) collective-permute-start(bf16[192,2304]{1,0:T(8,128)(2,1)} %get-tuple-element.156), channel_id=1, source_target_pairs={{0,16},{1,17},{2,18},{3,19},{4,20},{5,21},{6,22},{7,23},{8,24},{9,... | collective-permute-start | bytes 2654216 | tf_op jit(solution)/shard_map/ppermute | solution.py:466
  25.8 37.8 %collective-permute-start.12 = (bf16[192,2304]{1,0:T(8,128)(2,1)}, bf16[192,2304]{1,0:T(8,128)(2,1)S(1)}, u32[]{:S(2)}, u32[]{:S(2)}) collective-permute-start(bf16[192,2304]{1,0:T(8,128)(2,1)} %get-tuple-element.157), channel_id=1, source_target_pairs={{0,18},{1,19},{2,16},{3,17},{4,22},{5,23},{6,20},{7,21},{8,26},{9,... | collective-permute-start | bytes 2654216 | tf_op jit(solution)/shard_map/ppermute | solution.py:466
  63.6 16.6 %collective-permute-start.20 = (bf16[48,6272]{1,0:T(8,128)(2,1)S(1)}, bf16[48,6272]{1,0:T(8,128)(2,1)S(1)}, u32[]{:S(2)}, u32[]{:S(2)}) collective-permute-start(bf16[48,6272]{1,0:T(8,128)(2,1)S(1)} %slice.72), channel_id=1, source_target_pairs={{0,2},{1,3},{2,0},{3,1},{4,6},{5,7},{6,4},{7,5},{8,10},{9,11},{10,... | collective-permute-start | bytes 1806344 | tf_op jit(solution)/shard_map/ppermute | solution.py:56
  65.2 5.0 %collective-permute-start.15 = (bf16[192,2304]{1,0:T(8,128)(2,1)}, bf16[192,2304]{1,0:T(8,128)(2,1)S(1)}, u32[]{:S(2)}, u32[]{:S(2)}) collective-permute-start(bf16[192,2304]{1,0:T(8,128)(2,1)} %collective-permute-done.10), channel_id=1, source_target_pairs={{0,1},{1,0},{2,3},{3,2},{4,5},{5,4},{6,7},{7,6},{8,9},{9,8},{10,11... | collective-permute-start | bytes 2654216 | tf_op jit(solution)/shard_map/ppermute | solution.py:56
  65.2 6.3 %collective-permute-start.16 = (bf16[192,2304]{1,0:T(8,128)(2,1)}, bf16[192,2304]{1,0:T(8,128)(2,1)S(1)}, u32[]{:S(2)}, u32[]{:S(2)}) collective-permute-start(bf16[192,2304]{1,0:T(8,128)(2,1)} %collective-permute-done.11), channel_id=1, source_target_pairs={{0,1},{1,0},{2,3},{3,2},{4,5},{5,4},{6,7},{7,6},{8,9},{9,8},{10,11... | collective-permute-start | bytes 2654216 | tf_op jit(solution)/shard_map/ppermute | solution.py:56
  65.7 6.4 %collective-permute-start.17 = (bf16[192,2304]{1,0:T(8,128)(2,1)S(1)}, bf16[192,2304]{1,0:T(8,128)(2,1)S(1)}, u32[]{:S(2)}, u32[]{:S(2)}) collective-permute-start(bf16[192,2304]{1,0:T(8,128)(2,1)S(1)} %collective-permute-done.12), channel_id=1, source_target_pairs={{0,1},{1,0},{2,3},{3,2},{4,5},{5,4},{6,7},{7,6},{8,9},{9,8},{10,11... | collective-permute-start | bytes 2654216 | tf_op jit(solution)/shard_map/ppermute | solution.py:56
  69.6 21.2 %collective-permute-start.19 = (bf16[48,6272]{1,0:T(8,128)(2,1)S(1)}, bf16[48,6272]{1,0:T(8,128)(2,1)S(1)}, u32[]{:S(2)}, u32[]{:S(2)}) collective-permute-start(bf16[48,6272]{1,0:T(8,128)(2,1)S(1)} %copy-done.2), channel_id=1, source_target_pairs={{0,2},{1,3},{2,0},{3,1},{4,6},{5,7},{6,4},{7,5},{8,10},{9,11},{10,... | collective-permute-start | bytes 1806344 | tf_op jit(solution)/shard_map/ppermute | solution.py:56
  70.8 20.9 %collective-permute-start.18 = (bf16[48,6272]{1,0:T(8,128)(2,1)S(1)}, bf16[48,6272]{1,0:T(8,128)(2,1)}, u32[]{:S(2)}, u32[]{:S(2)}) collective-permute-start(bf16[48,6272]{1,0:T(8,128)(2,1)S(1)} %copy-done.32), channel_id=1, source_target_pairs={{0,12},{1,13},{2,14},{3,15},{4,8},{5,9},{6,10},{7,11},{8,4},{9,5},... | collective-permute-start | bytes 1806344 | tf_op jit(solution)/shard_map/ppermute | solution.py:56
  72.1 32.6 %copy-start.31 = (f32[1,384]{1,0:T(1,128)S(1)}, f32[1,384]{1,0:T(1,128)}, u32[]{:S(2)}) copy-start(f32[1,384]{1,0:T(1,128)} %get-tuple-element.182) | copy-start | bytes 4612
  72.7 29.2 %copy-start.24 = (f32[1280,512]{1,0:T(8,128)}, f32[1280,512]{1,0:T(8,128)S(1)}, u32[]{:S(2)}) copy-start(f32[1280,512]{1,0:T(8,128)S(1)} %convolution_add_fusion.5) | copy-start | bytes 7864324
  92.6 24.4 %collective-permute-start.21 = (bf16[640,512]{1,0:T(8,128)(2,1)}, bf16[640,512]{1,0:T(8,128)(2,1)}, u32[]{:S(2)}, u32[]{:S(2)}) collective-permute-start(bf16[640,512]{1,0:T(8,128)(2,1)} %dynamic-slice_convert_fusion.2), channel_id=1, source_target_pairs={{0,4},{1,5},{2,6},{3,7},{4,0},{5,1},{6,2},{7,3},{8,12},{9,13},{10,... | collective-permute-start | bytes 1966088 | tf_op jit(solution)/shard_map/ppermute | solution.py:56
  101.9 22.1 %collective-permute-start.22 = (bf16[48,6272]{1,0:T(8,128)(2,1)}, bf16[48,6272]{1,0:T(8,128)(2,1)S(1)}, u32[]{:S(2)}, u32[]{:S(2)}) collective-permute-start(bf16[48,6272]{1,0:T(8,128)(2,1)} %slice.73), channel_id=1, source_target_pairs={{0,2},{1,3},{2,0},{3,1},{4,6},{5,7},{6,4},{7,5},{8,10},{9,11},{10,... | collective-permute-start | bytes 1806344 | tf_op jit(solution)/shard_map/ppermute | solution.py:56
  103.3 20.0 %collective-permute-start.23 = (bf16[24,6272]{1,0:T(8,128)(2,1)}, bf16[24,6272]{1,0:T(8,128)(2,1)S(1)}, u32[]{:S(2)}, u32[]{:S(2)}) collective-permute-start(bf16[24,6272]{1,0:T(8,128)(2,1)} %get-tuple-element.181), channel_id=1, source_target_pairs={{0,12},{1,13},{2,14},{3,15},{4,8},{5,9},{6,10},{7,11},{8,4},{9,5},... | collective-permute-start | bytes 903176 | tf_op jit(solution)/shard_map/ppermute | solution.py:56
  104.7 3.6 %collective-permute-start.24 = (f32[1,384]{1,0:T(1,128)S(1)}, f32[1,384]{1,0:T(1,128)S(1)}, u32[]{:S(2)}, u32[]{:S(2)}) collective-permute-start(f32[1,384]{1,0:T(1,128)S(1)} %copy-done.31), channel_id=1, source_target_pairs={{0,16},{16,0},{1,17},{17,1},{2,18},{18,2},{3,19},{19,3},{4,20},{20... | collective-permute-start | bytes 4616 | tf_op jit(solution)/shard_map/ppermute | solution.py:56
  108.3 1.2 collective-permute-start.25
  109.4 7.5 %collective-permute-start.26 = (f32[1,384]{1,0:T(1,128)S(1)}, f32[1,384]{1,0:T(1,128)S(1)}, u32[]{:S(2)}, u32[]{:S(2)}) collective-permute-start(f32[1,384]{1,0:T(1,128)S(1)} %add.299), channel_id=1, source_target_pairs={{0,2},{1,3},{2,0},{3,1},{4,6},{5,7},{6,4},{7,5},{8,10},{9,11},{10,... | collective-permute-start | bytes 4616 | tf_op jit(solution)/shard_map/ppermute | solution.py:56
  116.9 21.2 %copy-start.20 = (bf16[24,6272]{1,0:T(8,128)(2,1)S(1)}, bf16[24,6272]{1,0:T(8,128)(2,1)}, u32[]{:S(2)}) copy-start(bf16[24,6272]{1,0:T(8,128)(2,1)} %get-tuple-element.191.refs_4_) | copy-start | bytes 903172
  124.8 23.6 %collective-permute-start.28 = (bf16[48,6272]{1,0:T(8,128)(2,1)}, bf16[48,6272]{1,0:T(8,128)(2,1)S(1)}, u32[]{:S(2)}, u32[]{:S(2)}) collective-permute-start(bf16[48,6272]{1,0:T(8,128)(2,1)} %collective-permute-done.18.refs_3_), channel_id=1, source_target_pairs={{0,2},{1,3},{2,0},{3,1},{4,6},{5,7},{6,4},{7,5},{8,10},{9,11},{10,... | collective-permute-start | bytes 1806344 | tf_op jit(solution)/shard_map/ppermute | solution.py:56
  126.8 20.5 %collective-permute-start.27 = (bf16[320,512]{1,0:T(8,128)(2,1)}, bf16[320,512]{1,0:T(8,128)(2,1)}, u32[]{:S(2)}, u32[]{:S(2)}) collective-permute-start(bf16[320,512]{1,0:T(8,128)(2,1)} %dynamic-slice_convert_fusion.3), channel_id=1, source_target_pairs={{0,8},{1,9},{2,10},{3,11},{4,12},{5,13},{6,14},{7,15},{8,0},{9,1},... | collective-permute-start | bytes 983048 | tf_op jit(solution)/shard_map/ppermute | solution.py:56
  126.8 6.0 %collective-permute-start.29 = (f32[1,384]{1,0:T(1,128)S(1)}, f32[1,384]{1,0:T(1,128)S(1)}, u32[]{:S(2)}, u32[]{:S(2)}) collective-permute-start(f32[1,384]{1,0:T(1,128)S(1)} %add.300), channel_id=1, source_target_pairs={{0,4},{1,5},{2,6},{3,7},{4,0},{5,1},{6,2},{7,3},{8,12},{9,13},{10,... | collective-permute-start | bytes 4616 | tf_op jit(solution)/shard_map/ppermute | solution.py:56
  132.8 14.5 %collective-permute-start.30 = (f32[1,384]{1,0:T(1,128)S(1)}, f32[1,384]{1,0:T(1,128)S(1)}, u32[]{:S(2)}, u32[]{:S(2)}) collective-permute-start(f32[1,384]{1,0:T(1,128)S(1)} %add.304), channel_id=1, source_target_pairs={{0,8},{1,9},{2,10},{3,11},{4,12},{5,13},{6,14},{7,15},{8,0},{9,1},... | collective-permute-start | bytes 4616 | tf_op jit(solution)/shard_map/ppermute | solution.py:56
  149.3 20.7 %collective-permute-start.33 = (bf16[432,6272]{1,0:T(8,128)(2,1)}, bf16[432,6272]{1,0:T(8,128)(2,1)}, u32[]{:S(2)}, u32[]{:S(2)}) collective-permute-start(bf16[432,6272]{1,0:T(8,128)(2,1)} %copy-done), channel_id=1, source_target_pairs={{0,1},{1,0},{2,3},{3,2},{4,5},{5,4},{6,7},{7,6},{8,9},{9,8},{10,11... | collective-permute-start | bytes 16257032 | tf_op jit(solution)/shard_map/ppermute | solution.py:56
  150.2 19.8 %collective-permute-start.34 = (bf16[48,6272]{1,0:T(8,128)(2,1)S(1)}, bf16[48,6272]{1,0:T(8,128)(2,1)S(1)}, u32[]{:S(2)}, u32[]{:S(2)}) collective-permute-start(bf16[48,6272]{1,0:T(8,128)(2,1)S(1)} %collective-permute-done.28.refs_1_), channel_id=1, source_target_pairs={{0,1},{1,0},{2,3},{3,2},{4,5},{5,4},{6,7},{7,6},{8,9},{9,8},{10,11... | collective-permute-start | bytes 1806344 | tf_op jit(solution)/shard_map/ppermute | solution.py:56
  151.9 7.1 %collective-permute-start.35 = (f32[320]{0:T(512)S(1)}, f32[320]{0:T(512)S(1)}, u32[]{:S(2)}, u32[]{:S(2)}) collective-permute-start(f32[320]{0:T(512)S(1)} %dynamic-slice_divide_fusion), channel_id=1, source_target_pairs={{0,1},{1,0},{2,3},{3,2},{4,5},{5,4},{6,7},{7,6},{8,9},{9,8},{10,11... | collective-permute-start | bytes 3848 | tf_op jit(solution)/shard_map/ppermute | solution.py:56
  152.1 10.6 %collective-permute-start.32 = (bf16[320,512]{1,0:T(8,128)(2,1)S(1)}, bf16[320,512]{1,0:T(8,128)(2,1)S(1)}, u32[]{:S(2)}, u32[]{:S(2)}) collective-permute-start(bf16[320,512]{1,0:T(8,128)(2,1)S(1)} %copy.19.refs_0_), channel_id=1, source_target_pairs={{0,2},{1,3},{2,0},{3,1},{4,6},{5,7},{6,4},{7,5},{8,10},{9,11},{10,... | collective-permute-start | bytes 983048 | tf_op jit(solution)/shard_map/ppermute | solution.py:56
  153.2 16.8 %collective-permute-start.31 = (bf16[320,512]{1,0:T(8,128)(2,1)S(1)}, bf16[320,512]{1,0:T(8,128)(2,1)S(1)}, u32[]{:S(2)}, u32[]{:S(2)}) collective-permute-start(bf16[320,512]{1,0:T(8,128)(2,1)S(1)} %copy.19.refs_0_), channel_id=1, source_target_pairs={{0,8},{1,9},{2,10},{3,11},{4,12},{5,13},{6,14},{7,15},{8,0},{9,1},... | collective-permute-start | bytes 983048 | tf_op jit(solution)/shard_map/ppermute | solution.py:56
  159.1 3.6 %collective-permute-start.36 = (f32[1,320]{1,0:T(1,128)S(1)}, f32[1,320]{1,0:T(1,128)S(1)}, u32[]{:S(2)}, u32[]{:S(2)}) collective-permute-start(f32[1,320]{1,0:T(1,128)S(1)} %broadcast_in_dim.158), channel_id=1, source_target_pairs={{0,16},{16,0},{1,17},{17,1},{2,18},{18,2},{3,19},{19,3},{4,20},{20... | collective-permute-start | bytes 3848 | tf_op jit(solution)/shard_map/ppermute | solution.py:56
  162.8 11.2 %copy-start.12 = (bf16[320,512]{1,0:T(8,128)(2,1)}, bf16[320,512]{1,0:T(8,128)(2,1)S(1)}, u32[]{:S(2)}) copy-start(bf16[320,512]{1,0:T(8,128)(2,1)S(1)} %collective-permute-done.32.refs_0_) | copy-start | bytes 983044
  170.0 19.6 %collective-permute-start.37 = (bf16[640,512]{1,0:T(8,128)(2,1)S(1)}, bf16[640,512]{1,0:T(8,128)(2,1)S(1)}, u32[]{:S(2)}, u32[]{:S(2)}) collective-permute-start(bf16[640,512]{1,0:T(8,128)(2,1)S(1)} %pad_maximum_fusion), channel_id=1, source_target_pairs={{0,4},{1,5},{2,6},{3,7},{4,0},{5,1},{6,2},{7,3},{8,12},{9,13},{10,... | collective-permute-start | bytes 1966088 | tf_op jit(solution)/shard_map/ppermute | solution.py:56
  170.2 19.5 %collective-permute-start.38 = (bf16[320,512]{1,0:T(8,128)(2,1)S(1)}, bf16[320,512]{1,0:T(8,128)(2,1)S(1)}, u32[]{:S(2)}, u32[]{:S(2)}) collective-permute-start(bf16[320,512]{1,0:T(8,128)(2,1)S(1)} %collective-permute-done.31.refs_1_), channel_id=1, source_target_pairs={{0,2},{1,3},{2,0},{3,1},{4,6},{5,7},{6,4},{7,5},{8,10},{9,11},{10,... | collective-permute-start | bytes 983048 | tf_op jit(solution)/shard_map/ppermute | solution.py:56
  171.3 18.3 %collective-permute-start.39 = (f32[2,320]{1,0:T(2,128)S(1)}, f32[2,320]{1,0:T(2,128)S(1)}, u32[]{:S(2)}, u32[]{:S(2)}) collective-permute-start(f32[2,320]{1,0:T(2,128)S(1)} %broadcast_select_fusion.4), channel_id=1, source_target_pairs={{0,8},{1,9},{2,10},{3,11},{4,12},{5,13},{6,14},{7,15},{8,0},{9,1},... | collective-permute-start | bytes 7688 | tf_op jit(solution)/shard_map/ppermute | solution.py:56
  177.6 18.4 %copy-start.30 = (s32[32,1]{0,1:T(1,128)S(1)}, s32[32,1]{0,1:T(1,128)}, u32[]{:S(2)}) copy-start(s32[32,1]{0,1:T(1,128)} %param.19) | copy-start | bytes 388
  189.7 5.8 %collective-permute-start.48 = (f32[2,2,320]{2,1,0:T(2,128)S(1)}, f32[2,2,320]{2,1,0:T(2,128)S(1)}, u32[]{:S(2)}, u32[]{:S(2)}) collective-permute-start(f32[2,2,320]{2,1,0:T(2,128)S(1)} %broadcast_select_fusion.3), channel_id=1, source_target_pairs={{0,6},{1,7},{2,4},{3,5},{4,2},{5,3},{6,0},{7,1},{8,14},{9,15},{10,... | collective-permute-start | bytes 15368 | tf_op jit(solution)/shard_map/ppermute | solution.py:56
  190.2 23.9 %collective-permute-start.47 = (f32[2,2,320]{2,1,0:T(2,128)S(1)}, f32[2,2,320]{2,1,0:T(2,128)S(1)}, u32[]{:S(2)}, u32[]{:S(2)}) collective-permute-start(f32[2,2,320]{2,1,0:T(2,128)S(1)} %broadcast_select_fusion.3), channel_id=1, source_target_pairs={{0,2},{1,3},{2,0},{3,1},{4,6},{5,7},{6,4},{7,5},{8,10},{9,11},{10,... | collective-permute-start | bytes 15368 | tf_op jit(solution)/shard_map/ppermute | solution.py:56
  191.3 23.2 %collective-permute-start.46 = (f32[2,2,320]{2,1,0:T(2,128)S(1)}, f32[2,2,320]{2,1,0:T(2,128)S(1)}, u32[]{:S(2)}, u32[]{:S(2)}) collective-permute-start(f32[2,2,320]{2,1,0:T(2,128)S(1)} %broadcast_select_fusion.3), channel_id=1, source_target_pairs={{0,4},{1,5},{2,6},{3,7},{4,0},{5,1},{6,2},{7,3},{8,12},{9,13},{10,... | collective-permute-start | bytes 15368 | tf_op jit(solution)/shard_map/ppermute | solution.py:56
  193.3 28.1 %collective-permute-start.43 = (bf16[640,512]{1,0:T(8,128)(2,1)S(1)}, bf16[640,512]{1,0:T(8,128)(2,1)S(1)}, u32[]{:S(2)}, u32[]{:S(2)}) collective-permute-start(bf16[640,512]{1,0:T(8,128)(2,1)S(1)} %collective-permute-done.37.refs_2_), channel_id=1, source_target_pairs={{0,2},{1,3},{2,0},{3,1},{4,6},{5,7},{6,4},{7,5},{8,10},{9,11},{10,... | collective-permute-start | bytes 1966088 | tf_op jit(solution)/shard_map/ppermute | solution.py:56
  194.2 21.6 %collective-permute-start.42 = (bf16[640,512]{1,0:T(8,128)(2,1)S(1)}, bf16[640,512]{1,0:T(8,128)(2,1)}, u32[]{:S(2)}, u32[]{:S(2)}) collective-permute-start(bf16[640,512]{1,0:T(8,128)(2,1)S(1)} %collective-permute-done.37.refs_2_), channel_id=1, source_target_pairs={{0,1},{1,0},{2,3},{3,2},{4,5},{5,4},{6,7},{7,6},{8,9},{9,8},{10,11... | collective-permute-start | bytes 1966088 | tf_op jit(solution)/shard_map/ppermute | solution.py:56
  195.4 19.3 %collective-permute-start.40 = (bf16[320,512]{1,0:T(8,128)(2,1)S(1)}, bf16[320,512]{1,0:T(8,128)(2,1)S(1)}, u32[]{:S(2)}, u32[]{:S(2)}) collective-permute-start(bf16[320,512]{1,0:T(8,128)(2,1)S(1)} %copy.19.refs_0_), channel_id=1, source_target_pairs={{0,1},{1,0},{2,3},{3,2},{4,5},{5,4},{6,7},{7,6},{8,9},{9,8},{10,11... | collective-permute-start | bytes 983048 | tf_op jit(solution)/shard_map/ppermute | solution.py:56
  196.0 18.4 %copy-start.13 = (bf16[320,512]{1,0:T(8,128)(2,1)S(1)}, bf16[320,512]{1,0:T(8,128)(2,1)}, u32[]{:S(2)}) copy-start(bf16[320,512]{1,0:T(8,128)(2,1)} %copy-done.12) | copy-start | bytes 983044
  196.0 18.7 %copy-start.16 = (bf16[320,512]{1,0:T(8,128)(2,1)S(1)}, bf16[320,512]{1,0:T(8,128)(2,1)}, u32[]{:S(2)}) copy-start(bf16[320,512]{1,0:T(8,128)(2,1)} %copy-done.15) | copy-start | bytes 983044
  214.1 1.7 collective-permute-start.41
  214.4 6.2 %collective-permute-start.44 = (bf16[320,512]{1,0:T(8,128)(2,1)S(1)}, bf16[320,512]{1,0:T(8,128)(2,1)S(1)}, u32[]{:S(2)}, u32[]{:S(2)}) collective-permute-start(bf16[320,512]{1,0:T(8,128)(2,1)S(1)} %copy-done.13), channel_id=1, source_target_pairs={{0,1},{1,0},{2,3},{3,2},{4,5},{5,4},{6,7},{7,6},{8,9},{9,8},{10,11... | collective-permute-start | bytes 983048 | tf_op jit(solution)/shard_map/ppermute | solution.py:56
  214.7 5.9 %collective-permute-start.45 = (bf16[320,512]{1,0:T(8,128)(2,1)S(1)}, bf16[320,512]{1,0:T(8,128)(2,1)S(1)}, u32[]{:S(2)}, u32[]{:S(2)}) collective-permute-start(bf16[320,512]{1,0:T(8,128)(2,1)S(1)} %copy-done.16), channel_id=1, source_target_pairs={{0,1},{1,0},{2,3},{3,2},{4,5},{5,4},{6,7},{7,6},{8,9},{9,8},{10,11... | collective-permute-start | bytes 983048 | tf_op jit(solution)/shard_map/ppermute | solution.py:56
  221.4 2.1 collective-permute-start.49
  (25 other events, 59.8 us)

commit v5 on v4

--- a/solution.py
+++ b/solution.py
@@ -15,7 +15,9 @@
 TAGS = 128
 STRIP = 512
 UNROLL = 5
-KEYS_MIB, STACK_MIB, PLACE_MIB, SLOTS_MIB = 56, 20, 36, 44
+EXTRA = 16
+CHUNK = 64
+KEYS_MIB, PRODUCTS_MIB, FINISH_MIB, STACK_MIB, PLACE_MIB, SLOTS_MIB = 56, 20, 8, 20, 36, 44
 
 
 epsilon = 1e-06
@@ -91,11 +93,11 @@
     main = outs[0].shape[0]
     planes, packet = plan[:2]
     packs, refs = refs[: len(pieces)], refs[len(pieces) :]
-    (keys_out, sums_out), held, (w_all, h_all, keys, sems) = refs[:2], refs[2:10], refs[10:]
+    (keys_out, sums_out), held, (w_all, h_all, keys, sums, sems) = refs[:2], refs[2:10], refs[10:]
 
     def spread(packed, first):
         for pack, (low, high) in zip(packs, pieces):
-            pack[:, first] = packed[low:high]
+            pack[: high - low, first] = packed[low:high]
 
     w_ref = sources[8]
     copies = [
@@ -131,29 +133,35 @@
     weight = token_weights(importance_ref[...], len_ref[...], version_ref[...])
     copies[0].wait()
 
-    def squares(i, total):
-        part = hidden_ref[:, strip(i)]
-        packed = jnp.dot(onehot, part, preferred_element_type=F32).astype(BF16)
-        spread(packed, strip(i))
-        x = part.astype(F32)
-        return total + jnp.sum(x * x, 1, keepdims=True)
-
-    square_sum = lax.fori_loop(
-        0, strips, squares, jnp.zeros((rows, 1), F32), unroll=UNROLL
-    )
+    sums[...] = jnp.zeros_like(sums)
+    spans = [slice(k, k + STRIP) for k in range(0, features, STRIP)]
+    for span in spans:
+        packed = jnp.dot(onehot, hidden_ref[:, span], preferred_element_type=F32).astype(BF16)
+        spread(packed, span)
+
+        def add(at):
+            x = hidden_ref[at, span].astype(F32)
+            sums[at, :] += lane_sums(x * x)
+
+        over_chunks(rows, add)
     packed = jnp.dot(onehot, tags, preferred_element_type=F32).astype(BF16)
     spread(packed, slice(features, features + TAGS))
-    inv = lax.rsqrt(square_sum / features + epsilon)
-    keys[...] = jnp.zeros_like(keys)
-
-    def project(i, carry):
-        h = (hidden_ref[:, strip(i)].astype(F32) * inv * gain_ref[:, strip(i)]).astype(BF16)
-        h_all[:, strip(i)] = jnp.dot(squeeze, h, preferred_element_type=F32).astype(BF16)
+    inv = lax.rsqrt(jnp.sum(sums[...], 1, keepdims=True) / features + epsilon)
+    sums[...] = jnp.broadcast_to(inv, sums.shape)
+    for i, span in enumerate(spans):
+        gain = gain_ref[:, span]
+
+        def scale(at):
+            by = jnp.concatenate([sums[at, :]] * (STRIP // 128), 1)
+            hidden_ref[at, span] = (hidden_ref[at, span].astype(F32) * by * gain).astype(BF16)
+
+        over_chunks(rows, scale)
+        h = hidden_ref[:, span]
+        h_all[:, span] = jnp.dot(squeeze, h, preferred_element_type=F32).astype(BF16)
         fetch(i).wait()
-        keys[...] += jnp.dot(h, w_all[strip(i), :], preferred_element_type=F32)
-        return carry
-
-    lax.fori_loop(0, strips, project, 0, unroll=UNROLL)
+        product = jnp.dot(h, w_all[span, :], preferred_element_type=F32)
+        keys[...] = keys[...] + product if i else product
+
     width = outs[0].shape[1] - keys.shape[1]
     for k in range(blocks):
         columns = pl.ds(pl.multiple_of(index_ref[k] * width, width), width)
@@ -181,6 +189,18 @@
         rests[k][:, width:] = packed[main:]
     packed = jnp.dot(onehot, keys_out[...], preferred_element_type=F32).astype(BF16)
     spread(packed, slice(features + TAGS, features + TAGS + keys.shape[1]))
+    value = kgain
+    line = lax.broadcasted_iota(jnp.int32, (EXTRA, head // 2), 0)
+    split = jnp.where(line == 6, over, jnp.where(line == 7, many, 0.0))
+    for i in range(3):
+        term = value.astype(BF16).astype(F32)
+        value = value - term
+        split = jnp.where(line == 2 * i, term[:, : head // 2], split)
+        split = jnp.where(line == 2 * i + 1, term[:, head // 2 :], split)
+    split = jnp.concatenate([jnp.zeros((EXTRA, TAGS - head // 2), F32), split], 1)
+    for pack in packs[2:]:
+        beside = pack[:EXTRA, features : features + TAGS].astype(F32) + split
+        pack[:EXTRA, features : features + TAGS] = beside.astype(BF16)
 
 
 def packet_plan(learn, len_row, dest_row, rows, main, planes, packet, passed_on, capacity):
@@ -229,6 +249,53 @@
     return position, tags.astype(F32).astype(BF16), over, order, many
 
 
+def products_kernel(count, core_ref, *refs):
+    sources, (out_ref, parts, sems) = refs[:count], refs[count:]
+    width, half = out_ref.shape
+    tall = width // 5
+    keys = pl.ds(pl.multiple_of(width + core_ref[0] * half, half), half)
+    copies = [
+        pltpu.make_async_copy(source, parts.at[k], sems.at[k]) for k, source in enumerate(sources)
+    ]
+    for copy in copies:
+        copy.start()
+    for k, copy in enumerate(copies):
+        copy.wait()
+
+        def block(i, carry):
+            rows = pl.ds(pl.multiple_of(i * tall, tall), tall)
+            product = lax.dot_general(
+                parts[k, :, rows],
+                parts[k, :, keys],
+                (((0,), (0,)), ((), ())),
+                preferred_element_type=F32,
+            )
+            out_ref[rows, :] = product + out_ref[rows, :] if k else product
+            return carry
+
+        lax.fori_loop(0, 5, block, 0, unroll=True)
+
+
+def finish_kernel(
+    index_ref, total_ref, w_ref, gain_ref, block_out, gains_out, w_part, gain, sems
+):
+    tall, half = total_ref.shape
+    rows = pl.ds(pl.multiple_of(index_ref[0] * tall, tall), tall)
+    columns = pl.ds(pl.multiple_of(index_ref[1] * half, half), half)
+    fetch_w = pltpu.make_async_copy(w_ref.at[rows, columns], w_part, sems.at[0])
+    fetch_gain = pltpu.make_async_copy(gain_ref, gain, sems.at[1])
+    fetch_w.start()
+    fetch_gain.start()
+    total = total_ref[...]
+    block_out[...] = total.astype(BF16)
+    fetch_gain.wait()
+    fetch_w.wait()
+    sums = jnp.sum(w_part[...].astype(F32) * total, 1, keepdims=True)
+    shape = (tall, tall)
+    same = lax.broadcasted_iota(jnp.int32, shape, 0) == lax.broadcasted_iota(jnp.int32, shape, 1)
+    gains_out[...] = jnp.sum(jnp.where(same, sums, 0.0), 0, keepdims=True) / gain[...]
+
+
 def stack_kernel(*refs):
     out, used = refs[-1], 0
     for part in refs[:-1]:
@@ -236,79 +303,104 @@
         used += part.shape[0]
 
 
-def place_kernel(me_ref, *refs):
-    sources, (rows_out, keys_out, held, chosen, sems) = refs[:4], refs[4:]
+def place_kernel(count, me_ref, *refs):
+    sources, (rows_out, keys_out, held, chosen, sems) = refs[:count], refs[count:]
     slots, features = rows_out.shape
-    copies, used = [], 0
-    for i, source in enumerate(sources):
-        place = held.at[pl.ds(used, source.shape[0])]
-        copies.append(pltpu.make_async_copy(source, place, sems.at[i]))
-        copies[-1].start()
-        used += source.shape[0]
+    width = held.shape[1]
+    tag = slice(features, features + TAGS)
+    spans = [tag] + [slice(k, k + STRIP) for k in range(0, features, STRIP)]
+    spans += [slice(features + TAGS, width)]
+    copies = []
+    for k, span in enumerate(spans):
+        used = 0
+        copies.append([])
+        for i, source in enumerate(sources):
+            place = held.at[pl.ds(used, source.shape[0]), span]
+            copies[k].append(pltpu.make_async_copy(source.at[:, span], place, sems.at[k, i]))
+            copies[k][-1].start()
+            used += source.shape[0]
     if used < held.shape[0]:
-        held[used:, :] = jnp.zeros((held.shape[0] - used, held.shape[1]), BF16)
-    for copy in copies:
+        held[used:, :] = jnp.zeros((held.shape[0] - used, width), BF16)
+    for copy in copies[0]:
         copy.wait()
-    tags = held[:, features : features + TAGS].astype(F32).T.astype(jnp.int32)
+    tags = held[:, tag].astype(F32).T.astype(jnp.int32)
     target = jnp.where(tags[0:1] == me_ref[0] + 1, tags[1:2] * TILE + tags[2:3], -1)
     places = lax.broadcasted_iota(jnp.int32, (slots, held.shape[0]), 0)
     chosen[...] = (places == target).astype(F32).astype(BF16)
-
-    def pick(columns):
-        return jnp.dot(
-            chosen[...], held[:, columns], preferred_element_type=F32
-        ).astype(BF16)
-
-    def put(i, carry):
-        strip = pl.ds(pl.multiple_of(i * STRIP, STRIP), STRIP)
-        rows_out[:, strip] = pick(strip)
-        return carry
-
-    lax.fori_loop(0, features // STRIP, put, 0, unroll=UNROLL)
-    keys_out[...] = pick(slice(features + TAGS, features + TAGS + keys_out.shape[1]))
-
-
-def slots_kernel(over_ref, rows_ref, keys_ref, w_ref, gain_ref, out_ref, w_all, grad, sems):
-    slots, features = out_ref.shape
-    strips = features // STRIP
-
-    def strip(i):
-        return pl.ds(pl.multiple_of(i * STRIP, STRIP), STRIP)
-
-    def fetch(i):
-        return pltpu.make_async_copy(w_ref.at[strip(i)], w_all.at[strip(i)], sems.at[i])
-
-    for i in range(strips):
-        fetch(i).start()
-
-    def back(i, total):
-        rows = rows_ref[:, strip(i)].astype(F32)
-        fetch(i).wait()
-        g = gain_ref[:, strip(i)] * lax.dot_general(
-            keys_ref[...], w_all[strip(i), :], (((1,), (1,)), ((), ())), preferred_element_type=F32
+    for k, span in enumerate(spans[1:], 1):
+        for copy in copies[k]:
+            copy.wait()
+        rows = jnp.dot(chosen[...], held[:, span], preferred_element_type=F32).astype(BF16)
+        if k + 1 < len(spans):
+            rows_out[:, span] = rows
+        else:
+            keys_out[...] = rows
+
+
+def lane_sums(x):
+    total = x[:, :128]
+    for k in range(1, x.shape[1] // 128):
+        total = total + x[:, k * 128 : (k + 1) * 128]
+    return total
+
+
+def over_chunks(rows, work):
+    lax.fori_loop(
+        0,
+        rows // CHUNK,
+        lambda j, carry: work(pl.ds(pl.multiple_of(j * CHUNK, CHUNK), CHUNK)) or carry,
+        0,
+        unroll=True,
+    )
+
+
+def slots_kernel(
+    over_ref, rows_ref, keys_ref, w_ref, gain_ref, out_ref, w_all, grad, rows_all, sums, sems
+):
+    slots, features = grad.shape
+    strips = [slice(k, k + STRIP) for k in range(0, features, STRIP)]
+    fetches, loads, stores = [], [], []
+    for i, strip in enumerate(strips):
+        fetches.append(pltpu.make_async_copy(w_ref.at[strip], w_all.at[strip], sems.at[0, i]))
+        here = rows_all.at[:, strip]
+        loads.append(pltpu.make_async_copy(rows_ref.at[:, strip], here, sems.at[1, i]))
+        stores.append(pltpu.make_async_copy(here, out_ref.at[:, strip], sems.at[2, i]))
+        fetches[i].start()
+        loads[i].start()
+    sums[...] = jnp.zeros_like(sums)
+    for i, strip in enumerate(strips):
+        fetches[i].wait()
+        loads[i].wait()
+        grad[:, strip] = lax.dot_general(
+            keys_ref[...], w_all[strip, :], (((1,), (1,)), ((), ())), preferred_element_type=F32
         )
-        grad[:, strip(i)] = g
-        squares, products = total
-        return (
-            squares + jnp.sum(rows * rows, 1, keepdims=True),
-            products + jnp.sum(g * rows, 1, keepdims=True),
-        )
-
-    zero = jnp.zeros((slots, 1), F32)
-    squares, products = lax.fori_loop(0, strips, back, (zero, zero), unroll=UNROLL)
-    inv = lax.rsqrt(squares / features + epsilon)
-    mean = products * inv / features
-
-    def finish(i, carry):
-        normed = rows_ref[:, strip(i)].astype(F32) * inv
-        out_ref[:, strip(i)] = (inv * (grad[:, strip(i)] - normed * mean)).astype(BF16)
-        return carry
-
-    lax.fori_loop(0, strips, finish, 0, unroll=UNROLL)
-
-    @pl.when(over_ref[0] > 0.5)
-    def _():
-        out_ref[...] = rows_ref[...]
+        gain = gain_ref[:, strip]
+
+        def add(at):
+            rows = rows_all[at, strip].astype(F32)
+            sums[0, at, :] += lane_sums(rows * rows)
+            sums[1, at, :] += lane_sums(grad[at, strip] * gain * rows)
+
+        over_chunks(slots, add)
+    inv = lax.rsqrt(jnp.sum(sums[0], 1, keepdims=True) / features + epsilon)
+    slope = jnp.sum(sums[1], 1, keepdims=True) * inv * inv * inv / features
+    sums[0] = jnp.broadcast_to(inv, sums.shape[1:])
+    sums[1] = jnp.broadcast_to(slope, sums.shape[1:])
+    dense = over_ref[0] > 0.5
+    for i, strip in enumerate(strips):
+        gain = gain_ref[:, strip]
+
+        def finish(at):
+            first = jnp.concatenate([sums[0, at, :]] * (STRIP // 128), 1)
+            second = jnp.concatenate([sums[1, at, :]] * (STRIP // 128), 1)
+            rows = rows_all[at, strip]
+            final = first * (grad[at, strip] * gain) - rows.astype(F32) * second
+            rows_all[at, strip] = jnp.where(dense, rows, final.astype(BF16))
+
+        over_chunks(slots, finish)
+        stores[i].start()
+    for store in stores:
+        store.wait()
 
 
 def output_kernel(sizes, index_ref, *refs):
@@ -351,6 +443,9 @@
         ),
         input_output_aliases={1 + 2 * len(sizes): 0} if more else {},
         compiler_params=pltpu.CompilerParams(vmem_limit_bytes=24 << 20),
+        cost_estimate=pl.CostEstimate(
+            flops=0, bytes_accessed=12 * sum(sizes) * tall * half, transcendentals=0
+        ),
     )(index, *mine, *others, *more)
 
 
@@ -403,7 +498,7 @@
     front = packet - passed_on
     pieces = []
     for k in range(planes):
-        cuts = (0, front, packet) if k in (0, planes - 1) else (0, packet)
+        cuts = (0, front, packet) if k == 0 else (0, packet)
         pieces += [(k * packet + low, k * packet + high) for low, high in zip(cuts, cuts[1:])]
     packed_width = features + TAGS + key_count
     steps = [(step, dy) for step in range(gens) for dy in range(2)]
@@ -416,7 +511,9 @@
         ),
         out_shape=[jax.ShapeDtypeStruct((main, width + key_count), BF16)] * blocks
         + [jax.ShapeDtypeStruct((rows - main, width + key_count), BF16)] * blocks
-        + [jax.ShapeDtypeStruct((high - low, packed_width), BF16) for low, high in pieces]
+        + [
+            jax.ShapeDtypeStruct((high - low, packed_width), BF16) for low, high in pieces
+        ]
         + [
             jax.ShapeDtypeStruct((rows, key_count), BF16),
             jax.ShapeDtypeStruct((1, 3 * head), F32),
@@ -435,6 +532,7 @@
             pltpu.VMEM((features, key_count), BF16),
             pltpu.VMEM((rows, features), BF16),
             pltpu.VMEM((rows, key_count), F32),
+            pltpu.VMEM((rows, 128), F32),
             pltpu.SemaphoreType.DMA((8 + strips,)),
         ],
         compiler_params=limit(KEYS_MIB),
@@ -511,88 +609,113 @@
         held[k] = across_learn(packs[1 + k], 4 * k)
     gathered, held, packs = barrier((gathered, held, packs))
 
+    def add_rests(state):
+        parts = [rests[0]] + [gather(k, rests) for k in range(1, blocks)]
+        parts += [across_learn(part, 1) for part in parts]
+        total = pl.pallas_call(
+            functools.partial(products_kernel, len(parts)),
+            out_shape=jax.ShapeDtypeStruct((width, half), F32),
+            in_specs=[SMEM] + [ANY] * len(parts),
+            out_specs=VMEM,
+            scratch_shapes=[
+                pltpu.VMEM((len(parts), rows - main, width + key_count), BF16),
+                pltpu.SemaphoreType.DMA((len(parts),)),
+            ],
+            compiler_params=limit(PRODUCTS_MIB),
+            cost_estimate=pl.CostEstimate(flops=0, bytes_accessed=0, transcendentals=0),
+        )(core[None], *parts)
+        for bit in bits:
+            total = halve(total, bit)
+        return jnp.zeros((), F32), state[1] + total
+
     total = add_products(0.0, [operands[0], *gathered])
     held[last] = across_learn(packs[-1], 4 * last)
-    passed[0] = over_y(held[0])
-    passed[1] = over_y(held[1])
-    total, held, passed, packs = barrier((total, held, passed, packs))
-
+    for k in range(last):
+        passed[k] = over_y(held[k])
+    total, held, passed = barrier((total, held, passed))
+
+    values = [sums]
+    for k in range(1, planes):
+        beside = held[k][:8, features + TAGS - head // 2 : features + TAGS].astype(F32)
+        terms = beside[:6].reshape(3, head)
+        flags = jnp.broadcast_to(beside[6:, :1], (2, head)).reshape(2 * head)
+        values.append(jnp.concatenate([terms[0] + (terms[1] + terms[2]), flags])[None])
+    while len(values) > 1:
+        values = [a + b for a, b in zip(values[::2], values[1::2])]
+    sums = values[0]
     for n, bit in enumerate(bits):
         total = halve(total, bit)
         if n == 0:
-            held[planes + 1] = across_learn(packs[-2], 4 * last)
-            for k in range(2, last):
-                passed[k] = over_y(held[k])
+            stacked = stack(list(held.values()) + list(passed.values()))
+            passed[last] = over_y(held[last])
             sums = butterfly_sum(sums, (("gen", gens),))
             sums = butterfly_sum(sums, (("learn", 4),), learners)
+            total, passed, stacked, sums = barrier((total, passed, stacked, sums))
         if n == 1:
-            stacked = stack(list(held.values()) + list(passed.values()))
-            passed[last] = over_y(held[last])
-            for other_bit in bits:
-                sums = sums + across_learn(sums, other_bit)
-            total, passed, stacked, sums = barrier((total, passed, stacked, sums))
-        else:
-            total, passed, held, sums = barrier((total, passed, held, sums))
-
-    def add_rests(state):
-        total = add_products(0.0, [rests[0]] + [gather(k, rests) for k in range(1, blocks)])
-        for bit in bits:
-            total = halve(total, bit)
-        return jnp.zeros((), F32), state[1] + total
-
+            stacks = [stacked, passed[last]]
+            stacks += [across_learn(part, 1) for part in stacks]
+            total, stacks, sums = barrier((total, stacks, sums))
     _, total = lax.while_loop(lambda state: state[0] > 0.5, add_rests, (sums[0, -1], total))
 
     tall = total.shape[0]
-    first = (gen * 2 + across) * width
-    for n, bit in enumerate(bits):
-        first = first + ((learn // bit) % 2) * (width >> (n + 1))
-    w_part = lax.dynamic_slice(w_key, (first, core * half), (tall, half)).astype(F32)
-    gains = jnp.sum(w_part * total, 1) / lax.dynamic_slice_in_dim(in_gain, first, tall)
-
-    parts, y_parts, offsets = [total.astype(BF16)], [], [0]
+    z_place = sum(((learn // bit) % 2) * (planes >> (n + 1)) for n, bit in enumerate(bits))
+    first = (gen * 2 + across) * planes + z_place
+    block, gains = pl.pallas_call(
+        finish_kernel,
+        out_shape=[
+            jax.ShapeDtypeStruct((tall, half), BF16),
+            jax.ShapeDtypeStruct((1, tall), F32),
+        ],
+        in_specs=[SMEM, VMEM, ANY, ANY],
+        out_specs=[VMEM] * 2,
+        scratch_shapes=[
+            pltpu.VMEM((tall, half), BF16),
+            pltpu.VMEM((1, tall), F32),
+            pltpu.SemaphoreType.DMA((2,)),
+        ],
+        compiler_params=limit(FINISH_MIB),
+    )(
+        jnp.stack([first, core]),
+        total,
+        w_key,
+        lax.dynamic_slice_in_dim(in_gain, first * tall, tall)[None],
+    )
+
+    parts, y_parts, offsets = [block], [], [0]
+    kgain_grad = sums[0, :head]
+    place = -(-sum(part.shape[0] for part in stacks) // 128) * 128
+    rows_placed, keys_placed = pl.pallas_call(
+        functools.partial(place_kernel, len(stacks)),
+        out_shape=[
+            jax.ShapeDtypeStruct((SLOTS * TILE, features), BF16),
+            jax.ShapeDtypeStruct((SLOTS * TILE, key_count), BF16),
+        ],
+        in_specs=[SMEM] + [ANY] * len(stacks),
+        out_specs=[VMEM] * 2,
+        scratch_shapes=[
+            pltpu.VMEM((place, packed_width), BF16),
+            pltpu.VMEM((SLOTS * TILE, place), BF16),
+            pltpu.SemaphoreType.DMA((strips + 2, len(stacks))),
+        ],
+        compiler_params=limit(PLACE_MIB),
+    )(learn[None], *stacks)
     for n, bit in enumerate(reversed(bits)):
         block = parts[0] if n == 0 else jnp.concatenate(parts, 0)
         received = across_learn(block, bit)
         y_parts.append(across_learn(parts[-1], 2))
+        upper = (learn // bit) % 2
+        if n + 1 == len(bits):
+            near = [across_learn(gains, far) for far in (bit, 2, bit + 2)]
+            gains = join_at(join(gains, near[0], upper), join(near[1], near[2], upper), across, 0)
+        else:
+            gains = join(gains, across_learn(gains, bit), upper)
         if n == 0:
-            other_stacked = across_learn(stacked, 1)
-            other_passed = across_learn(passed[last], 1)
-            gains = gains + across_learn(gains, 1)
-            gains = gains[None]
-            step = 1
-            while step < gens:
-                gains = join(gains, swap(gains, "gen", gens, step), (gen // step) % 2)
-                step *= 2
-            received, y_parts, other_stacked, other_passed, gains = barrier(
-                (received, y_parts, other_stacked, other_passed, gains)
+            received, y_parts, gains, rows_placed, keys_placed = barrier(
+                (received, y_parts, gains, rows_placed, keys_placed)
             )
         parts = parts + [received]
         weight = planes >> (bits.index(bit) + 1)
         offsets = offsets + [o ^ weight for o in offsets]
-        if n:
-            wide = bits[-n]
-            gains = join_at(gains, across_learn(gains, wide), (learn // wide) % 2, 1)
-    place = -(-2 * (stacked.shape[0] + passed_on) // 128) * 128
-    rows_placed, keys_placed = pl.pallas_call(
-        place_kernel,
-        out_shape=[
-            jax.ShapeDtypeStruct((SLOTS * TILE, features), BF16),
-            jax.ShapeDtypeStruct((SLOTS * TILE, key_count), BF16),
-        ],
-        in_specs=[SMEM] + [ANY] * 4,
-        out_specs=[VMEM] * 2,
-        scratch_shapes=[
-            pltpu.VMEM((place, packed_width), BF16),
-            pltpu.VMEM((SLOTS * TILE, place), BF16),
-            pltpu.SemaphoreType.DMA((4,)),
-        ],
-        compiler_params=limit(PLACE_MIB),
-    )(learn[None], stacked, passed[last], other_stacked, other_passed)
-    parts, y_parts, gains, sums, rows_placed, keys_placed = barrier(
-        (parts, y_parts, gains, sums, rows_placed, keys_placed)
-    )
-
-    y_parts.append(across_learn(parts[-1], 2))
     _, rows_placed = lax.while_loop(
         lambda state: state[0] > 0.5,
         lambda state: (
@@ -604,41 +727,50 @@
     grad_slots = pl.pallas_call(
         slots_kernel,
         out_shape=jax.ShapeDtypeStruct((SLOTS * TILE, features), BF16),
-        in_specs=[SMEM, VMEM, VMEM, ANY, VMEM],
-        out_specs=VMEM,
+        in_specs=[SMEM, ANY, VMEM, ANY, VMEM],
+        out_specs=ANY,
         scratch_shapes=[
             pltpu.VMEM((features, key_count), BF16),
             pltpu.VMEM((SLOTS * TILE, features), F32),
-            pltpu.SemaphoreType.DMA((strips,)),
+            pltpu.VMEM((SLOTS * TILE, features), BF16),
+            pltpu.VMEM((2, SLOTS * TILE, 128), F32),
+            pltpu.SemaphoreType.DMA((3, strips)),
         ],
         compiler_params=limit(SLOTS_MIB),
     )(sums[0, head : head + 1], rows_placed, keys_placed, w_key, in_gain_row)
+    parts, y_parts, gains, grad_slots, kgain_grad = barrier(
+        (parts, y_parts, gains, grad_slots, kgain_grad)
+    )
+
+    y_parts.append(across_learn(parts[-1], 2))
     core_parts = [across_learn(part, 1) for part in parts]
     core_y = [across_learn(part, 1) for part in y_parts[:-1]]
-    first = sum(((learn // bit) % 2) * (planes >> (n + 1)) for n, bit in enumerate(bits))
-    first = first ^ jnp.asarray(offsets, jnp.int32)
+    first = z_place ^ jnp.asarray(offsets, jnp.int32)
     w_rows = 2 * width
+    done = sum(part.shape[0] for part in y_parts[:-1]) // tall
+    own_first, other_first = across * planes + first, (1 - across) * planes + first
     w_grad = lay_out(
-        jnp.concatenate([across * planes + first, core[None]]), parts, core_parts, tall, w_rows
-    )
-    near = [across_learn(gains, bit) for bit in (bits[0], 2, bits[0] + 2)]
-    upper = (learn // bits[0]) % 2
-    gains = join_at(
-        join_at(gains, near[0], upper, 1), join_at(near[1], near[2], upper, 1), across, 1
-    )
-    w_grad, y_parts, core_y, gains, sums, grad_slots = barrier(
-        (w_grad, y_parts, core_y, gains, sums, grad_slots)
-    )
-    core_y.append(across_learn(y_parts[-1], 1))
+        jnp.concatenate([own_first, other_first[:done], core[None]]),
+        parts + y_parts[:-1],
+        core_parts + core_y,
+        tall,
+        w_rows,
+    )
+    gains = gains + across_learn(gains, 1)
+    step = 1
+    while step < gens:
+        gains = join(gains, swap(gains, "gen", gens, step), (gen // step) % 2)
+        step *= 2
+    w_grad, y_parts, gains = barrier((w_grad, y_parts, gains))
     w_grad = lay_out(
-        jnp.concatenate([(1 - across) * planes + first, core[None]]),
-        y_parts,
-        core_y,
+        jnp.concatenate([other_first[done:], core[None]]),
+        y_parts[-1:],
+        [across_learn(y_parts[-1], 1)],
         tall,
         w_rows,
         w_grad,
     )
-    return (grad_slots, w_grad, gains.reshape(-1), sums[0, :head])
+    return (grad_slots, w_grad, gains.reshape(-1), kgain_grad)
 
 
 def solution(mesh):

time: 229 us -> 232 us (1.013); the launches traced: 228 us -> 228 us
  loops' own time: 0.84 us -> 12.1 us
  local copies, waits for them, and re-layouts: 25.1 us -> 16.7 us
  starting transfers between devices: 46.8 us -> 41.2 us
  Pallas kernels: 54.5 us -> 51.4 us
  matrix products: 7.72 us -> 10.2 us
    another operation x1, loops' own time: 0.01 us -> 11.5 us  [body(): lax.while_loop(lambda state: state[0] > 0.5, lambda state: (jnp.zeros((),...]
    unnamed x65 -> x42, local copies, waits for them, and re-layouts: 18.2 us -> 8.62 us
    ppermute x38 -> x35, starting transfers between devices: 43.3 us -> 37.7 us  [swap(): return lax.ppermute(x, axis, [(i, i ^ bit) for i in range(size)])]
    pallas_call x1, Pallas kernels: 18.1 us -> 13.5 us  [body(): pl.pallas_call(slots_kernel, out_shape=jax.ShapeDtypeStruct((SLOTS * TILE...]
    dot_general x8, matrix products: 7.72 us -> 10.2 us  [dot_rows(): lax.dot_general(a, b, (((0,), (0,)), ((), ())), preferred_element_type=F32)]
    pallas_call x1 -> x2, Pallas kernels: 12 us -> 13.6 us  [the longest x1 11.3 us: body(): pl.pallas_call(functools.partial(place_kernel, len(stacks)), out_shape=[j...]
    ppermute x38 -> x35, waiting for transfers between devices: 51.5 us -> 51.6 us  [swap(): return lax.ppermute(x, axis, [(i, i ^ bit) for i in range(size)])]
  transfers between devices with their start and end apart: 41 -> 38, of which waited for: 15 -> 16; matrix products, arithmetic and copies ran while one was open for 8% -> 10% of each run, Pallas kernels for 16% -> 14%
where the time goes in v5:
time: 232 us; the launch traced here: 228 us
  waiting for transfers between devices  87.8 us (38%)
  Pallas kernels  51.4 us (22%)
  starting transfers between devices  41.2 us (18%)
  local copies, waits for them, and re-layouts  16.7 us (7%)
  loops' own time  12.1 us (5%)
  matrix products  10.2 us (4%)
  other arithmetic  6.13 us (3%)
    ppermute x35, waiting for transfers between devices, swap(): return lax.ppermute(x, axis, [(i, i ^ bit) for i in range(size)])  51.6 us
    ppermute x35, starting transfers between devices, swap(): return lax.ppermute(x, axis, [(i, i ^ bit) for i in range(size)])  37.7 us
    ppermute x3, waiting for transfers between devices, gather(): return lax.ppermute(operands[k], BOTH, pairs)  36.2 us
    pallas_call x1, Pallas kernels, body(): pl.pallas_call(functools.partial(keys_kernel, blocks, (planes, packet, pa...  14 us
    pallas_call x1, Pallas kernels, body(): pl.pallas_call(slots_kernel, out_shape=jax.ShapeDtypeStruct((SLOTS * TILE...  13.5 us
    another operation x1, loops' own time, body(): lax.while_loop(lambda state: state[0] > 0.5, lambda state: (jnp.zeros((),...  11.5 us
    pallas_call x1, Pallas kernels, body(): pl.pallas_call(functools.partial(place_kernel, len(stacks)), out_shape=[j...  11.3 us
    dot_general x8, matrix products, dot_rows(): lax.dot_general(a, b, (((0,), (0,)), ((), ())), preferred_element_type=F32)  10.2 us
  transfers between devices with their start and end apart: 38, of which 16 were waited for; matrix products, arithmetic and copies ran while one was open for 10% of the time, Pallas kernels for 14%

profile of v5, /device:TPU:0, one launch (start us, length us, event | category | flops | bytes accessed | tf_op | source)
XLA Modules:
  0.0 227.6 jit_solution(7605504692339285710)
XLA Ops:
  1.3 14.0 %shard_map.129 = (bf16[192,2304]{1,0:T(8,128)(2,1)}, bf16[192,2304]{1,0:T(8,128)(2,1)}, bf16[192,2304]{1,0:T(8,128)(2,1)}, bf16[192,2304]{1,0:T(8,128)(2,1)}, bf...) custom-call(s32[5]{0:T(128)} %stack.35.index_ref, ...), custom_call_target="tpu_custom_call" | custom-call | flops 2684354560 | bytes 16777216 | tf_op jit(solution)/shard_map/pallas_call | solution.py:508
  15.9 2.6 %collective-permute-start.13 = (bf16[72,6272]{1,0:T(8,128)(2,1)}, bf16[72,6272]{1,0:T(8,128)(2,1)S(1)}, u32[]{:S(2)}, u32[]{:S(2)}) collective-permute-start(bf16[72,6272]{1,0:T(8,128)(2,1)} %get-tuple-element.147), channel_id=1, source_target_pairs={{0,4},{1,5},{2,6},{3,7},{4,0},{5,1},{6,2},{7,3},{8,12},{9,13},{10,... | collective-permute-start | bytes 2709512 | tf_op jit(solution)/shard_map/ppermute | solution.py:58
  18.5 2.6 %collective-permute-start.14 = (bf16[72,6272]{1,0:T(8,128)(2,1)}, bf16[72,6272]{1,0:T(8,128)(2,1)S(1)}, u32[]{:S(2)}, u32[]{:S(2)}) collective-permute-start(bf16[72,6272]{1,0:T(8,128)(2,1)} %get-tuple-element.148), channel_id=1, source_target_pairs={{0,8},{1,9},{2,10},{3,11},{4,12},{5,13},{6,14},{7,15},{8,0},{9,1},... | collective-permute-start | bytes 2709512 | tf_op jit(solution)/shard_map/ppermute | solution.py:58
  21.1 1.5 collective-permute-start.10
  22.6 1.5 collective-permute-start.11
  24.6 1.6 fusion.23
  26.8 16.3 %collective-permute-done.10 = bf16[192,2304]{1,0:T(8,128)(2,1)} collective-permute-done((bf16[192,2304]{1,0:T(8,128)(2,1)}, bf16[192,2304]{1,0:T(8,128)(2,1)}, u32[]{:S(2)}, u32[]{:S(2)}) %collective-permute-start.10) | collective-permute-done | bytes 884768 | tf_op jit(solution)/shard_map/ppermute | solution.py:564
  43.1 2.4 %collective-permute-done.11 = bf16[192,2304]{1,0:T(8,128)(2,1)} collective-permute-done((bf16[192,2304]{1,0:T(8,128)(2,1)}, bf16[192,2304]{1,0:T(8,128)(2,1)}, u32[]{:S(2)}, u32[]{:S(2)}) %collective-permute-start.11) | collective-permute-done | bytes 884768 | tf_op jit(solution)/shard_map/ppermute | solution.py:564
  45.5 17.5 %collective-permute-done.12 = bf16[192,2304]{1,0:T(8,128)(2,1)} collective-permute-done((bf16[192,2304]{1,0:T(8,128)(2,1)}, bf16[192,2304]{1,0:T(8,128)(2,1)}, u32[]{:S(2)}, u32[]{:S(2)}) %collective-permute-start.12) | collective-permute-done | bytes 884768 | tf_op jit(solution)/shard_map/ppermute | solution.py:564
  63.1 1.6 collective-permute-start.21
  65.2 1.6 fusion.18
  66.8 1.6 convolution_add_fusion.3
  68.5 1.7 fusion.20
  72.0 1.5 collective-permute-start.19
  74.1 2.0 convolution_add_fusion
  76.1 3.6 %collective-permute-done.21.refs_7_ = bf16[48,6272]{1,0:T(8,128)(2,1)S(1)} collective-permute-done((bf16[48,6272]{1,0:T(8,128)(2,1)S(1)}, bf16[48,6272]{1,0:T(8,128)(2,1)S(1)}, u32[]{:S(2)}, u32[]{:S(2)}) %collective-permute-start.21) | collective-permute-done | bytes 602144 | tf_op jit(solution)/shard_map/ppermute | solution.py:58
  80.5 12.1 %collective-permute-done.20.refs_6_ = bf16[48,6272]{1,0:T(8,128)(2,1)S(1)} collective-permute-done((bf16[48,6272]{1,0:T(8,128)(2,1)S(1)}, bf16[48,6272]{1,0:T(8,128)(2,1)S(1)}, u32[]{:S(2)}, u32[]{:S(2)}) %collective-permute-start.20) | collective-permute-done | bytes 602144 | tf_op jit(solution)/shard_map/ppermute | solution.py:58
  93.4 9.7 %collective-permute-done.19.refs_5_ = bf16[48,6272]{1,0:T(8,128)(2,1)S(1)} collective-permute-done((bf16[48,6272]{1,0:T(8,128)(2,1)S(1)}, bf16[48,6272]{1,0:T(8,128)(2,1)S(1)}, u32[]{:S(2)}, u32[]{:S(2)}) %collective-permute-start.19) | collective-permute-done | bytes 602144 | tf_op jit(solution)/shard_map/ppermute | solution.py:58
  105.5 1.5 collective-permute-start.23
  107.0 2.3 dynamic-slice_convert_fusion.2
  109.3 7.7 %collective-permute-start.22 = (bf16[640,512]{1,0:T(8,128)(2,1)}, bf16[640,512]{1,0:T(8,128)(2,1)}, u32[]{:S(2)}, u32[]{:S(2)}) collective-permute-start(bf16[640,512]{1,0:T(8,128)(2,1)} %dynamic-slice_convert_fusion.2), channel_id=1, source_target_pairs={{0,4},{1,5},{2,6},{3,7},{4,0},{5,1},{6,2},{7,3},{8,12},{9,13},{10,... | collective-permute-start | bytes 1966088 | tf_op jit(solution)/shard_map/ppermute | solution.py:58
  117.4 1.6 collective-permute-start.24
  118.9 2.1 collective-permute-done.24
  121.0 1.1 collective-permute-done.25
  122.2 1.5 collective-permute-start.26
  123.7 1.1 copy-done.13
  124.8 1.1 copy-done.15
  125.8 1.1 copy-done.17
  128.9 2.8 %shard_map.130.refs_0_ = bf16[432,6272]{1,0:T(8,128)(2,1)} custom-call(bf16[48,6272]{1,0:T(8,128)(2,1)S(1)} %copy-done.13, bf16[72,6272]{1,0:T(8,128)(2,1)S(1)} %collective-permute-done.13.refs_1_, bf16[72,6272]{1,0:T(8,128)(2,1)S(1)} %collective-permute-done.14.refs_2_, bf16[72,6272]{1,0:T(8,128)(2,1)S(1)} %collective-permute-done.18.refs_3_, ...), custom_call_target="tpu_custom_call" | custom-call | tf_op jit(solution)/shard_map/pallas_call | solution.py:597
  131.8 2.4 %convert_add_fusion.1 = f32[640,512]{1,0:T(8,128)} fusion(bf16[640,512]{1,0:T(8,128)(2,1)} %collective-permute-done.22, f32[1280,512]{1,0:T(8,128)S(1)} %copy-done.24, s32[]{:T(128)S(6)} %select_n.152), kind=kLoop, calls=%fused_computation.33 | loop fusion | flops 655360 | bytes 3276804 | tf_op jit(solution)/shard_map/add | solution.py:594
  135.0 1.1 dynamic-slice_convert_fusion.3
  136.1 1.5 collective-permute-start.27
  137.8 16.0 %collective-permute-done.27 = bf16[320,512]{1,0:T(8,128)(2,1)S(1)} collective-permute-done((bf16[320,512]{1,0:T(8,128)(2,1)S(1)}, bf16[320,512]{1,0:T(8,128)(2,1)S(1)}, u32[]{:S(2)}, u32[]{:S(2)}) %collective-permute-start.27) | collective-permute-done | bytes 327712 | tf_op jit(solution)/shard_map/ppermute | solution.py:58
  153.8 2.0 convert_add_fusion.2
  158.0 2.3 %shard_map.131 = (bf16[320,512]{1,0:T(8,128)(2,1)S(1)}, f32[1,320]{1,0:T(1,128)S(1)}) custom-call(s32[2]{0:T(128)S(1)} %pad_add_fusion.index_ref, f32[320,512]{1,0:T(8,128)} %get-tuple-element.409, bf16[5120,1024]{1,0:T(8,128)(2,1)} %w_ref.3, f32[1,320]{1,0:T(1,128)S(1)} %broadcast_in_dim.210.gain_ref), custom_call_target="tpu_custom_call" | custom-call | tf_op jit(solution)/shard_map/pallas_call | solution.py:663
  160.3 1.4 collective-permute-start.31
  161.8 2.9 %collective-permute-start.32 = (f32[1,320]{1,0:T(1,128)S(1)}, f32[1,320]{1,0:T(1,128)S(1)}, u32[]{:S(2)}, u32[]{:S(2)}) collective-permute-start(f32[1,320]{1,0:T(1,128)S(1)} %get-tuple-element.181), channel_id=1, source_target_pairs={{0,8},{1,9},{2,10},{3,11},{4,12},{5,13},{6,14},{7,15},{8,0},{9,1},... | collective-permute-start | bytes 3848 | tf_op jit(solution)/shard_map/ppermute | solution.py:58
  165.9 11.3 %shard_map.132 = (bf16[512,5120]{1,0:T(8,128)(2,1)}, bf16[512,1024]{1,0:T(8,128)(2,1)S(1)}) custom-call(s32[1]{0:T(128)} %bitcast.10.me_ref, bf16[432,6272]{1,0:T(8,128)(2,1)} %shard_map.130.refs_0_, bf16[48,6272]{1,0:T(8,128)(2,1)S(1)} %copy-done.9, bf16[432,6272]{1,0:T(8,128)(2,1)} %collective-permute-done.28.refs_2_, bf16[48,6272]{1,0:T(8,128)(2,1)S(1)} %copy-done.11), custom_call_target="tpu_custom_call" | custom-call | tf_op jit(solution)/shard_map/pallas_call | solution.py:687
  178.3 2.6 %collective-permute-start.35 = (f32[2,320]{1,0:T(2,128)S(1)}, f32[2,320]{1,0:T(2,128)S(1)}, u32[]{:S(2)}, u32[]{:S(2)}) collective-permute-start(f32[2,320]{1,0:T(2,128)S(1)} %broadcast_select_fusion.3), channel_id=1, source_target_pairs={{0,4},{1,5},{2,6},{3,7},{4,0},{5,1},{6,2},{7,3},{8,12},{9,13},{10,... | collective-permute-start | bytes 7688 | tf_op jit(solution)/shard_map/ppermute | solution.py:58
  182.5 11.5 %while.19 = (f32[]{:T(128)}, bf16[512,5120]{1,0:T(8,128)(2,1)}, s32[32,1]{0,1:T(1,128)S(1)}, bf16[256,5120]{1,0:T(8,128)(2,1)}, f32[5120]{0:T(1024)S(1)}, /*inde...) while((f32[]{:T(128)}, bf16[512,5120]{1,0:T(8,128)(2,1)}, s32[32,1]{0,1:T(1,128)S(1)}, bf16[256,5120]{1,0:T(8,128)(2,1)}, ...), condition=%region_7.8_spmd, body=%region_2.7_spmd | while | flops 4047654400 | bytes 60860424 | solution.py:719
  194.0 13.5 %shard_map.133 = bf16[512,5120]{1,0:T(8,128)(2,1)} custom-call(f32[1]{0:T(128)} %bitcast.21.over_ref, bf16[512,5120]{1,0:T(8,128)(2,1)} %get-tuple-element.193.rows_ref, bf16[512,1024]{1,0:T(8,128)(2,1)S(1)} %get-tuple-element.194.keys_ref, bf16[5120,1024]{1,0:T(8,128)(2,1)} %get-tuple-element.349, f32[1,5120]{1,0:T(1,128)S(1)} %bitcast.35), custom_call_target="tpu_custom_call" | custom-call | tf_op jit(solution)/shard_map/pallas_call | solution.py:727
  207.8 1.5 collective-permute-start.43
  209.9 2.0 collective-permute-done.44
  211.9 1.5 collective-permute-start.45
  213.6 2.0 collective-permute-done.45
  217.7 5.4 %shard_map.134.refs_2_ = f32[2560,1024]{1,0:T(8,128)} custom-call(s32[7]{0:T(128)S(1)} %pad_add_fusion.2.index_ref, bf16[320,512]{1,0:T(8,128)(2,1)S(1)} %get-tuple-element.196.refs_0_, bf16[320,512]{1,0:T(8,128)(2,1)S(1)} %collective-permute-done.30.refs_1_, bf16[640,512]{1,0:T(8,128)(2,1)S(1)} %collective-permute-done.33.refs_2_, ...), custom_call_target="tpu_custom_call" | custom-call | bytes 11796480 | tf_op jit(solution)/shard_map/pallas_call | solution.py:435
  224.0 1.3 collective-permute-done.46.refs_1_
  225.3 2.1 shard_map.135
  (149 shorter events, 21.7 us)
Async XLA Ops:
  15.3 8.8 %collective-permute-start.9 = (bf16[192,2304]{1,0:T(8,128)(2,1)}, bf16[192,2304]{1,0:T(8,128)(2,1)S(1)}, u32[]{:S(2)}, u32[]{:S(2)}) collective-permute-start(bf16[192,2304]{1,0:T(8,128)(2,1)} %get-tuple-element.142), channel_id=1, source_target_pairs={{0,1},{1,0},{2,3},{3,2},{4,5},{5,4},{6,7},{7,6},{8,9},{9,8},{10,11... | collective-permute-start | bytes 2654216 | tf_op jit(solution)/shard_map/ppermute | solution.py:58
  15.9 47.1 %collective-permute-start.13 = (bf16[72,6272]{1,0:T(8,128)(2,1)}, bf16[72,6272]{1,0:T(8,128)(2,1)S(1)}, u32[]{:S(2)}, u32[]{:S(2)}) collective-permute-start(bf16[72,6272]{1,0:T(8,128)(2,1)} %get-tuple-element.147), channel_id=1, source_target_pairs={{0,4},{1,5},{2,6},{3,7},{4,0},{5,1},{6,2},{7,3},{8,12},{9,13},{10,... | collective-permute-start | bytes 2709512 | tf_op jit(solution)/shard_map/ppermute | solution.py:58
  18.5 44.5 %collective-permute-start.14 = (bf16[72,6272]{1,0:T(8,128)(2,1)}, bf16[72,6272]{1,0:T(8,128)(2,1)S(1)}, u32[]{:S(2)}, u32[]{:S(2)}) collective-permute-start(bf16[72,6272]{1,0:T(8,128)(2,1)} %get-tuple-element.148), channel_id=1, source_target_pairs={{0,8},{1,9},{2,10},{3,11},{4,12},{5,13},{6,14},{7,15},{8,0},{9,1},... | collective-permute-start | bytes 2709512 | tf_op jit(solution)/shard_map/ppermute | solution.py:58
  21.1 22.0 %collective-permute-start.10 = (bf16[192,2304]{1,0:T(8,128)(2,1)}, bf16[192,2304]{1,0:T(8,128)(2,1)}, u32[]{:S(2)}, u32[]{:S(2)}) collective-permute-start(bf16[192,2304]{1,0:T(8,128)(2,1)} %get-tuple-element.143), channel_id=1, source_target_pairs={{0,2},{1,3},{2,0},{3,1},{4,6},{5,7},{6,4},{7,5},{8,10},{9,11},{10,... | collective-permute-start | bytes 2654216 | tf_op jit(solution)/shard_map/ppermute | solution.py:564
  22.6 22.9 %collective-permute-start.11 = (bf16[192,2304]{1,0:T(8,128)(2,1)}, bf16[192,2304]{1,0:T(8,128)(2,1)}, u32[]{:S(2)}, u32[]{:S(2)}) collective-permute-start(bf16[192,2304]{1,0:T(8,128)(2,1)} %get-tuple-element.144), channel_id=1, source_target_pairs={{0,16},{1,17},{2,18},{3,19},{4,20},{5,21},{6,22},{7,23},{8,24},{9,... | collective-permute-start | bytes 2654216 | tf_op jit(solution)/shard_map/ppermute | solution.py:564
  24.1 38.9 %collective-permute-start.12 = (bf16[192,2304]{1,0:T(8,128)(2,1)}, bf16[192,2304]{1,0:T(8,128)(2,1)}, u32[]{:S(2)}, u32[]{:S(2)}) collective-permute-start(bf16[192,2304]{1,0:T(8,128)(2,1)} %get-tuple-element.145), channel_id=1, source_target_pairs={{0,18},{1,19},{2,16},{3,17},{4,22},{5,23},{6,20},{7,21},{8,26},{9,... | collective-permute-start | bytes 2654216 | tf_op jit(solution)/shard_map/ppermute | solution.py:564
  63.1 16.6 %collective-permute-start.21 = (bf16[48,6272]{1,0:T(8,128)(2,1)S(1)}, bf16[48,6272]{1,0:T(8,128)(2,1)S(1)}, u32[]{:S(2)}, u32[]{:S(2)}) collective-permute-start(bf16[48,6272]{1,0:T(8,128)(2,1)S(1)} %slice.124), channel_id=1, source_target_pairs={{0,2},{1,3},{2,0},{3,1},{4,6},{5,7},{6,4},{7,5},{8,10},{9,11},{10,... | collective-permute-start | bytes 1806344 | tf_op jit(solution)/shard_map/ppermute | solution.py:58
  64.7 6.2 %collective-permute-start.15 = (bf16[192,2304]{1,0:T(8,128)(2,1)}, bf16[192,2304]{1,0:T(8,128)(2,1)S(1)}, u32[]{:S(2)}, u32[]{:S(2)}) collective-permute-start(bf16[192,2304]{1,0:T(8,128)(2,1)} %collective-permute-done.10), channel_id=1, source_target_pairs={{0,1},{1,0},{2,3},{3,2},{4,5},{5,4},{6,7},{7,6},{8,9},{9,8},{10,11... | collective-permute-start | bytes 2654216 | tf_op jit(solution)/shard_map/ppermute | solution.py:58
  64.7 7.3 %collective-permute-start.16 = (bf16[192,2304]{1,0:T(8,128)(2,1)}, bf16[192,2304]{1,0:T(8,128)(2,1)S(1)}, u32[]{:S(2)}, u32[]{:S(2)}) collective-permute-start(bf16[192,2304]{1,0:T(8,128)(2,1)} %collective-permute-done.11), channel_id=1, source_target_pairs={{0,1},{1,0},{2,3},{3,2},{4,5},{5,4},{6,7},{7,6},{8,9},{9,8},{10,11... | collective-permute-start | bytes 2654216 | tf_op jit(solution)/shard_map/ppermute | solution.py:58
  65.2 8.9 %collective-permute-start.17 = (bf16[192,2304]{1,0:T(8,128)(2,1)}, bf16[192,2304]{1,0:T(8,128)(2,1)S(1)}, u32[]{:S(2)}, u32[]{:S(2)}) collective-permute-start(bf16[192,2304]{1,0:T(8,128)(2,1)} %collective-permute-done.12), channel_id=1, source_target_pairs={{0,1},{1,0},{2,3},{3,2},{4,5},{5,4},{6,7},{7,6},{8,9},{9,8},{10,11... | collective-permute-start | bytes 2654216 | tf_op jit(solution)/shard_map/ppermute | solution.py:58
  70.2 33.8 %collective-permute-start.18 = (bf16[72,6272]{1,0:T(8,128)(2,1)S(1)}, bf16[72,6272]{1,0:T(8,128)(2,1)S(1)}, u32[]{:S(2)}, u32[]{:S(2)}) collective-permute-start(bf16[72,6272]{1,0:T(8,128)(2,1)S(1)} %copy-done.30), channel_id=1, source_target_pairs={{0,12},{1,13},{2,14},{3,15},{4,8},{5,9},{6,10},{7,11},{8,4},{9,5},... | collective-permute-start | bytes 2709512 | tf_op jit(solution)/shard_map/ppermute | solution.py:58
  71.4 21.2 %collective-permute-start.20 = (bf16[48,6272]{1,0:T(8,128)(2,1)S(1)}, bf16[48,6272]{1,0:T(8,128)(2,1)S(1)}, u32[]{:S(2)}, u32[]{:S(2)}) collective-permute-start(bf16[48,6272]{1,0:T(8,128)(2,1)S(1)} %slice.123), channel_id=1, source_target_pairs={{0,2},{1,3},{2,0},{3,1},{4,6},{5,7},{6,4},{7,5},{8,10},{9,11},{10,... | collective-permute-start | bytes 1806344 | tf_op jit(solution)/shard_map/ppermute | solution.py:58
  72.0 31.2 %collective-permute-start.19 = (bf16[48,6272]{1,0:T(8,128)(2,1)S(1)}, bf16[48,6272]{1,0:T(8,128)(2,1)S(1)}, u32[]{:S(2)}, u32[]{:S(2)}) collective-permute-start(bf16[48,6272]{1,0:T(8,128)(2,1)S(1)} %copy-done.12), channel_id=1, source_target_pairs={{0,2},{1,3},{2,0},{3,1},{4,6},{5,7},{6,4},{7,5},{8,10},{9,11},{10,... | collective-permute-start | bytes 1806344 | tf_op jit(solution)/shard_map/ppermute | solution.py:58
  74.1 43.3 %copy-start.29 = (f32[1,384]{1,0:T(1,128)S(1)}, f32[1,384]{1,0:T(1,128)}, u32[]{:S(2)}) copy-start(f32[1,384]{1,0:T(1,128)} %get-tuple-element.168) | copy-start | bytes 4612
  105.5 28.7 %collective-permute-start.23 = (bf16[48,6272]{1,0:T(8,128)(2,1)}, bf16[48,6272]{1,0:T(8,128)(2,1)S(1)}, u32[]{:S(2)}, u32[]{:S(2)}) collective-permute-start(bf16[48,6272]{1,0:T(8,128)(2,1)} %slice.125), channel_id=1, source_target_pairs={{0,2},{1,3},{2,0},{3,1},{4,6},{5,7},{6,4},{7,5},{8,10},{9,11},{10,... | collective-permute-start | bytes 1806344 | tf_op jit(solution)/shard_map/ppermute | solution.py:58
  109.3 22.5 %collective-permute-start.22 = (bf16[640,512]{1,0:T(8,128)(2,1)}, bf16[640,512]{1,0:T(8,128)(2,1)}, u32[]{:S(2)}, u32[]{:S(2)}) collective-permute-start(bf16[640,512]{1,0:T(8,128)(2,1)} %dynamic-slice_convert_fusion.2), channel_id=1, source_target_pairs={{0,4},{1,5},{2,6},{3,7},{4,0},{5,1},{6,2},{7,3},{8,12},{9,13},{10,... | collective-permute-start | bytes 1966088 | tf_op jit(solution)/shard_map/ppermute | solution.py:58
  117.4 3.6 %collective-permute-start.24 = (f32[1,384]{1,0:T(1,128)S(1)}, f32[1,384]{1,0:T(1,128)S(1)}, u32[]{:S(2)}, u32[]{:S(2)}) collective-permute-start(f32[1,384]{1,0:T(1,128)S(1)} %fusion.41), channel_id=1, source_target_pairs={{0,16},{16,0},{1,17},{17,1},{2,18},{18,2},{3,19},{19,3},{4,20},{20... | collective-permute-start | bytes 4616 | tf_op jit(solution)/shard_map/ppermute | solution.py:58
  121.0 1.2 collective-permute-start.25
  122.2 9.5 %collective-permute-start.26 = (f32[1,384]{1,0:T(1,128)S(1)}, f32[1,384]{1,0:T(1,128)S(1)}, u32[]{:S(2)}, u32[]{:S(2)}) collective-permute-start(f32[1,384]{1,0:T(1,128)S(1)} %add.312), channel_id=1, source_target_pairs={{0,2},{1,3},{2,0},{3,1},{4,6},{5,7},{6,4},{7,5},{8,10},{9,11},{10,... | collective-permute-start | bytes 4616 | tf_op jit(solution)/shard_map/ppermute | solution.py:58
  128.9 2.8 %copy-start.24 = (f32[1280,512]{1,0:T(8,128)S(1)}, f32[1280,512]{1,0:T(8,128)}, u32[]{:S(2)}) copy-start(f32[1280,512]{1,0:T(8,128)} %convolution_add_fusion) | copy-start | bytes 7864324
  131.7 2.8 %copy-start.27 = (f32[5120]{0:T(1024)S(1)}, f32[5120]{0:T(1024)}, u32[]{:S(2)}) copy-start(f32[5120]{0:T(1024)} %param.21) | copy-start | bytes 61444
  131.7 25.6 %copy-start.25 = (bf16[64,2304]{1,0:T(8,128)(2,1)S(1)}, bf16[64,2304]{1,0:T(8,128)(2,1)}, u32[]{:S(2)}) copy-start(bf16[64,2304]{1,0:T(8,128)(2,1)} %get-tuple-element.267) | copy-start | bytes 884740
  131.7 25.6 %copy-start.31 = (bf16[64,2304]{1,0:T(8,128)(2,1)S(1)}, bf16[64,2304]{1,0:T(8,128)(2,1)}, u32[]{:S(2)}) copy-start(bf16[64,2304]{1,0:T(8,128)(2,1)} %get-tuple-element.264) | copy-start | bytes 884740
  131.7 25.6 %copy-start.33 = (bf16[64,2304]{1,0:T(8,128)(2,1)S(1)}, bf16[64,2304]{1,0:T(8,128)(2,1)}, u32[]{:S(2)}) copy-start(bf16[64,2304]{1,0:T(8,128)(2,1)} %get-tuple-element.265) | copy-start | bytes 884740
  134.2 23.1 %copy-start.8 = (bf16[48,6272]{1,0:T(8,128)(2,1)}, bf16[48,6272]{1,0:T(8,128)(2,1)S(1)}, u32[]{:S(2)}) copy-start(bf16[48,6272]{1,0:T(8,128)(2,1)S(1)} %collective-permute-done.23.refs_1_) | copy-start | bytes 1806340
  134.2 22.5 %collective-permute-start.28 = (bf16[432,6272]{1,0:T(8,128)(2,1)}, bf16[432,6272]{1,0:T(8,128)(2,1)}, u32[]{:S(2)}, u32[]{:S(2)}) collective-permute-start(bf16[432,6272]{1,0:T(8,128)(2,1)} %shard_map.130.refs_0_), channel_id=1, source_target_pairs={{0,1},{1,0},{2,3},{3,2},{4,5},{5,4},{6,7},{7,6},{8,9},{9,8},{10,11... | collective-permute-start | bytes 16257032 | tf_op jit(solution)/shard_map/ppermute | solution.py:58
  134.6 21.3 %collective-permute-start.29 = (bf16[48,6272]{1,0:T(8,128)(2,1)S(1)}, bf16[48,6272]{1,0:T(8,128)(2,1)S(1)}, u32[]{:S(2)}, u32[]{:S(2)}) collective-permute-start(bf16[48,6272]{1,0:T(8,128)(2,1)S(1)} %collective-permute-done.23.refs_1_), channel_id=1, source_target_pairs={{0,1},{1,0},{2,3},{3,2},{4,5},{5,4},{6,7},{7,6},{8,9},{9,8},{10,11... | collective-permute-start | bytes 1806344 | tf_op jit(solution)/shard_map/ppermute | solution.py:58
  136.1 17.7 %collective-permute-start.27 = (bf16[320,512]{1,0:T(8,128)(2,1)S(1)}, bf16[320,512]{1,0:T(8,128)(2,1)S(1)}, u32[]{:S(2)}, u32[]{:S(2)}) collective-permute-start(bf16[320,512]{1,0:T(8,128)(2,1)S(1)} %dynamic-slice_convert_fusion.3), channel_id=1, source_target_pairs={{0,8},{1,9},{2,10},{3,11},{4,12},{5,13},{6,14},{7,15},{8,0},{9,1},... | collective-permute-start | bytes 983048 | tf_op jit(solution)/shard_map/ppermute | solution.py:58
  158.0 7.9 %copy-start.9 = (bf16[48,6272]{1,0:T(8,128)(2,1)S(1)}, bf16[48,6272]{1,0:T(8,128)(2,1)}, u32[]{:S(2)}) copy-start(bf16[48,6272]{1,0:T(8,128)(2,1)} %copy-done.8) | copy-start | bytes 1806340
  158.0 7.9 %copy-start.11 = (bf16[48,6272]{1,0:T(8,128)(2,1)S(1)}, bf16[48,6272]{1,0:T(8,128)(2,1)}, u32[]{:S(2)}) copy-start(bf16[48,6272]{1,0:T(8,128)(2,1)} %copy-done.10) | copy-start | bytes 1806340
  160.3 17.1 %collective-permute-start.31 = (bf16[320,512]{1,0:T(8,128)(2,1)S(1)}, bf16[320,512]{1,0:T(8,128)(2,1)S(1)}, u32[]{:S(2)}, u32[]{:S(2)}) collective-permute-start(bf16[320,512]{1,0:T(8,128)(2,1)S(1)} %get-tuple-element.196.refs_0_), channel_id=1, source_target_pairs={{0,2},{1,3},{2,0},{3,1},{4,6},{5,7},{6,4},{7,5},{8,10},{9,11},{10,... | collective-permute-start | bytes 983048 | tf_op jit(solution)/shard_map/ppermute | solution.py:58
  161.8 15.6 %collective-permute-start.30 = (bf16[320,512]{1,0:T(8,128)(2,1)S(1)}, bf16[320,512]{1,0:T(8,128)(2,1)S(1)}, u32[]{:S(2)}, u32[]{:S(2)}) collective-permute-start(bf16[320,512]{1,0:T(8,128)(2,1)S(1)} %get-tuple-element.196.refs_0_), channel_id=1, source_target_pairs={{0,8},{1,9},{2,10},{3,11},{4,12},{5,13},{6,14},{7,15},{8,0},{9,1},... | collective-permute-start | bytes 983048 | tf_op jit(solution)/shard_map/ppermute | solution.py:58
  161.8 15.5 %collective-permute-start.32 = (f32[1,320]{1,0:T(1,128)S(1)}, f32[1,320]{1,0:T(1,128)S(1)}, u32[]{:S(2)}, u32[]{:S(2)}) collective-permute-start(f32[1,320]{1,0:T(1,128)S(1)} %get-tuple-element.181), channel_id=1, source_target_pairs={{0,8},{1,9},{2,10},{3,11},{4,12},{5,13},{6,14},{7,15},{8,0},{9,1},... | collective-permute-start | bytes 3848 | tf_op jit(solution)/shard_map/ppermute | solution.py:58
  165.9 16.6 %copy-start.28 = (s32[32,1]{0,1:T(1,128)S(1)}, s32[32,1]{0,1:T(1,128)}, u32[]{:S(2)}) copy-start(s32[32,1]{0,1:T(1,128)} %param.19) | copy-start | bytes 388
  177.4 30.1 %collective-permute-start.37 = (f32[2,320]{1,0:T(2,128)S(1)}, f32[2,320]{1,0:T(2,128)S(1)}, u32[]{:S(2)}, u32[]{:S(2)}) collective-permute-start(f32[2,320]{1,0:T(2,128)S(1)} %broadcast_select_fusion.3), channel_id=1, source_target_pairs={{0,6},{1,7},{2,4},{3,5},{4,2},{5,3},{6,0},{7,1},{8,14},{9,15},{10,... | collective-permute-start | bytes 7688 | tf_op jit(solution)/shard_map/ppermute | solution.py:58
  177.5 30.1 %collective-permute-start.36 = (f32[2,320]{1,0:T(2,128)S(1)}, f32[2,320]{1,0:T(2,128)S(1)}, u32[]{:S(2)}, u32[]{:S(2)}) collective-permute-start(f32[2,320]{1,0:T(2,128)S(1)} %broadcast_select_fusion.3), channel_id=1, source_target_pairs={{0,2},{1,3},{2,0},{3,1},{4,6},{5,7},{6,4},{7,5},{8,10},{9,11},{10,... | collective-permute-start | bytes 7688 | tf_op jit(solution)/shard_map/ppermute | solution.py:58
  178.3 29.3 %collective-permute-start.35 = (f32[2,320]{1,0:T(2,128)S(1)}, f32[2,320]{1,0:T(2,128)S(1)}, u32[]{:S(2)}, u32[]{:S(2)}) collective-permute-start(f32[2,320]{1,0:T(2,128)S(1)} %broadcast_select_fusion.3), channel_id=1, source_target_pairs={{0,4},{1,5},{2,6},{3,7},{4,0},{5,1},{6,2},{7,3},{8,12},{9,13},{10,... | collective-permute-start | bytes 7688 | tf_op jit(solution)/shard_map/ppermute | solution.py:58
  180.9 26.8 %collective-permute-start.34 = (bf16[320,512]{1,0:T(8,128)(2,1)S(1)}, bf16[320,512]{1,0:T(8,128)(2,1)S(1)}, u32[]{:S(2)}, u32[]{:S(2)}) collective-permute-start(bf16[320,512]{1,0:T(8,128)(2,1)S(1)} %collective-permute-done.30.refs_1_), channel_id=1, source_target_pairs={{0,2},{1,3},{2,0},{3,1},{4,6},{5,7},{6,4},{7,5},{8,10},{9,11},{10,... | collective-permute-start | bytes 983048 | tf_op jit(solution)/shard_map/ppermute | solution.py:58
  182.4 25.4 %collective-permute-start.33 = (bf16[640,512]{1,0:T(8,128)(2,1)}, bf16[640,512]{1,0:T(8,128)(2,1)S(1)}, u32[]{:S(2)}, u32[]{:S(2)}) collective-permute-start(bf16[640,512]{1,0:T(8,128)(2,1)} %pad_maximum_fusion), channel_id=1, source_target_pairs={{0,4},{1,5},{2,6},{3,7},{4,0},{5,1},{6,2},{7,3},{8,12},{9,13},{10,... | collective-permute-start | bytes 1966088 | tf_op jit(solution)/shard_map/ppermute | solution.py:58
  207.8 15.4 %collective-permute-start.43 = (bf16[640,512]{1,0:T(8,128)(2,1)S(1)}, bf16[640,512]{1,0:T(8,128)(2,1)S(1)}, u32[]{:S(2)}, u32[]{:S(2)}) collective-permute-start(bf16[640,512]{1,0:T(8,128)(2,1)S(1)} %collective-permute-done.33.refs_2_), channel_id=1, source_target_pairs={{0,2},{1,3},{2,0},{3,1},{4,6},{5,7},{6,4},{7,5},{8,10},{9,11},{10,... | collective-permute-start | bytes 1966088 | tf_op jit(solution)/shard_map/ppermute | solution.py:58
  209.3 8.4 %collective-permute-start.40 = (bf16[640,512]{1,0:T(8,128)(2,1)S(1)}, bf16[640,512]{1,0:T(8,128)(2,1)S(1)}, u32[]{:S(2)}, u32[]{:S(2)}) collective-permute-start(bf16[640,512]{1,0:T(8,128)(2,1)S(1)} %collective-permute-done.33.refs_2_), channel_id=1, source_target_pairs={{0,1},{1,0},{2,3},{3,2},{4,5},{5,4},{6,7},{7,6},{8,9},{9,8},{10,11... | collective-permute-start | bytes 1966088 | tf_op jit(solution)/shard_map/ppermute | solution.py:58
  209.3 6.3 %collective-permute-start.38 = (bf16[320,512]{1,0:T(8,128)(2,1)S(1)}, bf16[320,512]{1,0:T(8,128)(2,1)}, u32[]{:S(2)}, u32[]{:S(2)}) collective-permute-start(bf16[320,512]{1,0:T(8,128)(2,1)S(1)} %get-tuple-element.196.refs_0_), channel_id=1, source_target_pairs={{0,1},{1,0},{2,3},{3,2},{4,5},{5,4},{6,7},{7,6},{8,9},{9,8},{10,11... | collective-permute-start | bytes 983048 | tf_op jit(solution)/shard_map/ppermute | solution.py:58
  209.8 2.1 collective-permute-start.44
  211.9 3.7 %collective-permute-start.45 = (f32[2,4,320]{2,1,0:T(4,128)S(1)}, f32[2,4,320]{2,1,0:T(4,128)S(1)}, u32[]{:S(2)}, u32[]{:S(2)}) collective-permute-start(f32[2,4,320]{2,1,0:T(4,128)S(1)} %add.322), channel_id=1, source_target_pairs={{0,16},{16,0},{1,17},{17,1},{2,18},{18,2},{3,19},{19,3},{4,20},{20... | collective-permute-start | bytes 30728 | tf_op jit(solution)/shard_map/ppermute | solution.py:58
  213.6 2.8 %collective-permute-start.39 = (bf16[320,512]{1,0:T(8,128)(2,1)S(1)}, bf16[320,512]{1,0:T(8,128)(2,1)S(1)}, u32[]{:S(2)}, u32[]{:S(2)}) collective-permute-start(bf16[320,512]{1,0:T(8,128)(2,1)S(1)} %collective-permute-done.30.refs_1_), channel_id=1, source_target_pairs={{0,1},{1,0},{2,3},{3,2},{4,5},{5,4},{6,7},{7,6},{8,9},{9,8},{10,11... | collective-permute-start | bytes 983048 | tf_op jit(solution)/shard_map/ppermute | solution.py:58
  215.6 1.6 collective-permute-start.41
  215.6 2.1 collective-permute-start.42
  223.2 2.1 collective-permute-start.46
  (11 other events, 12.1 us)

commit v6 on v5

--- a/solution.py
+++ b/solution.py
@@ -14,7 +14,7 @@
 PASSED_ON = 48
 TAGS = 128
 STRIP = 512
-UNROLL = 5
+UNROLL, KEYS_UNROLL = 2, 5
 EXTRA = 16
 CHUNK = 64
 KEYS_MIB, PRODUCTS_MIB, FINISH_MIB, STACK_MIB, PLACE_MIB, SLOTS_MIB = 56, 20, 8, 20, 36, 44
@@ -134,8 +134,9 @@
     copies[0].wait()
 
     sums[...] = jnp.zeros_like(sums)
-    spans = [slice(k, k + STRIP) for k in range(0, features, STRIP)]
-    for span in spans:
+
+    def squares(i, carry):
+        span = strip(i)
         packed = jnp.dot(onehot, hidden_ref[:, span], preferred_element_type=F32).astype(BF16)
         spread(packed, span)
 
@@ -144,11 +145,17 @@
             sums[at, :] += lane_sums(x * x)
 
         over_chunks(rows, add)
+        return carry
+
+    lax.fori_loop(0, strips, squares, 0, unroll=KEYS_UNROLL)
     packed = jnp.dot(onehot, tags, preferred_element_type=F32).astype(BF16)
     spread(packed, slice(features, features + TAGS))
     inv = lax.rsqrt(jnp.sum(sums[...], 1, keepdims=True) / features + epsilon)
     sums[...] = jnp.broadcast_to(inv, sums.shape)
-    for i, span in enumerate(spans):
+    keys[...] = jnp.zeros_like(keys)
+
+    def project(i, carry):
+        span = strip(i)
         gain = gain_ref[:, span]
 
         def scale(at):
@@ -159,9 +166,10 @@
         h = hidden_ref[:, span]
         h_all[:, span] = jnp.dot(squeeze, h, preferred_element_type=F32).astype(BF16)
         fetch(i).wait()
-        product = jnp.dot(h, w_all[span, :], preferred_element_type=F32)
-        keys[...] = keys[...] + product if i else product
-
+        keys[...] += jnp.dot(h, w_all[span, :], preferred_element_type=F32)
+        return carry
+
+    lax.fori_loop(0, strips, project, 0, unroll=KEYS_UNROLL)
     width = outs[0].shape[1] - keys.shape[1]
     for k in range(blocks):
         columns = pl.ds(pl.multiple_of(index_ref[k] * width, width), width)
@@ -276,17 +284,28 @@
         lax.fori_loop(0, 5, block, 0, unroll=True)
 
 
+def halve_kernel(index_ref, total_ref, other_ref, sent_out, kept_out, mine, sem):
+    rows = other_ref.shape[0]
+    first = pl.multiple_of(index_ref[0] * rows, rows)
+    copy = pltpu.make_async_copy(total_ref.at[pl.ds(first, rows)], mine, sem)
+    copy.start()
+    copy.wait()
+    for out, place in ((sent_out, 1 - index_ref[1]), (kept_out, index_ref[1])):
+        part = pl.ds(pl.multiple_of(place * (rows // 2), rows // 2), rows // 2)
+        out[...] = (mine[part, :] + other_ref[part, :].astype(F32)).astype(out.dtype)
+
+
 def finish_kernel(
-    index_ref, total_ref, w_ref, gain_ref, block_out, gains_out, w_part, gain, sems
+    index_ref, kept_ref, other_ref, w_ref, gain_ref, block_out, gains_out, w_part, gain, sems
 ):
-    tall, half = total_ref.shape
+    tall, half = kept_ref.shape
     rows = pl.ds(pl.multiple_of(index_ref[0] * tall, tall), tall)
     columns = pl.ds(pl.multiple_of(index_ref[1] * half, half), half)
     fetch_w = pltpu.make_async_copy(w_ref.at[rows, columns], w_part, sems.at[0])
     fetch_gain = pltpu.make_async_copy(gain_ref, gain, sems.at[1])
     fetch_w.start()
     fetch_gain.start()
-    total = total_ref[...]
+    total = kept_ref[...] + other_ref[...].astype(F32)
     block_out[...] = total.astype(BF16)
     fetch_gain.wait()
     fetch_w.wait()
@@ -358,49 +377,69 @@
     over_ref, rows_ref, keys_ref, w_ref, gain_ref, out_ref, w_all, grad, rows_all, sums, sems
 ):
     slots, features = grad.shape
-    strips = [slice(k, k + STRIP) for k in range(0, features, STRIP)]
-    fetches, loads, stores = [], [], []
-    for i, strip in enumerate(strips):
-        fetches.append(pltpu.make_async_copy(w_ref.at[strip], w_all.at[strip], sems.at[0, i]))
-        here = rows_all.at[:, strip]
-        loads.append(pltpu.make_async_copy(rows_ref.at[:, strip], here, sems.at[1, i]))
-        stores.append(pltpu.make_async_copy(here, out_ref.at[:, strip], sems.at[2, i]))
-        fetches[i].start()
-        loads[i].start()
+    strips = features // STRIP
+
+    def strip(i):
+        return pl.ds(pl.multiple_of(i * STRIP, STRIP), STRIP)
+
+    def fetch(i):
+        return pltpu.make_async_copy(w_ref.at[strip(i)], w_all.at[strip(i)], sems.at[0, i])
+
+    def load(i):
+        here = rows_all.at[:, strip(i)]
+        return pltpu.make_async_copy(rows_ref.at[:, strip(i)], here, sems.at[1, i])
+
+    def store(i):
+        here = rows_all.at[:, strip(i)]
+        return pltpu.make_async_copy(here, out_ref.at[:, strip(i)], sems.at[2, i])
+
+    for i in range(strips):
+        fetch(i).start()
+        load(i).start()
     sums[...] = jnp.zeros_like(sums)
-    for i, strip in enumerate(strips):
-        fetches[i].wait()
-        loads[i].wait()
-        grad[:, strip] = lax.dot_general(
-            keys_ref[...], w_all[strip, :], (((1,), (1,)), ((), ())), preferred_element_type=F32
+
+    def back(i, carry):
+        here = strip(i)
+        fetch(i).wait()
+        load(i).wait()
+        grad[:, here] = lax.dot_general(
+            keys_ref[...], w_all[here, :], (((1,), (1,)), ((), ())), preferred_element_type=F32
         )
-        gain = gain_ref[:, strip]
+        gain = gain_ref[:, here]
 
         def add(at):
-            rows = rows_all[at, strip].astype(F32)
+            rows = rows_all[at, here].astype(F32)
             sums[0, at, :] += lane_sums(rows * rows)
-            sums[1, at, :] += lane_sums(grad[at, strip] * gain * rows)
+            sums[1, at, :] += lane_sums(grad[at, here] * gain * rows)
 
         over_chunks(slots, add)
+        return carry
+
+    lax.fori_loop(0, strips, back, 0, unroll=UNROLL)
     inv = lax.rsqrt(jnp.sum(sums[0], 1, keepdims=True) / features + epsilon)
     slope = jnp.sum(sums[1], 1, keepdims=True) * inv * inv * inv / features
     sums[0] = jnp.broadcast_to(inv, sums.shape[1:])
     sums[1] = jnp.broadcast_to(slope, sums.shape[1:])
     dense = over_ref[0] > 0.5
-    for i, strip in enumerate(strips):
-        gain = gain_ref[:, strip]
+
+    def last(i, carry):
+        here = strip(i)
+        gain = gain_ref[:, here]
 
         def finish(at):
             first = jnp.concatenate([sums[0, at, :]] * (STRIP // 128), 1)
             second = jnp.concatenate([sums[1, at, :]] * (STRIP // 128), 1)
-            rows = rows_all[at, strip]
-            final = first * (grad[at, strip] * gain) - rows.astype(F32) * second
-            rows_all[at, strip] = jnp.where(dense, rows, final.astype(BF16))
+            rows = rows_all[at, here]
+            final = first * (grad[at, here] * gain) - rows.astype(F32) * second
+            rows_all[at, here] = jnp.where(dense, rows, final.astype(BF16))
 
         over_chunks(slots, finish)
-        stores[i].start()
-    for store in stores:
-        store.wait()
+        store(i).start()
+        return carry
+
+    lax.fori_loop(0, strips, last, 0)
+    for i in range(strips):
+        store(i).wait()
 
 
 def output_kernel(sizes, index_ref, *refs):
@@ -579,11 +618,6 @@
     last = planes - 1
     held, passed = {0: packs[1], planes: packs[0]}, {}
 
-    def add_products(total, parts):
-        for part in parts:
-            total = total + products(part) + products(across_learn(part, 1))
-        return total
-
     bits = [4 << b for b in range(planes.bit_length() - 1)]
 
     def halve(total, bit):
@@ -628,7 +662,9 @@
             total = halve(total, bit)
         return jnp.zeros((), F32), state[1] + total
 
-    total = add_products(0.0, [operands[0], *gathered])
+    total = 0.0
+    for part in [operands[0], *gathered]:
+        total = total + products(part) + products(across_learn(part, 1))
     held[last] = across_learn(packs[-1], 4 * last)
     for k in range(last):
         passed[k] = over_y(held[k])
@@ -643,21 +679,42 @@
     while len(values) > 1:
         values = [a + b for a, b in zip(values[::2], values[1::2])]
     sums = values[0]
+    uppers = [(learn // bit) % 2 for bit in bits]
+    rows_sent = width // 2
+    sent = lax.dynamic_slice_in_dim(total, (1 - uppers[0]) * rows_sent, rows_sent, 0).astype(BF16)
+    kept, kept_at = total, uppers[0]
     for n, bit in enumerate(bits):
-        total = halve(total, bit)
+        received = across_learn(sent, bit)
         if n == 0:
             stacked = stack(list(held.values()) + list(passed.values()))
             passed[last] = over_y(held[last])
             sums = butterfly_sum(sums, (("gen", gens),))
             sums = butterfly_sum(sums, (("learn", 4),), learners)
-            total, passed, stacked, sums = barrier((total, passed, stacked, sums))
+            received, kept, passed, stacked, sums = barrier(
+                (received, kept, passed, stacked, sums)
+            )
         if n == 1:
             stacks = [stacked, passed[last]]
             stacks += [across_learn(part, 1) for part in stacks]
-            total, stacks, sums = barrier((total, stacks, sums))
-    _, total = lax.while_loop(lambda state: state[0] > 0.5, add_rests, (sums[0, -1], total))
-
-    tall = total.shape[0]
+        if n + 1 == len(bits):
+            break
+        tall = received.shape[0]
+        sent, kept = pl.pallas_call(
+            halve_kernel,
+            out_shape=[
+                jax.ShapeDtypeStruct((tall // 2, half), BF16),
+                jax.ShapeDtypeStruct((tall // 2, half), F32),
+            ],
+            in_specs=[SMEM, ANY, VMEM],
+            out_specs=[VMEM] * 2,
+            scratch_shapes=[pltpu.VMEM((tall, half), F32), pltpu.SemaphoreType.DMA],
+            compiler_params=limit(FINISH_MIB),
+        )(jnp.stack([kept_at, uppers[n + 1]]), kept, received)
+        kept_at = jnp.zeros((), jnp.int32)
+    _, kept = lax.while_loop(lambda state: state[0] > 0.5, add_rests, (sums[0, -1], kept))
+    received, kept, stacks, sums = barrier((received, kept, stacks, sums))
+
+    tall = kept.shape[0]
     z_place = sum(((learn // bit) % 2) * (planes >> (n + 1)) for n, bit in enumerate(bits))
     first = (gen * 2 + across) * planes + z_place
     block, gains = pl.pallas_call(
@@ -666,7 +723,7 @@
             jax.ShapeDtypeStruct((tall, half), BF16),
             jax.ShapeDtypeStruct((1, tall), F32),
         ],
-        in_specs=[SMEM, VMEM, ANY, ANY],
+        in_specs=[SMEM, VMEM, VMEM, ANY, ANY],
         out_specs=[VMEM] * 2,
         scratch_shapes=[
             pltpu.VMEM((tall, half), BF16),
@@ -676,7 +733,8 @@
         compiler_params=limit(FINISH_MIB),
     )(
         jnp.stack([first, core]),
-        total,
+        kept,
+        received,
         w_key,
         lax.dynamic_slice_in_dim(in_gain, first * tall, tall)[None],
     )

time: 232 us -> 217 us (0.935); the launches traced: 228 us -> 216 us
  loops' own time: 12.1 us -> 1.03 us
  waiting for transfers between devices: 87.8 us -> 92.6 us
  starting transfers between devices: 41.2 us -> 37.6 us
  other arithmetic: 6.13 us -> 3 us
  Pallas kernels: 51.4 us -> 54 us
  matrix products: 10.2 us -> 7.73 us
    another operation x1, loops' own time: 11.5 us -> 0.23 us  [body(): lax.while_loop(lambda state: state[0] > 0.5, lambda state: (jnp.zeros((),...]
    ppermute x35, waiting for transfers between devices: 51.6 us -> 57.5 us  [swap(): return lax.ppermute(x, axis, [(i, i ^ bit) for i in range(size)])]
    add x2 -> x0, other arithmetic: 4.46 us -> none  [halve(): return kept + across_learn(sent, bit).astype(F32)]
    ppermute x35, starting transfers between devices: 37.7 us -> 34.1 us  [swap(): return lax.ppermute(x, axis, [(i, i ^ bit) for i in range(size)])]
    unnamed x42 -> x40, local copies, waits for them, and re-layouts: 8.62 us -> 11.8 us
    dot_general x8, matrix products: 10.2 us -> 7.73 us  [dot_rows(): lax.dot_general(a, b, (((0,), (0,)), ((), ())), preferred_element_type=F32)]
    convert_element_type x2 -> x1, local copies, waits for them, and re-layouts: 3.39 us -> 0.94 us  [body(): lax.dynamic_slice_in_dim(total, (1 - uppers[0]) * rows_sent, rows_sent, 0)]
  transfers between devices with their start and end apart: 38 -> 38, of which waited for: 16 -> 17; matrix products, arithmetic and copies ran while one was open for 10% -> 7% of each run, Pallas kernels for 14% -> 16%
where the time goes in v6:
time: 217 us; the launch traced here: 216 us
  waiting for transfers between devices  92.6 us (43%)
  Pallas kernels  54 us (25%)
  starting transfers between devices  37.6 us (17%)
  local copies, waits for them, and re-layouts  18.5 us (9%)
  matrix products  7.73 us (4%)
  other arithmetic  3 us (1%)
    ppermute x35, waiting for transfers between devices, swap(): return lax.ppermute(x, axis, [(i, i ^ bit) for i in range(size)])  57.5 us
    ppermute x3, waiting for transfers between devices, gather(): return lax.ppermute(operands[k], BOTH, pairs)  35.1 us
    ppermute x35, starting transfers between devices, swap(): return lax.ppermute(x, axis, [(i, i ^ bit) for i in range(size)])  34.1 us
    pallas_call x1, Pallas kernels, body(): pl.pallas_call(functools.partial(keys_kernel, blocks, (planes, packet, pa...  14.7 us
    pallas_call x1, Pallas kernels, body(): pl.pallas_call(slots_kernel, out_shape=jax.ShapeDtypeStruct((SLOTS * TILE...  13.3 us
    unnamed x40, local copies, waits for them, and re-layouts  11.8 us
    pallas_call x1, Pallas kernels, body(): pl.pallas_call(functools.partial(place_kernel, len(stacks)), out_shape=[j...  11.3 us
    dot_general x8, matrix products, dot_rows(): lax.dot_general(a, b, (((0,), (0,)), ((), ())), preferred_element_type=F32)  7.73 us
  transfers between devices with their start and end apart: 38, of which 17 were waited for; matrix products, arithmetic and copies ran while one was open for 7% of the time, Pallas kernels for 16%

profile of v6, /device:TPU:0, one launch (start us, length us, event | category | flops | bytes accessed | tf_op | source)
XLA Modules:
  0.0 216.2 jit_solution(12349353463222320028)
XLA Ops:
  1.3 14.7 %shard_map.129 = (bf16[192,2304]{1,0:T(8,128)(2,1)}, bf16[192,2304]{1,0:T(8,128)(2,1)}, bf16[192,2304]{1,0:T(8,128)(2,1)}, bf16[192,2304]{1,0:T(8,128)(2,1)}, bf...) custom-call(s32[5]{0:T(128)} %stack.47.index_ref, ...), custom_call_target="tpu_custom_call" | custom-call | flops 2684354560 | bytes 16777216 | tf_op jit(solution)/shard_map/pallas_call | solution.py:547
  16.5 2.6 %collective-permute-start.13 = (bf16[72,6272]{1,0:T(8,128)(2,1)}, bf16[72,6272]{1,0:T(8,128)(2,1)S(1)}, u32[]{:S(2)}, u32[]{:S(2)}) collective-permute-start(bf16[72,6272]{1,0:T(8,128)(2,1)} %get-tuple-element.151), channel_id=1, source_target_pairs={{0,4},{1,5},{2,6},{3,7},{4,0},{5,1},{6,2},{7,3},{8,12},{9,13},{10,... | collective-permute-start | bytes 2709512 | tf_op jit(solution)/shard_map/ppermute | solution.py:58
  19.1 2.6 %collective-permute-start.14 = (bf16[72,6272]{1,0:T(8,128)(2,1)}, bf16[72,6272]{1,0:T(8,128)(2,1)S(1)}, u32[]{:S(2)}, u32[]{:S(2)}) collective-permute-start(bf16[72,6272]{1,0:T(8,128)(2,1)} %get-tuple-element.152), channel_id=1, source_target_pairs={{0,8},{1,9},{2,10},{3,11},{4,12},{5,13},{6,14},{7,15},{8,0},{9,1},... | collective-permute-start | bytes 2709512 | tf_op jit(solution)/shard_map/ppermute | solution.py:58
  21.7 1.5 collective-permute-start.10
  23.3 1.5 collective-permute-start.11
  26.1 1.7 fusion.23
  28.4 15.3 %collective-permute-done.10 = bf16[192,2304]{1,0:T(8,128)(2,1)} collective-permute-done((bf16[192,2304]{1,0:T(8,128)(2,1)}, bf16[192,2304]{1,0:T(8,128)(2,1)}, u32[]{:S(2)}, u32[]{:S(2)}) %collective-permute-start.10) | collective-permute-done | bytes 884768 | tf_op jit(solution)/shard_map/ppermute | solution.py:603
  43.7 2.4 %collective-permute-done.11 = bf16[192,2304]{1,0:T(8,128)(2,1)} collective-permute-done((bf16[192,2304]{1,0:T(8,128)(2,1)}, bf16[192,2304]{1,0:T(8,128)(2,1)}, u32[]{:S(2)}, u32[]{:S(2)}) %collective-permute-start.11) | collective-permute-done | bytes 884768 | tf_op jit(solution)/shard_map/ppermute | solution.py:603
  46.1 17.4 %collective-permute-done.12 = bf16[192,2304]{1,0:T(8,128)(2,1)S(1)} collective-permute-done((bf16[192,2304]{1,0:T(8,128)(2,1)}, bf16[192,2304]{1,0:T(8,128)(2,1)S(1)}, u32[]{:S(2)}, u32[]{:S(2)}) %collective-permute-start.12) | collective-permute-done | bytes 884768 | tf_op jit(solution)/shard_map/ppermute | solution.py:603
  63.6 1.6 collective-permute-start.21
  66.3 1.6 convolution_add_fusion.3
  67.9 1.7 fusion.20
  71.6 1.5 collective-permute-start.19
  74.2 6.0 %collective-permute-done.21.refs_7_ = bf16[48,6272]{1,0:T(8,128)(2,1)S(1)} collective-permute-done((bf16[48,6272]{1,0:T(8,128)(2,1)S(1)}, bf16[48,6272]{1,0:T(8,128)(2,1)S(1)}, u32[]{:S(2)}, u32[]{:S(2)}) %collective-permute-start.21) | collective-permute-done | bytes 602144 | tf_op jit(solution)/shard_map/ppermute | solution.py:58
  81.0 12.1 %collective-permute-done.20.refs_6_ = bf16[48,6272]{1,0:T(8,128)(2,1)S(1)} collective-permute-done((bf16[48,6272]{1,0:T(8,128)(2,1)S(1)}, bf16[48,6272]{1,0:T(8,128)(2,1)S(1)}, u32[]{:S(2)}, u32[]{:S(2)}) %collective-permute-start.20) | collective-permute-done | bytes 602144 | tf_op jit(solution)/shard_map/ppermute | solution.py:58
  93.9 9.8 %collective-permute-done.19.refs_5_ = bf16[48,6272]{1,0:T(8,128)(2,1)S(1)} collective-permute-done((bf16[48,6272]{1,0:T(8,128)(2,1)S(1)}, bf16[48,6272]{1,0:T(8,128)(2,1)S(1)}, u32[]{:S(2)}, u32[]{:S(2)}) %collective-permute-start.19) | collective-permute-done | bytes 602144 | tf_op jit(solution)/shard_map/ppermute | solution.py:58
  104.8 0.9 slice.125
  106.5 1.6 collective-permute-start.23
  108.1 0.9 dynamic-slice_convert_fusion.2
  109.0 6.4 %collective-permute-start.22 = (bf16[640,512]{1,0:T(8,128)(2,1)}, bf16[640,512]{1,0:T(8,128)(2,1)}, u32[]{:S(2)}, u32[]{:S(2)}) collective-permute-start(bf16[640,512]{1,0:T(8,128)(2,1)} %dynamic-slice_convert_fusion.2), channel_id=1, source_target_pairs={{0,4},{1,5},{2,6},{3,7},{4,0},{5,1},{6,2},{7,3},{8,12},{9,13},{10,... | collective-permute-start | bytes 1966088 | tf_op jit(solution)/shard_map/ppermute | solution.py:58
  117.2 1.6 collective-permute-start.24
  118.8 2.1 collective-permute-done.24
  120.9 1.1 collective-permute-done.25
  122.0 1.5 collective-permute-start.26
  123.6 1.2 copy-done.9
  124.8 1.2 copy-done.11
  125.9 1.1 copy-done.13
  127.0 1.1 copy-done.15
  128.1 1.1 copy-done.17
  129.1 1.1 copy-done.19
  130.2 1.0 copy-done.20
  131.2 2.8 %shard_map.130.refs_0_ = bf16[432,6272]{1,0:T(8,128)(2,1)} custom-call(bf16[48,6272]{1,0:T(8,128)(2,1)S(1)} %copy-done.13, bf16[72,6272]{1,0:T(8,128)(2,1)S(1)} %collective-permute-done.13.refs_1_, bf16[72,6272]{1,0:T(8,128)(2,1)S(1)} %copy-done.9, bf16[72,6272]{1,0:T(8,128)(2,1)S(1)} %copy-done.11, bf16[24,6272]{1,0:T(8,128)(2,1)S(1)} %copy-done.20, ...), custom_call_target="tpu_custom_call" | custom-call | tf_op jit(solution)/shard_map/pallas_call | solution.py:631
  134.8 2.1 shard_map.131
  139.2 17.0 %collective-permute-done.27.other_ref = bf16[320,512]{1,0:T(8,128)(2,1)S(1)} collective-permute-done((bf16[320,512]{1,0:T(8,128)(2,1)}, bf16[320,512]{1,0:T(8,128)(2,1)S(1)}, u32[]{:S(2)}, u32[]{:S(2)}) %collective-permute-start.27) | collective-permute-done | bytes 327712 | tf_op jit(solution)/shard_map/ppermute | solution.py:58
  156.3 2.2 %shard_map.132 = (bf16[320,512]{1,0:T(8,128)(2,1)S(1)}, f32[1,320]{1,0:T(1,128)S(1)}) custom-call(s32[2]{0:T(128)S(1)} %get-tuple-element.250.index_ref, f32[320,512]{1,0:T(8,128)} %get-tuple-element.185.kept_ref, bf16[320,512]{1,0:T(8,128)(2,1)S(1)} %collective-permute-done.27.other_ref, bf16[5120,1024]{1,0:T(8,128)(2,1)} %w_ref.3, ...), custom_call_target="tpu_custom_call" | custom-call | tf_op jit(solution)/shard_map/pallas_call | solution.py:720
  159.1 2.9 %collective-permute-start.32 = (f32[1,320]{1,0:T(1,128)S(1)}, f32[1,320]{1,0:T(1,128)S(1)}, u32[]{:S(2)}, u32[]{:S(2)}) collective-permute-start(f32[1,320]{1,0:T(1,128)S(1)} %get-tuple-element.188), channel_id=1, source_target_pairs={{0,8},{1,9},{2,10},{3,11},{4,12},{5,13},{6,14},{7,15},{8,0},{9,1},... | collective-permute-start | bytes 3848 | tf_op jit(solution)/shard_map/ppermute | solution.py:58
  163.7 11.3 %shard_map.133 = (bf16[512,5120]{1,0:T(8,128)(2,1)}, bf16[512,1024]{1,0:T(8,128)(2,1)S(1)}) custom-call(s32[1]{0:T(128)} %bitcast.12.me_ref, bf16[432,6272]{1,0:T(8,128)(2,1)} %shard_map.130.refs_0_, bf16[48,6272]{1,0:T(8,128)(2,1)} %collective-permute-done.23.refs_1_, bf16[432,6272]{1,0:T(8,128)(2,1)} %collective-permute-done.28.refs_2_, ...), custom_call_target="tpu_custom_call" | custom-call | tf_op jit(solution)/shard_map/pallas_call | solution.py:745
  175.9 1.4 collective-permute-start.36
  177.3 1.9 collective-permute-start.35
  179.2 1.5 collective-permute-start.34
  181.9 13.3 %shard_map.134 = bf16[512,5120]{1,0:T(8,128)(2,1)} custom-call(f32[1]{0:T(128)} %bitcast.23.over_ref, bf16[512,5120]{1,0:T(8,128)(2,1)} %get-tuple-element.201.rows_ref, bf16[512,1024]{1,0:T(8,128)(2,1)S(1)} %get-tuple-element.202.keys_ref, bf16[5120,1024]{1,0:T(8,128)(2,1)} %get-tuple-element.357, f32[1,5120]{1,0:T(1,128)S(1)} %bitcast.37), custom_call_target="tpu_custom_call" | custom-call | tf_op jit(solution)/shard_map/pallas_call | solution.py:785
  195.6 1.8 collective-permute-done.33.refs_2_
  198.5 2.0 collective-permute-done.44
  200.5 1.5 collective-permute-start.45
  202.2 2.0 collective-permute-done.45
  206.3 5.4 %shard_map.135.refs_2_ = f32[2560,1024]{1,0:T(8,128)} custom-call(s32[7]{0:T(128)S(1)} %pad_add_fusion.3.index_ref, bf16[320,512]{1,0:T(8,128)(2,1)S(1)} %get-tuple-element.204.refs_0_, bf16[320,512]{1,0:T(8,128)(2,1)S(1)} %collective-permute-done.30.refs_1_, bf16[640,512]{1,0:T(8,128)(2,1)S(1)} %collective-permute-done.33.refs_2_, ...), custom_call_target="tpu_custom_call" | custom-call | bytes 11796480 | tf_op jit(solution)/shard_map/pallas_call | solution.py:474
  212.8 1.3 collective-permute-done.46.refs_1_
  214.1 2.1 shard_map.136
  (146 shorter events, 24.0 us)
Async XLA Ops:
  16.0 8.8 %collective-permute-start.9 = (bf16[192,2304]{1,0:T(8,128)(2,1)}, bf16[192,2304]{1,0:T(8,128)(2,1)S(1)}, u32[]{:S(2)}, u32[]{:S(2)}) collective-permute-start(bf16[192,2304]{1,0:T(8,128)(2,1)} %get-tuple-element.146), channel_id=1, source_target_pairs={{0,1},{1,0},{2,3},{3,2},{4,5},{5,4},{6,7},{7,6},{8,9},{9,8},{10,11... | collective-permute-start | bytes 2654216 | tf_op jit(solution)/shard_map/ppermute | solution.py:58
  16.5 47.0 %collective-permute-start.13 = (bf16[72,6272]{1,0:T(8,128)(2,1)}, bf16[72,6272]{1,0:T(8,128)(2,1)S(1)}, u32[]{:S(2)}, u32[]{:S(2)}) collective-permute-start(bf16[72,6272]{1,0:T(8,128)(2,1)} %get-tuple-element.151), channel_id=1, source_target_pairs={{0,4},{1,5},{2,6},{3,7},{4,0},{5,1},{6,2},{7,3},{8,12},{9,13},{10,... | collective-permute-start | bytes 2709512 | tf_op jit(solution)/shard_map/ppermute | solution.py:58
  19.1 44.4 %collective-permute-start.14 = (bf16[72,6272]{1,0:T(8,128)(2,1)}, bf16[72,6272]{1,0:T(8,128)(2,1)S(1)}, u32[]{:S(2)}, u32[]{:S(2)}) collective-permute-start(bf16[72,6272]{1,0:T(8,128)(2,1)} %get-tuple-element.152), channel_id=1, source_target_pairs={{0,8},{1,9},{2,10},{3,11},{4,12},{5,13},{6,14},{7,15},{8,0},{9,1},... | collective-permute-start | bytes 2709512 | tf_op jit(solution)/shard_map/ppermute | solution.py:58
  21.7 22.0 %collective-permute-start.10 = (bf16[192,2304]{1,0:T(8,128)(2,1)}, bf16[192,2304]{1,0:T(8,128)(2,1)}, u32[]{:S(2)}, u32[]{:S(2)}) collective-permute-start(bf16[192,2304]{1,0:T(8,128)(2,1)} %get-tuple-element.147), channel_id=1, source_target_pairs={{0,2},{1,3},{2,0},{3,1},{4,6},{5,7},{6,4},{7,5},{8,10},{9,11},{10,... | collective-permute-start | bytes 2654216 | tf_op jit(solution)/shard_map/ppermute | solution.py:603
  23.3 22.9 %collective-permute-start.11 = (bf16[192,2304]{1,0:T(8,128)(2,1)}, bf16[192,2304]{1,0:T(8,128)(2,1)}, u32[]{:S(2)}, u32[]{:S(2)}) collective-permute-start(bf16[192,2304]{1,0:T(8,128)(2,1)} %get-tuple-element.148), channel_id=1, source_target_pairs={{0,16},{1,17},{2,18},{3,19},{4,20},{5,21},{6,22},{7,23},{8,24},{9,... | collective-permute-start | bytes 2654216 | tf_op jit(solution)/shard_map/ppermute | solution.py:603
  25.7 37.8 %collective-permute-start.12 = (bf16[192,2304]{1,0:T(8,128)(2,1)}, bf16[192,2304]{1,0:T(8,128)(2,1)S(1)}, u32[]{:S(2)}, u32[]{:S(2)}) collective-permute-start(bf16[192,2304]{1,0:T(8,128)(2,1)} %get-tuple-element.149), channel_id=1, source_target_pairs={{0,18},{1,19},{2,16},{3,17},{4,22},{5,23},{6,20},{7,21},{8,26},{9,... | collective-permute-start | bytes 2654216 | tf_op jit(solution)/shard_map/ppermute | solution.py:603
  26.1 1.7 copy-start.27
  63.5 2.7 %copy-start.8 = (bf16[72,6272]{1,0:T(8,128)(2,1)}, bf16[72,6272]{1,0:T(8,128)(2,1)S(1)}, u32[]{:S(2)}) copy-start(bf16[72,6272]{1,0:T(8,128)(2,1)S(1)} %collective-permute-done.14.refs_2_) | copy-start | bytes 2709508
  63.6 16.6 %collective-permute-start.21 = (bf16[48,6272]{1,0:T(8,128)(2,1)S(1)}, bf16[48,6272]{1,0:T(8,128)(2,1)S(1)}, u32[]{:S(2)}, u32[]{:S(2)}) collective-permute-start(bf16[48,6272]{1,0:T(8,128)(2,1)S(1)} %slice.124), channel_id=1, source_target_pairs={{0,2},{1,3},{2,0},{3,1},{4,6},{5,7},{6,4},{7,5},{8,10},{9,11},{10,... | collective-permute-start | bytes 1806344 | tf_op jit(solution)/shard_map/ppermute | solution.py:58
  65.2 5.2 %collective-permute-start.15 = (bf16[192,2304]{1,0:T(8,128)(2,1)}, bf16[192,2304]{1,0:T(8,128)(2,1)S(1)}, u32[]{:S(2)}, u32[]{:S(2)}) collective-permute-start(bf16[192,2304]{1,0:T(8,128)(2,1)} %collective-permute-done.10), channel_id=1, source_target_pairs={{0,1},{1,0},{2,3},{3,2},{4,5},{5,4},{6,7},{7,6},{8,9},{9,8},{10,11... | collective-permute-start | bytes 2654216 | tf_op jit(solution)/shard_map/ppermute | solution.py:58
  65.2 6.3 %collective-permute-start.16 = (bf16[192,2304]{1,0:T(8,128)(2,1)}, bf16[192,2304]{1,0:T(8,128)(2,1)S(1)}, u32[]{:S(2)}, u32[]{:S(2)}) collective-permute-start(bf16[192,2304]{1,0:T(8,128)(2,1)} %collective-permute-done.11), channel_id=1, source_target_pairs={{0,1},{1,0},{2,3},{3,2},{4,5},{5,4},{6,7},{7,6},{8,9},{9,8},{10,11... | collective-permute-start | bytes 2654216 | tf_op jit(solution)/shard_map/ppermute | solution.py:58
  65.7 7.9 %collective-permute-start.17 = (bf16[192,2304]{1,0:T(8,128)(2,1)S(1)}, bf16[192,2304]{1,0:T(8,128)(2,1)S(1)}, u32[]{:S(2)}, u32[]{:S(2)}) collective-permute-start(bf16[192,2304]{1,0:T(8,128)(2,1)S(1)} %collective-permute-done.12), channel_id=1, source_target_pairs={{0,1},{1,0},{2,3},{3,2},{4,5},{5,4},{6,7},{7,6},{8,9},{9,8},{10,11... | collective-permute-start | bytes 2654216 | tf_op jit(solution)/shard_map/ppermute | solution.py:58
  67.9 1.7 copy-start.31
  69.6 1.9 copy-start.12
  69.6 35.0 %collective-permute-start.18 = (bf16[72,6272]{1,0:T(8,128)(2,1)S(1)}, bf16[72,6272]{1,0:T(8,128)(2,1)S(1)}, u32[]{:S(2)}, u32[]{:S(2)}) collective-permute-start(bf16[72,6272]{1,0:T(8,128)(2,1)S(1)} %copy-done.31), channel_id=1, source_target_pairs={{0,12},{1,13},{2,14},{3,15},{4,8},{5,9},{6,10},{7,11},{8,4},{9,5},... | collective-permute-start | bytes 2709512 | tf_op jit(solution)/shard_map/ppermute | solution.py:58
  71.0 22.1 %collective-permute-start.20 = (bf16[48,6272]{1,0:T(8,128)(2,1)S(1)}, bf16[48,6272]{1,0:T(8,128)(2,1)S(1)}, u32[]{:S(2)}, u32[]{:S(2)}) collective-permute-start(bf16[48,6272]{1,0:T(8,128)(2,1)S(1)} %slice.123), channel_id=1, source_target_pairs={{0,2},{1,3},{2,0},{3,1},{4,6},{5,7},{6,4},{7,5},{8,10},{9,11},{10,... | collective-permute-start | bytes 1806344 | tf_op jit(solution)/shard_map/ppermute | solution.py:58
  71.6 32.1 %collective-permute-start.19 = (bf16[48,6272]{1,0:T(8,128)(2,1)S(1)}, bf16[48,6272]{1,0:T(8,128)(2,1)S(1)}, u32[]{:S(2)}, u32[]{:S(2)}) collective-permute-start(bf16[48,6272]{1,0:T(8,128)(2,1)S(1)} %copy-done.12), channel_id=1, source_target_pairs={{0,2},{1,3},{2,0},{3,1},{4,6},{5,7},{6,4},{7,5},{8,10},{9,11},{10,... | collective-permute-start | bytes 1806344 | tf_op jit(solution)/shard_map/ppermute | solution.py:58
  73.6 43.6 %copy-start.30 = (f32[1,384]{1,0:T(1,128)S(1)}, f32[1,384]{1,0:T(1,128)}, u32[]{:S(2)}) copy-start(f32[1,384]{1,0:T(1,128)} %get-tuple-element.172) | copy-start | bytes 4612
  104.6 1.1 copy-start.10
  106.5 27.5 %collective-permute-start.23 = (bf16[48,6272]{1,0:T(8,128)(2,1)}, bf16[48,6272]{1,0:T(8,128)(2,1)}, u32[]{:S(2)}, u32[]{:S(2)}) collective-permute-start(bf16[48,6272]{1,0:T(8,128)(2,1)} %slice.125), channel_id=1, source_target_pairs={{0,2},{1,3},{2,0},{3,1},{4,6},{5,7},{6,4},{7,5},{8,10},{9,11},{10,... | collective-permute-start | bytes 1806344 | tf_op jit(solution)/shard_map/ppermute | solution.py:58
  109.0 24.9 %collective-permute-start.22 = (bf16[640,512]{1,0:T(8,128)(2,1)}, bf16[640,512]{1,0:T(8,128)(2,1)}, u32[]{:S(2)}, u32[]{:S(2)}) collective-permute-start(bf16[640,512]{1,0:T(8,128)(2,1)} %dynamic-slice_convert_fusion.2), channel_id=1, source_target_pairs={{0,4},{1,5},{2,6},{3,7},{4,0},{5,1},{6,2},{7,3},{8,12},{9,13},{10,... | collective-permute-start | bytes 1966088 | tf_op jit(solution)/shard_map/ppermute | solution.py:58
  117.2 3.6 %collective-permute-start.24 = (f32[1,384]{1,0:T(1,128)S(1)}, f32[1,384]{1,0:T(1,128)S(1)}, u32[]{:S(2)}, u32[]{:S(2)}) collective-permute-start(f32[1,384]{1,0:T(1,128)S(1)} %fusion.41), channel_id=1, source_target_pairs={{0,16},{16,0},{1,17},{17,1},{2,18},{18,2},{3,19},{19,3},{4,20},{20... | collective-permute-start | bytes 4616 | tf_op jit(solution)/shard_map/ppermute | solution.py:58
  120.9 1.2 collective-permute-start.25
  122.0 11.9 %collective-permute-start.26 = (f32[1,384]{1,0:T(1,128)S(1)}, f32[1,384]{1,0:T(1,128)S(1)}, u32[]{:S(2)}, u32[]{:S(2)}) collective-permute-start(f32[1,384]{1,0:T(1,128)S(1)} %add.295), channel_id=1, source_target_pairs={{0,2},{1,3},{2,0},{3,1},{4,6},{5,7},{6,4},{7,5},{8,10},{9,11},{10,... | collective-permute-start | bytes 4616 | tf_op jit(solution)/shard_map/ppermute | solution.py:58
  123.6 1.2 copy-start.9
  124.7 1.2 copy-start.11
  134.0 22.3 %collective-permute-start.28 = (bf16[432,6272]{1,0:T(8,128)(2,1)}, bf16[432,6272]{1,0:T(8,128)(2,1)}, u32[]{:S(2)}, u32[]{:S(2)}) collective-permute-start(bf16[432,6272]{1,0:T(8,128)(2,1)} %shard_map.130.refs_0_), channel_id=1, source_target_pairs={{0,1},{1,0},{2,3},{3,2},{4,5},{5,4},{6,7},{7,6},{8,9},{9,8},{10,11... | collective-permute-start | bytes 16257032 | tf_op jit(solution)/shard_map/ppermute | solution.py:58
  137.6 1.5 copy-start.28
  138.5 17.8 %collective-permute-start.29 = (bf16[48,6272]{1,0:T(8,128)(2,1)}, bf16[48,6272]{1,0:T(8,128)(2,1)S(1)}, u32[]{:S(2)}, u32[]{:S(2)}) collective-permute-start(bf16[48,6272]{1,0:T(8,128)(2,1)} %collective-permute-done.23.refs_1_), channel_id=1, source_target_pairs={{0,1},{1,0},{2,3},{3,2},{4,5},{5,4},{6,7},{7,6},{8,9},{9,8},{10,11... | collective-permute-start | bytes 1806344 | tf_op jit(solution)/shard_map/ppermute | solution.py:58
  139.0 17.3 %collective-permute-start.27 = (bf16[320,512]{1,0:T(8,128)(2,1)}, bf16[320,512]{1,0:T(8,128)(2,1)S(1)}, u32[]{:S(2)}, u32[]{:S(2)}) collective-permute-start(bf16[320,512]{1,0:T(8,128)(2,1)} %copy-done.21), channel_id=1, source_target_pairs={{0,8},{1,9},{2,10},{3,11},{4,12},{5,13},{6,14},{7,15},{8,0},{9,1},... | collective-permute-start | bytes 983048 | tf_op jit(solution)/shard_map/ppermute | solution.py:58
  158.5 17.1 %collective-permute-start.31 = (bf16[320,512]{1,0:T(8,128)(2,1)S(1)}, bf16[320,512]{1,0:T(8,128)(2,1)S(1)}, u32[]{:S(2)}, u32[]{:S(2)}) collective-permute-start(bf16[320,512]{1,0:T(8,128)(2,1)S(1)} %get-tuple-element.204.refs_0_), channel_id=1, source_target_pairs={{0,2},{1,3},{2,0},{3,1},{4,6},{5,7},{6,4},{7,5},{8,10},{9,11},{10,... | collective-permute-start | bytes 983048 | tf_op jit(solution)/shard_map/ppermute | solution.py:58
  159.1 16.6 %collective-permute-start.30 = (bf16[320,512]{1,0:T(8,128)(2,1)S(1)}, bf16[320,512]{1,0:T(8,128)(2,1)S(1)}, u32[]{:S(2)}, u32[]{:S(2)}) collective-permute-start(bf16[320,512]{1,0:T(8,128)(2,1)S(1)} %get-tuple-element.204.refs_0_), channel_id=1, source_target_pairs={{0,8},{1,9},{2,10},{3,11},{4,12},{5,13},{6,14},{7,15},{8,0},{9,1},... | collective-permute-start | bytes 983048 | tf_op jit(solution)/shard_map/ppermute | solution.py:58
  159.1 16.5 %collective-permute-start.32 = (f32[1,320]{1,0:T(1,128)S(1)}, f32[1,320]{1,0:T(1,128)S(1)}, u32[]{:S(2)}, u32[]{:S(2)}) collective-permute-start(f32[1,320]{1,0:T(1,128)S(1)} %get-tuple-element.188), channel_id=1, source_target_pairs={{0,8},{1,9},{2,10},{3,11},{4,12},{5,13},{6,14},{7,15},{8,0},{9,1},... | collective-permute-start | bytes 3848 | tf_op jit(solution)/shard_map/ppermute | solution.py:58
  163.7 18.0 %copy-start.29 = (s32[32,1]{0,1:T(1,128)S(1)}, s32[32,1]{0,1:T(1,128)}, u32[]{:S(2)}) copy-start(s32[32,1]{0,1:T(1,128)} %param.19) | copy-start | bytes 388
  175.7 19.6 %collective-permute-start.37 = (f32[2,320]{1,0:T(2,128)S(1)}, f32[2,320]{1,0:T(2,128)S(1)}, u32[]{:S(2)}, u32[]{:S(2)}) collective-permute-start(f32[2,320]{1,0:T(2,128)S(1)} %broadcast_select_fusion.3), channel_id=1, source_target_pairs={{0,6},{1,7},{2,4},{3,5},{4,2},{5,3},{6,0},{7,1},{8,14},{9,15},{10,... | collective-permute-start | bytes 7688 | tf_op jit(solution)/shard_map/ppermute | solution.py:58
  175.9 19.4 %collective-permute-start.36 = (f32[2,320]{1,0:T(2,128)S(1)}, f32[2,320]{1,0:T(2,128)S(1)}, u32[]{:S(2)}, u32[]{:S(2)}) collective-permute-start(f32[2,320]{1,0:T(2,128)S(1)} %broadcast_select_fusion.3), channel_id=1, source_target_pairs={{0,2},{1,3},{2,0},{3,1},{4,6},{5,7},{6,4},{7,5},{8,10},{9,11},{10,... | collective-permute-start | bytes 7688 | tf_op jit(solution)/shard_map/ppermute | solution.py:58
  177.3 18.1 %collective-permute-start.35 = (f32[2,320]{1,0:T(2,128)S(1)}, f32[2,320]{1,0:T(2,128)S(1)}, u32[]{:S(2)}, u32[]{:S(2)}) collective-permute-start(f32[2,320]{1,0:T(2,128)S(1)} %broadcast_select_fusion.3), channel_id=1, source_target_pairs={{0,4},{1,5},{2,6},{3,7},{4,0},{5,1},{6,2},{7,3},{8,12},{9,13},{10,... | collective-permute-start | bytes 7688 | tf_op jit(solution)/shard_map/ppermute | solution.py:58
  179.2 16.4 %collective-permute-start.34 = (bf16[320,512]{1,0:T(8,128)(2,1)S(1)}, bf16[320,512]{1,0:T(8,128)(2,1)S(1)}, u32[]{:S(2)}, u32[]{:S(2)}) collective-permute-start(bf16[320,512]{1,0:T(8,128)(2,1)S(1)} %collective-permute-done.30.refs_1_), channel_id=1, source_target_pairs={{0,2},{1,3},{2,0},{3,1},{4,6},{5,7},{6,4},{7,5},{8,10},{9,11},{10,... | collective-permute-start | bytes 983048 | tf_op jit(solution)/shard_map/ppermute | solution.py:58
  181.6 15.8 %collective-permute-start.33 = (bf16[640,512]{1,0:T(8,128)(2,1)}, bf16[640,512]{1,0:T(8,128)(2,1)S(1)}, u32[]{:S(2)}, u32[]{:S(2)}) collective-permute-start(bf16[640,512]{1,0:T(8,128)(2,1)} %pad_maximum_fusion), channel_id=1, source_target_pairs={{0,4},{1,5},{2,6},{3,7},{4,0},{5,1},{6,2},{7,3},{8,12},{9,13},{10,... | collective-permute-start | bytes 1966088 | tf_op jit(solution)/shard_map/ppermute | solution.py:58
  197.4 14.6 %collective-permute-start.43 = (bf16[640,512]{1,0:T(8,128)(2,1)S(1)}, bf16[640,512]{1,0:T(8,128)(2,1)S(1)}, u32[]{:S(2)}, u32[]{:S(2)}) collective-permute-start(bf16[640,512]{1,0:T(8,128)(2,1)S(1)} %collective-permute-done.33.refs_2_), channel_id=1, source_target_pairs={{0,2},{1,3},{2,0},{3,1},{4,6},{5,7},{6,4},{7,5},{8,10},{9,11},{10,... | collective-permute-start | bytes 1966088 | tf_op jit(solution)/shard_map/ppermute | solution.py:58
  197.9 8.4 %collective-permute-start.40 = (bf16[640,512]{1,0:T(8,128)(2,1)S(1)}, bf16[640,512]{1,0:T(8,128)(2,1)S(1)}, u32[]{:S(2)}, u32[]{:S(2)}) collective-permute-start(bf16[640,512]{1,0:T(8,128)(2,1)S(1)} %collective-permute-done.33.refs_2_), channel_id=1, source_target_pairs={{0,1},{1,0},{2,3},{3,2},{4,5},{5,4},{6,7},{7,6},{8,9},{9,8},{10,11... | collective-permute-start | bytes 1966088 | tf_op jit(solution)/shard_map/ppermute | solution.py:58
  197.9 6.3 %collective-permute-start.38 = (bf16[320,512]{1,0:T(8,128)(2,1)S(1)}, bf16[320,512]{1,0:T(8,128)(2,1)}, u32[]{:S(2)}, u32[]{:S(2)}) collective-permute-start(bf16[320,512]{1,0:T(8,128)(2,1)S(1)} %get-tuple-element.204.refs_0_), channel_id=1, source_target_pairs={{0,1},{1,0},{2,3},{3,2},{4,5},{5,4},{6,7},{7,6},{8,9},{9,8},{10,11... | collective-permute-start | bytes 983048 | tf_op jit(solution)/shard_map/ppermute | solution.py:58
  198.4 2.1 collective-permute-start.44
  200.5 3.7 %collective-permute-start.45 = (f32[2,4,320]{2,1,0:T(4,128)S(1)}, f32[2,4,320]{2,1,0:T(4,128)S(1)}, u32[]{:S(2)}, u32[]{:S(2)}) collective-permute-start(f32[2,4,320]{2,1,0:T(4,128)S(1)} %add.302), channel_id=1, source_target_pairs={{0,16},{16,0},{1,17},{17,1},{2,18},{18,2},{3,19},{19,3},{4,20},{20... | collective-permute-start | bytes 30728 | tf_op jit(solution)/shard_map/ppermute | solution.py:58
  202.2 2.8 %collective-permute-start.39 = (bf16[320,512]{1,0:T(8,128)(2,1)S(1)}, bf16[320,512]{1,0:T(8,128)(2,1)S(1)}, u32[]{:S(2)}, u32[]{:S(2)}) collective-permute-start(bf16[320,512]{1,0:T(8,128)(2,1)S(1)} %collective-permute-done.30.refs_1_), channel_id=1, source_target_pairs={{0,1},{1,0},{2,3},{3,2},{4,5},{5,4},{6,7},{7,6},{8,9},{9,8},{10,11... | collective-permute-start | bytes 983048 | tf_op jit(solution)/shard_map/ppermute | solution.py:58
  204.2 1.6 collective-permute-start.41
  204.2 2.1 collective-permute-start.42
  212.0 2.1 collective-permute-start.46
  (10 other events, 9.4 us)

commit v7 on v6

--- a/solution.py
+++ b/solution.py
@@ -14,7 +14,7 @@
 PASSED_ON = 48
 TAGS = 128
 STRIP = 512
-UNROLL, KEYS_UNROLL = 2, 5
+UNROLL, KEYS_UNROLL = 2, 10
 EXTRA = 16
 CHUNK = 64
 KEYS_MIB, PRODUCTS_MIB, FINISH_MIB, STACK_MIB, PLACE_MIB, SLOTS_MIB = 56, 20, 8, 20, 36, 44
@@ -662,12 +662,12 @@
             total = halve(total, bit)
         return jnp.zeros((), F32), state[1] + total
 
+    held[last] = across_learn(packs[-1], 4 * last)
+    for k in range(last):
+        passed[k] = over_y(held[k])
     total = 0.0
     for part in [operands[0], *gathered]:
         total = total + products(part) + products(across_learn(part, 1))
-    held[last] = across_learn(packs[-1], 4 * last)
-    for k in range(last):
-        passed[k] = over_y(held[k])
     total, held, passed = barrier((total, held, passed))
 
     values = [sums]

time: 217 us -> 216 us (level)
  no operation moved by 1% of the time
where the time goes in v7:
time: 216 us; the launch traced here: 215 us
  waiting for transfers between devices  92.7 us (43%)
  Pallas kernels  53.4 us (25%)
  starting transfers between devices  37.5 us (17%)
  local copies, waits for them, and re-layouts  18.5 us (9%)
  matrix products  7.71 us (4%)
  other arithmetic  3 us (1%)
    ppermute x35, waiting for transfers between devices, swap(): return lax.ppermute(x, axis, [(i, i ^ bit) for i in range(size)])  57.6 us
    ppermute x3, waiting for transfers between devices, gather(): return lax.ppermute(operands[k], BOTH, pairs)  35.1 us
    ppermute x35, starting transfers between devices, swap(): return lax.ppermute(x, axis, [(i, i ^ bit) for i in range(size)])  34 us
    pallas_call x1, Pallas kernels, body(): pl.pallas_call(functools.partial(keys_kernel, blocks, (planes, packet, pa...  14.1 us
    pallas_call x1, Pallas kernels, body(): pl.pallas_call(slots_kernel, out_shape=jax.ShapeDtypeStruct((SLOTS * TILE...  13.3 us
    unnamed x40, local copies, waits for them, and re-layouts  11.8 us
    pallas_call x1, Pallas kernels, body(): pl.pallas_call(functools.partial(place_kernel, len(stacks)), out_shape=[j...  11.3 us
    dot_general x8, matrix products, dot_rows(): lax.dot_general(a, b, (((0,), (0,)), ((), ())), preferred_element_type=F32)  7.71 us
  transfers between devices with their start and end apart: 38, of which 17 were waited for; matrix products, arithmetic and copies ran while one was open for 7% of the time, Pallas kernels for 16%

profile of v7, /device:TPU:0, one launch (start us, length us, event | category | flops | bytes accessed | tf_op | source)
XLA Modules:
  0.0 215.4 jit_solution(12675778814228089178)
XLA Ops:
  1.3 14.1 %shard_map.129 = (bf16[192,2304]{1,0:T(8,128)(2,1)}, bf16[192,2304]{1,0:T(8,128)(2,1)}, bf16[192,2304]{1,0:T(8,128)(2,1)}, bf16[192,2304]{1,0:T(8,128)(2,1)}, bf...) custom-call(s32[5]{0:T(128)} %stack.47.index_ref, ...), custom_call_target="tpu_custom_call" | custom-call | flops 2684354560 | bytes 16777216 | tf_op jit(solution)/shard_map/pallas_call | solution.py:547
  15.9 2.7 %collective-permute-start.13 = (bf16[72,6272]{1,0:T(8,128)(2,1)}, bf16[72,6272]{1,0:T(8,128)(2,1)S(1)}, u32[]{:S(2)}, u32[]{:S(2)}) collective-permute-start(bf16[72,6272]{1,0:T(8,128)(2,1)} %get-tuple-element.151), channel_id=1, source_target_pairs={{0,4},{1,5},{2,6},{3,7},{4,0},{5,1},{6,2},{7,3},{8,12},{9,13},{10,... | collective-permute-start | bytes 2709512 | tf_op jit(solution)/shard_map/ppermute | solution.py:58
  18.5 2.6 %collective-permute-start.14 = (bf16[72,6272]{1,0:T(8,128)(2,1)}, bf16[72,6272]{1,0:T(8,128)(2,1)S(1)}, u32[]{:S(2)}, u32[]{:S(2)}) collective-permute-start(bf16[72,6272]{1,0:T(8,128)(2,1)} %get-tuple-element.152), channel_id=1, source_target_pairs={{0,8},{1,9},{2,10},{3,11},{4,12},{5,13},{6,14},{7,15},{8,0},{9,1},... | collective-permute-start | bytes 2709512 | tf_op jit(solution)/shard_map/ppermute | solution.py:58
  21.1 1.5 collective-permute-start.10
  22.7 1.5 collective-permute-start.11
  25.5 1.7 fusion.23
  27.8 15.3 %collective-permute-done.10 = bf16[192,2304]{1,0:T(8,128)(2,1)} collective-permute-done((bf16[192,2304]{1,0:T(8,128)(2,1)}, bf16[192,2304]{1,0:T(8,128)(2,1)}, u32[]{:S(2)}, u32[]{:S(2)}) %collective-permute-start.10) | collective-permute-done | bytes 884768 | tf_op jit(solution)/shard_map/ppermute | solution.py:603
  43.1 2.4 %collective-permute-done.11 = bf16[192,2304]{1,0:T(8,128)(2,1)} collective-permute-done((bf16[192,2304]{1,0:T(8,128)(2,1)}, bf16[192,2304]{1,0:T(8,128)(2,1)}, u32[]{:S(2)}, u32[]{:S(2)}) %collective-permute-start.11) | collective-permute-done | bytes 884768 | tf_op jit(solution)/shard_map/ppermute | solution.py:603
  45.5 17.4 %collective-permute-done.12 = bf16[192,2304]{1,0:T(8,128)(2,1)S(1)} collective-permute-done((bf16[192,2304]{1,0:T(8,128)(2,1)}, bf16[192,2304]{1,0:T(8,128)(2,1)S(1)}, u32[]{:S(2)}, u32[]{:S(2)}) %collective-permute-start.12) | collective-permute-done | bytes 884768 | tf_op jit(solution)/shard_map/ppermute | solution.py:603
  63.0 1.6 collective-permute-start.21
  65.7 1.6 convolution_add_fusion.3
  67.3 1.7 fusion.20
  71.0 1.5 collective-permute-start.19
  73.6 6.0 %collective-permute-done.21.refs_7_ = bf16[48,6272]{1,0:T(8,128)(2,1)S(1)} collective-permute-done((bf16[48,6272]{1,0:T(8,128)(2,1)S(1)}, bf16[48,6272]{1,0:T(8,128)(2,1)S(1)}, u32[]{:S(2)}, u32[]{:S(2)}) %collective-permute-start.21) | collective-permute-done | bytes 602144 | tf_op jit(solution)/shard_map/ppermute | solution.py:58
  80.4 12.1 %collective-permute-done.20.refs_6_ = bf16[48,6272]{1,0:T(8,128)(2,1)S(1)} collective-permute-done((bf16[48,6272]{1,0:T(8,128)(2,1)S(1)}, bf16[48,6272]{1,0:T(8,128)(2,1)S(1)}, u32[]{:S(2)}, u32[]{:S(2)}) %collective-permute-start.20) | collective-permute-done | bytes 602144 | tf_op jit(solution)/shard_map/ppermute | solution.py:58
  93.4 9.8 %collective-permute-done.19.refs_5_ = bf16[48,6272]{1,0:T(8,128)(2,1)S(1)} collective-permute-done((bf16[48,6272]{1,0:T(8,128)(2,1)S(1)}, bf16[48,6272]{1,0:T(8,128)(2,1)S(1)}, u32[]{:S(2)}, u32[]{:S(2)}) %collective-permute-start.19) | collective-permute-done | bytes 602144 | tf_op jit(solution)/shard_map/ppermute | solution.py:58
  104.2 0.9 slice.125
  105.9 1.6 collective-permute-start.23
  107.5 0.9 dynamic-slice_convert_fusion.2
  108.4 6.4 %collective-permute-start.22 = (bf16[640,512]{1,0:T(8,128)(2,1)}, bf16[640,512]{1,0:T(8,128)(2,1)}, u32[]{:S(2)}, u32[]{:S(2)}) collective-permute-start(bf16[640,512]{1,0:T(8,128)(2,1)} %dynamic-slice_convert_fusion.2), channel_id=1, source_target_pairs={{0,4},{1,5},{2,6},{3,7},{4,0},{5,1},{6,2},{7,3},{8,12},{9,13},{10,... | collective-permute-start | bytes 1966088 | tf_op jit(solution)/shard_map/ppermute | solution.py:58
  116.6 1.6 collective-permute-start.24
  118.2 2.1 collective-permute-done.24
  120.3 1.1 collective-permute-done.25
  121.5 1.5 collective-permute-start.26
  123.0 1.2 copy-done.9
  124.1 1.2 copy-done.11
  125.3 1.1 copy-done.13
  126.4 1.1 copy-done.15
  127.5 1.1 copy-done.17
  128.5 1.1 copy-done.19
  129.6 1.0 copy-done.20
  130.6 2.8 %shard_map.130.refs_0_ = bf16[432,6272]{1,0:T(8,128)(2,1)} custom-call(bf16[48,6272]{1,0:T(8,128)(2,1)S(1)} %copy-done.13, bf16[72,6272]{1,0:T(8,128)(2,1)S(1)} %collective-permute-done.13.refs_1_, bf16[72,6272]{1,0:T(8,128)(2,1)S(1)} %copy-done.9, bf16[72,6272]{1,0:T(8,128)(2,1)S(1)} %copy-done.11, bf16[24,6272]{1,0:T(8,128)(2,1)S(1)} %copy-done.20, ...), custom_call_target="tpu_custom_call" | custom-call | tf_op jit(solution)/shard_map/pallas_call | solution.py:631
  134.2 2.1 shard_map.131
  138.5 17.0 %collective-permute-done.27.other_ref = bf16[320,512]{1,0:T(8,128)(2,1)S(1)} collective-permute-done((bf16[320,512]{1,0:T(8,128)(2,1)}, bf16[320,512]{1,0:T(8,128)(2,1)S(1)}, u32[]{:S(2)}, u32[]{:S(2)}) %collective-permute-start.27) | collective-permute-done | bytes 327712 | tf_op jit(solution)/shard_map/ppermute | solution.py:58
  155.5 2.2 %shard_map.132 = (bf16[320,512]{1,0:T(8,128)(2,1)S(1)}, f32[1,320]{1,0:T(1,128)S(1)}) custom-call(s32[2]{0:T(128)S(1)} %get-tuple-element.250.index_ref, f32[320,512]{1,0:T(8,128)} %get-tuple-element.185.kept_ref, bf16[320,512]{1,0:T(8,128)(2,1)S(1)} %collective-permute-done.27.other_ref, bf16[5120,1024]{1,0:T(8,128)(2,1)} %w_ref.3, ...), custom_call_target="tpu_custom_call" | custom-call | tf_op jit(solution)/shard_map/pallas_call | solution.py:720
  158.3 2.9 %collective-permute-start.32 = (f32[1,320]{1,0:T(1,128)S(1)}, f32[1,320]{1,0:T(1,128)S(1)}, u32[]{:S(2)}, u32[]{:S(2)}) collective-permute-start(f32[1,320]{1,0:T(1,128)S(1)} %get-tuple-element.188), channel_id=1, source_target_pairs={{0,8},{1,9},{2,10},{3,11},{4,12},{5,13},{6,14},{7,15},{8,0},{9,1},... | collective-permute-start | bytes 3848 | tf_op jit(solution)/shard_map/ppermute | solution.py:58
  162.9 11.3 %shard_map.133 = (bf16[512,5120]{1,0:T(8,128)(2,1)}, bf16[512,1024]{1,0:T(8,128)(2,1)S(1)}) custom-call(s32[1]{0:T(128)} %bitcast.12.me_ref, bf16[432,6272]{1,0:T(8,128)(2,1)} %shard_map.130.refs_0_, bf16[48,6272]{1,0:T(8,128)(2,1)} %collective-permute-done.23.refs_1_, bf16[432,6272]{1,0:T(8,128)(2,1)} %collective-permute-done.28.refs_2_, ...), custom_call_target="tpu_custom_call" | custom-call | tf_op jit(solution)/shard_map/pallas_call | solution.py:745
  175.1 1.4 collective-permute-start.36
  176.5 1.9 collective-permute-start.35
  178.4 1.5 collective-permute-start.34
  181.2 13.3 %shard_map.134 = bf16[512,5120]{1,0:T(8,128)(2,1)} custom-call(f32[1]{0:T(128)} %bitcast.23.over_ref, bf16[512,5120]{1,0:T(8,128)(2,1)} %get-tuple-element.201.rows_ref, bf16[512,1024]{1,0:T(8,128)(2,1)S(1)} %get-tuple-element.202.keys_ref, bf16[5120,1024]{1,0:T(8,128)(2,1)} %get-tuple-element.357, f32[1,5120]{1,0:T(1,128)S(1)} %bitcast.37), custom_call_target="tpu_custom_call" | custom-call | tf_op jit(solution)/shard_map/pallas_call | solution.py:785
  194.8 1.8 collective-permute-done.33.refs_2_
  197.7 2.0 collective-permute-done.44
  199.7 1.5 collective-permute-start.45
  201.4 2.0 collective-permute-done.45
  205.5 5.4 %shard_map.135.refs_2_ = f32[2560,1024]{1,0:T(8,128)} custom-call(s32[7]{0:T(128)S(1)} %pad_add_fusion.3.index_ref, bf16[320,512]{1,0:T(8,128)(2,1)S(1)} %get-tuple-element.204.refs_0_, bf16[320,512]{1,0:T(8,128)(2,1)S(1)} %collective-permute-done.30.refs_1_, bf16[640,512]{1,0:T(8,128)(2,1)S(1)} %collective-permute-done.33.refs_2_, ...), custom_call_target="tpu_custom_call" | custom-call | bytes 11796480 | tf_op jit(solution)/shard_map/pallas_call | solution.py:474
  212.0 1.3 collective-permute-done.46.refs_1_
  213.3 2.1 shard_map.136
  (146 shorter events, 23.8 us)
Async XLA Ops:
  15.4 8.8 %collective-permute-start.9 = (bf16[192,2304]{1,0:T(8,128)(2,1)}, bf16[192,2304]{1,0:T(8,128)(2,1)S(1)}, u32[]{:S(2)}, u32[]{:S(2)}) collective-permute-start(bf16[192,2304]{1,0:T(8,128)(2,1)} %get-tuple-element.146), channel_id=1, source_target_pairs={{0,1},{1,0},{2,3},{3,2},{4,5},{5,4},{6,7},{7,6},{8,9},{9,8},{10,11... | collective-permute-start | bytes 2654216 | tf_op jit(solution)/shard_map/ppermute | solution.py:58
  15.9 47.0 %collective-permute-start.13 = (bf16[72,6272]{1,0:T(8,128)(2,1)}, bf16[72,6272]{1,0:T(8,128)(2,1)S(1)}, u32[]{:S(2)}, u32[]{:S(2)}) collective-permute-start(bf16[72,6272]{1,0:T(8,128)(2,1)} %get-tuple-element.151), channel_id=1, source_target_pairs={{0,4},{1,5},{2,6},{3,7},{4,0},{5,1},{6,2},{7,3},{8,12},{9,13},{10,... | collective-permute-start | bytes 2709512 | tf_op jit(solution)/shard_map/ppermute | solution.py:58
  18.5 44.4 %collective-permute-start.14 = (bf16[72,6272]{1,0:T(8,128)(2,1)}, bf16[72,6272]{1,0:T(8,128)(2,1)S(1)}, u32[]{:S(2)}, u32[]{:S(2)}) collective-permute-start(bf16[72,6272]{1,0:T(8,128)(2,1)} %get-tuple-element.152), channel_id=1, source_target_pairs={{0,8},{1,9},{2,10},{3,11},{4,12},{5,13},{6,14},{7,15},{8,0},{9,1},... | collective-permute-start | bytes 2709512 | tf_op jit(solution)/shard_map/ppermute | solution.py:58
  21.1 22.0 %collective-permute-start.10 = (bf16[192,2304]{1,0:T(8,128)(2,1)}, bf16[192,2304]{1,0:T(8,128)(2,1)}, u32[]{:S(2)}, u32[]{:S(2)}) collective-permute-start(bf16[192,2304]{1,0:T(8,128)(2,1)} %get-tuple-element.147), channel_id=1, source_target_pairs={{0,2},{1,3},{2,0},{3,1},{4,6},{5,7},{6,4},{7,5},{8,10},{9,11},{10,... | collective-permute-start | bytes 2654216 | tf_op jit(solution)/shard_map/ppermute | solution.py:603
  22.7 22.9 %collective-permute-start.11 = (bf16[192,2304]{1,0:T(8,128)(2,1)}, bf16[192,2304]{1,0:T(8,128)(2,1)}, u32[]{:S(2)}, u32[]{:S(2)}) collective-permute-start(bf16[192,2304]{1,0:T(8,128)(2,1)} %get-tuple-element.148), channel_id=1, source_target_pairs={{0,16},{1,17},{2,18},{3,19},{4,20},{5,21},{6,22},{7,23},{8,24},{9,... | collective-permute-start | bytes 2654216 | tf_op jit(solution)/shard_map/ppermute | solution.py:603
  25.1 37.9 %collective-permute-start.12 = (bf16[192,2304]{1,0:T(8,128)(2,1)}, bf16[192,2304]{1,0:T(8,128)(2,1)S(1)}, u32[]{:S(2)}, u32[]{:S(2)}) collective-permute-start(bf16[192,2304]{1,0:T(8,128)(2,1)} %get-tuple-element.149), channel_id=1, source_target_pairs={{0,18},{1,19},{2,16},{3,17},{4,22},{5,23},{6,20},{7,21},{8,26},{9,... | collective-permute-start | bytes 2654216 | tf_op jit(solution)/shard_map/ppermute | solution.py:603
  25.5 1.7 copy-start.27
  62.9 2.8 %copy-start.8 = (bf16[72,6272]{1,0:T(8,128)(2,1)}, bf16[72,6272]{1,0:T(8,128)(2,1)S(1)}, u32[]{:S(2)}) copy-start(bf16[72,6272]{1,0:T(8,128)(2,1)S(1)} %collective-permute-done.14.refs_2_) | copy-start | bytes 2709508
  63.0 16.6 %collective-permute-start.21 = (bf16[48,6272]{1,0:T(8,128)(2,1)S(1)}, bf16[48,6272]{1,0:T(8,128)(2,1)S(1)}, u32[]{:S(2)}, u32[]{:S(2)}) collective-permute-start(bf16[48,6272]{1,0:T(8,128)(2,1)S(1)} %slice.124), channel_id=1, source_target_pairs={{0,2},{1,3},{2,0},{3,1},{4,6},{5,7},{6,4},{7,5},{8,10},{9,11},{10,... | collective-permute-start | bytes 1806344 | tf_op jit(solution)/shard_map/ppermute | solution.py:58
  64.6 5.2 %collective-permute-start.15 = (bf16[192,2304]{1,0:T(8,128)(2,1)}, bf16[192,2304]{1,0:T(8,128)(2,1)S(1)}, u32[]{:S(2)}, u32[]{:S(2)}) collective-permute-start(bf16[192,2304]{1,0:T(8,128)(2,1)} %collective-permute-done.10), channel_id=1, source_target_pairs={{0,1},{1,0},{2,3},{3,2},{4,5},{5,4},{6,7},{7,6},{8,9},{9,8},{10,11... | collective-permute-start | bytes 2654216 | tf_op jit(solution)/shard_map/ppermute | solution.py:58
  64.6 6.3 %collective-permute-start.16 = (bf16[192,2304]{1,0:T(8,128)(2,1)}, bf16[192,2304]{1,0:T(8,128)(2,1)S(1)}, u32[]{:S(2)}, u32[]{:S(2)}) collective-permute-start(bf16[192,2304]{1,0:T(8,128)(2,1)} %collective-permute-done.11), channel_id=1, source_target_pairs={{0,1},{1,0},{2,3},{3,2},{4,5},{5,4},{6,7},{7,6},{8,9},{9,8},{10,11... | collective-permute-start | bytes 2654216 | tf_op jit(solution)/shard_map/ppermute | solution.py:58
  65.1 7.9 %collective-permute-start.17 = (bf16[192,2304]{1,0:T(8,128)(2,1)S(1)}, bf16[192,2304]{1,0:T(8,128)(2,1)S(1)}, u32[]{:S(2)}, u32[]{:S(2)}) collective-permute-start(bf16[192,2304]{1,0:T(8,128)(2,1)S(1)} %collective-permute-done.12), channel_id=1, source_target_pairs={{0,1},{1,0},{2,3},{3,2},{4,5},{5,4},{6,7},{7,6},{8,9},{9,8},{10,11... | collective-permute-start | bytes 2654216 | tf_op jit(solution)/shard_map/ppermute | solution.py:58
  67.3 1.7 copy-start.31
  69.0 1.9 copy-start.12
  69.0 35.0 %collective-permute-start.18 = (bf16[72,6272]{1,0:T(8,128)(2,1)S(1)}, bf16[72,6272]{1,0:T(8,128)(2,1)S(1)}, u32[]{:S(2)}, u32[]{:S(2)}) collective-permute-start(bf16[72,6272]{1,0:T(8,128)(2,1)S(1)} %copy-done.31), channel_id=1, source_target_pairs={{0,12},{1,13},{2,14},{3,15},{4,8},{5,9},{6,10},{7,11},{8,4},{9,5},... | collective-permute-start | bytes 2709512 | tf_op jit(solution)/shard_map/ppermute | solution.py:58
  70.4 22.2 %collective-permute-start.20 = (bf16[48,6272]{1,0:T(8,128)(2,1)S(1)}, bf16[48,6272]{1,0:T(8,128)(2,1)S(1)}, u32[]{:S(2)}, u32[]{:S(2)}) collective-permute-start(bf16[48,6272]{1,0:T(8,128)(2,1)S(1)} %slice.123), channel_id=1, source_target_pairs={{0,2},{1,3},{2,0},{3,1},{4,6},{5,7},{6,4},{7,5},{8,10},{9,11},{10,... | collective-permute-start | bytes 1806344 | tf_op jit(solution)/shard_map/ppermute | solution.py:58
  71.0 32.1 %collective-permute-start.19 = (bf16[48,6272]{1,0:T(8,128)(2,1)S(1)}, bf16[48,6272]{1,0:T(8,128)(2,1)S(1)}, u32[]{:S(2)}, u32[]{:S(2)}) collective-permute-start(bf16[48,6272]{1,0:T(8,128)(2,1)S(1)} %copy-done.12), channel_id=1, source_target_pairs={{0,2},{1,3},{2,0},{3,1},{4,6},{5,7},{6,4},{7,5},{8,10},{9,11},{10,... | collective-permute-start | bytes 1806344 | tf_op jit(solution)/shard_map/ppermute | solution.py:58
  73.0 43.6 %copy-start.30 = (f32[1,384]{1,0:T(1,128)S(1)}, f32[1,384]{1,0:T(1,128)}, u32[]{:S(2)}) copy-start(f32[1,384]{1,0:T(1,128)} %get-tuple-element.172) | copy-start | bytes 4612
  104.0 1.1 copy-start.10
  105.9 27.5 %collective-permute-start.23 = (bf16[48,6272]{1,0:T(8,128)(2,1)}, bf16[48,6272]{1,0:T(8,128)(2,1)}, u32[]{:S(2)}, u32[]{:S(2)}) collective-permute-start(bf16[48,6272]{1,0:T(8,128)(2,1)} %slice.125), channel_id=1, source_target_pairs={{0,2},{1,3},{2,0},{3,1},{4,6},{5,7},{6,4},{7,5},{8,10},{9,11},{10,... | collective-permute-start | bytes 1806344 | tf_op jit(solution)/shard_map/ppermute | solution.py:58
  108.4 24.9 %collective-permute-start.22 = (bf16[640,512]{1,0:T(8,128)(2,1)}, bf16[640,512]{1,0:T(8,128)(2,1)}, u32[]{:S(2)}, u32[]{:S(2)}) collective-permute-start(bf16[640,512]{1,0:T(8,128)(2,1)} %dynamic-slice_convert_fusion.2), channel_id=1, source_target_pairs={{0,4},{1,5},{2,6},{3,7},{4,0},{5,1},{6,2},{7,3},{8,12},{9,13},{10,... | collective-permute-start | bytes 1966088 | tf_op jit(solution)/shard_map/ppermute | solution.py:58
  116.6 3.6 %collective-permute-start.24 = (f32[1,384]{1,0:T(1,128)S(1)}, f32[1,384]{1,0:T(1,128)S(1)}, u32[]{:S(2)}, u32[]{:S(2)}) collective-permute-start(f32[1,384]{1,0:T(1,128)S(1)} %fusion.41), channel_id=1, source_target_pairs={{0,16},{16,0},{1,17},{17,1},{2,18},{18,2},{3,19},{19,3},{4,20},{20... | collective-permute-start | bytes 4616 | tf_op jit(solution)/shard_map/ppermute | solution.py:58
  120.3 1.2 collective-permute-start.25
  121.5 11.9 %collective-permute-start.26 = (f32[1,384]{1,0:T(1,128)S(1)}, f32[1,384]{1,0:T(1,128)S(1)}, u32[]{:S(2)}, u32[]{:S(2)}) collective-permute-start(f32[1,384]{1,0:T(1,128)S(1)} %add.295), channel_id=1, source_target_pairs={{0,2},{1,3},{2,0},{3,1},{4,6},{5,7},{6,4},{7,5},{8,10},{9,11},{10,... | collective-permute-start | bytes 4616 | tf_op jit(solution)/shard_map/ppermute | solution.py:58
  123.0 1.2 copy-start.9
  124.1 1.2 copy-start.11
  133.4 22.1 %collective-permute-start.28 = (bf16[432,6272]{1,0:T(8,128)(2,1)}, bf16[432,6272]{1,0:T(8,128)(2,1)}, u32[]{:S(2)}, u32[]{:S(2)}) collective-permute-start(bf16[432,6272]{1,0:T(8,128)(2,1)} %shard_map.130.refs_0_), channel_id=1, source_target_pairs={{0,1},{1,0},{2,3},{3,2},{4,5},{5,4},{6,7},{7,6},{8,9},{9,8},{10,11... | collective-permute-start | bytes 16257032 | tf_op jit(solution)/shard_map/ppermute | solution.py:58
  137.0 1.3 copy-start.28
  137.7 17.8 %collective-permute-start.29 = (bf16[48,6272]{1,0:T(8,128)(2,1)}, bf16[48,6272]{1,0:T(8,128)(2,1)S(1)}, u32[]{:S(2)}, u32[]{:S(2)}) collective-permute-start(bf16[48,6272]{1,0:T(8,128)(2,1)} %collective-permute-done.23.refs_1_), channel_id=1, source_target_pairs={{0,1},{1,0},{2,3},{3,2},{4,5},{5,4},{6,7},{7,6},{8,9},{9,8},{10,11... | collective-permute-start | bytes 1806344 | tf_op jit(solution)/shard_map/ppermute | solution.py:58
  138.2 17.3 %collective-permute-start.27 = (bf16[320,512]{1,0:T(8,128)(2,1)}, bf16[320,512]{1,0:T(8,128)(2,1)S(1)}, u32[]{:S(2)}, u32[]{:S(2)}) collective-permute-start(bf16[320,512]{1,0:T(8,128)(2,1)} %copy-done.21), channel_id=1, source_target_pairs={{0,8},{1,9},{2,10},{3,11},{4,12},{5,13},{6,14},{7,15},{8,0},{9,1},... | collective-permute-start | bytes 983048 | tf_op jit(solution)/shard_map/ppermute | solution.py:58
  157.7 17.2 %collective-permute-start.31 = (bf16[320,512]{1,0:T(8,128)(2,1)S(1)}, bf16[320,512]{1,0:T(8,128)(2,1)S(1)}, u32[]{:S(2)}, u32[]{:S(2)}) collective-permute-start(bf16[320,512]{1,0:T(8,128)(2,1)S(1)} %get-tuple-element.204.refs_0_), channel_id=1, source_target_pairs={{0,2},{1,3},{2,0},{3,1},{4,6},{5,7},{6,4},{7,5},{8,10},{9,11},{10,... | collective-permute-start | bytes 983048 | tf_op jit(solution)/shard_map/ppermute | solution.py:58
  158.3 16.6 %collective-permute-start.30 = (bf16[320,512]{1,0:T(8,128)(2,1)S(1)}, bf16[320,512]{1,0:T(8,128)(2,1)S(1)}, u32[]{:S(2)}, u32[]{:S(2)}) collective-permute-start(bf16[320,512]{1,0:T(8,128)(2,1)S(1)} %get-tuple-element.204.refs_0_), channel_id=1, source_target_pairs={{0,8},{1,9},{2,10},{3,11},{4,12},{5,13},{6,14},{7,15},{8,0},{9,1},... | collective-permute-start | bytes 983048 | tf_op jit(solution)/shard_map/ppermute | solution.py:58
  158.3 16.5 %collective-permute-start.32 = (f32[1,320]{1,0:T(1,128)S(1)}, f32[1,320]{1,0:T(1,128)S(1)}, u32[]{:S(2)}, u32[]{:S(2)}) collective-permute-start(f32[1,320]{1,0:T(1,128)S(1)} %get-tuple-element.188), channel_id=1, source_target_pairs={{0,8},{1,9},{2,10},{3,11},{4,12},{5,13},{6,14},{7,15},{8,0},{9,1},... | collective-permute-start | bytes 3848 | tf_op jit(solution)/shard_map/ppermute | solution.py:58
  162.9 18.0 %copy-start.29 = (s32[32,1]{0,1:T(1,128)S(1)}, s32[32,1]{0,1:T(1,128)}, u32[]{:S(2)}) copy-start(s32[32,1]{0,1:T(1,128)} %param.19) | copy-start | bytes 388
  174.9 19.6 %collective-permute-start.37 = (f32[2,320]{1,0:T(2,128)S(1)}, f32[2,320]{1,0:T(2,128)S(1)}, u32[]{:S(2)}, u32[]{:S(2)}) collective-permute-start(f32[2,320]{1,0:T(2,128)S(1)} %broadcast_select_fusion.3), channel_id=1, source_target_pairs={{0,6},{1,7},{2,4},{3,5},{4,2},{5,3},{6,0},{7,1},{8,14},{9,15},{10,... | collective-permute-start | bytes 7688 | tf_op jit(solution)/shard_map/ppermute | solution.py:58
  175.1 19.4 %collective-permute-start.36 = (f32[2,320]{1,0:T(2,128)S(1)}, f32[2,320]{1,0:T(2,128)S(1)}, u32[]{:S(2)}, u32[]{:S(2)}) collective-permute-start(f32[2,320]{1,0:T(2,128)S(1)} %broadcast_select_fusion.3), channel_id=1, source_target_pairs={{0,2},{1,3},{2,0},{3,1},{4,6},{5,7},{6,4},{7,5},{8,10},{9,11},{10,... | collective-permute-start | bytes 7688 | tf_op jit(solution)/shard_map/ppermute | solution.py:58
  176.5 18.1 %collective-permute-start.35 = (f32[2,320]{1,0:T(2,128)S(1)}, f32[2,320]{1,0:T(2,128)S(1)}, u32[]{:S(2)}, u32[]{:S(2)}) collective-permute-start(f32[2,320]{1,0:T(2,128)S(1)} %broadcast_select_fusion.3), channel_id=1, source_target_pairs={{0,4},{1,5},{2,6},{3,7},{4,0},{5,1},{6,2},{7,3},{8,12},{9,13},{10,... | collective-permute-start | bytes 7688 | tf_op jit(solution)/shard_map/ppermute | solution.py:58
  178.4 16.3 %collective-permute-start.34 = (bf16[320,512]{1,0:T(8,128)(2,1)S(1)}, bf16[320,512]{1,0:T(8,128)(2,1)S(1)}, u32[]{:S(2)}, u32[]{:S(2)}) collective-permute-start(bf16[320,512]{1,0:T(8,128)(2,1)S(1)} %collective-permute-done.30.refs_1_), channel_id=1, source_target_pairs={{0,2},{1,3},{2,0},{3,1},{4,6},{5,7},{6,4},{7,5},{8,10},{9,11},{10,... | collective-permute-start | bytes 983048 | tf_op jit(solution)/shard_map/ppermute | solution.py:58
  180.8 15.8 %collective-permute-start.33 = (bf16[640,512]{1,0:T(8,128)(2,1)}, bf16[640,512]{1,0:T(8,128)(2,1)S(1)}, u32[]{:S(2)}, u32[]{:S(2)}) collective-permute-start(bf16[640,512]{1,0:T(8,128)(2,1)} %pad_maximum_fusion), channel_id=1, source_target_pairs={{0,4},{1,5},{2,6},{3,7},{4,0},{5,1},{6,2},{7,3},{8,12},{9,13},{10,... | collective-permute-start | bytes 1966088 | tf_op jit(solution)/shard_map/ppermute | solution.py:58
  196.6 14.6 %collective-permute-start.43 = (bf16[640,512]{1,0:T(8,128)(2,1)S(1)}, bf16[640,512]{1,0:T(8,128)(2,1)S(1)}, u32[]{:S(2)}, u32[]{:S(2)}) collective-permute-start(bf16[640,512]{1,0:T(8,128)(2,1)S(1)} %collective-permute-done.33.refs_2_), channel_id=1, source_target_pairs={{0,2},{1,3},{2,0},{3,1},{4,6},{5,7},{6,4},{7,5},{8,10},{9,11},{10,... | collective-permute-start | bytes 1966088 | tf_op jit(solution)/shard_map/ppermute | solution.py:58
  197.1 8.4 %collective-permute-start.40 = (bf16[640,512]{1,0:T(8,128)(2,1)S(1)}, bf16[640,512]{1,0:T(8,128)(2,1)S(1)}, u32[]{:S(2)}, u32[]{:S(2)}) collective-permute-start(bf16[640,512]{1,0:T(8,128)(2,1)S(1)} %collective-permute-done.33.refs_2_), channel_id=1, source_target_pairs={{0,1},{1,0},{2,3},{3,2},{4,5},{5,4},{6,7},{7,6},{8,9},{9,8},{10,11... | collective-permute-start | bytes 1966088 | tf_op jit(solution)/shard_map/ppermute | solution.py:58
  197.1 6.3 %collective-permute-start.38 = (bf16[320,512]{1,0:T(8,128)(2,1)S(1)}, bf16[320,512]{1,0:T(8,128)(2,1)}, u32[]{:S(2)}, u32[]{:S(2)}) collective-permute-start(bf16[320,512]{1,0:T(8,128)(2,1)S(1)} %get-tuple-element.204.refs_0_), channel_id=1, source_target_pairs={{0,1},{1,0},{2,3},{3,2},{4,5},{5,4},{6,7},{7,6},{8,9},{9,8},{10,11... | collective-permute-start | bytes 983048 | tf_op jit(solution)/shard_map/ppermute | solution.py:58
  197.6 2.1 collective-permute-start.44
  199.7 3.7 %collective-permute-start.45 = (f32[2,4,320]{2,1,0:T(4,128)S(1)}, f32[2,4,320]{2,1,0:T(4,128)S(1)}, u32[]{:S(2)}, u32[]{:S(2)}) collective-permute-start(f32[2,4,320]{2,1,0:T(4,128)S(1)} %add.302), channel_id=1, source_target_pairs={{0,16},{16,0},{1,17},{17,1},{2,18},{18,2},{3,19},{19,3},{4,20},{20... | collective-permute-start | bytes 30728 | tf_op jit(solution)/shard_map/ppermute | solution.py:58
  201.4 2.8 %collective-permute-start.39 = (bf16[320,512]{1,0:T(8,128)(2,1)S(1)}, bf16[320,512]{1,0:T(8,128)(2,1)S(1)}, u32[]{:S(2)}, u32[]{:S(2)}) collective-permute-start(bf16[320,512]{1,0:T(8,128)(2,1)S(1)} %collective-permute-done.30.refs_1_), channel_id=1, source_target_pairs={{0,1},{1,0},{2,3},{3,2},{4,5},{5,4},{6,7},{7,6},{8,9},{9,8},{10,11... | collective-permute-start | bytes 983048 | tf_op jit(solution)/shard_map/ppermute | solution.py:58
  203.4 1.6 collective-permute-start.41
  203.4 2.1 collective-permute-start.42
  211.2 2.1 collective-permute-start.46
  (10 other events, 9.4 us)
